TPU v7x, 32 devices: a whole 2x2x4 slice. The times are simulated.
32 devices in a mesh: wide: 8 (over y, x, core), narrow: 4 (over z).
Axes of the slice: x: 2, y: 2, z: 4, core: 2. Of those that a mesh axis runs over, the one named last changes fastest.
Arguments:
- tokens: bfloat16 [16, 1024, 2048], P('wide', 'narrow'), may hold values from -6 to 6
- active: int32 [16, 1024], P('wide'), may hold values from 0 to 1, as said below
- cotangent: bfloat16 [16, 1024, 2048], P('wide', 'narrow'), may hold values from -6 to 6
- gain_rows: float32 [2, 2048], P(None, ('wide', 'narrow')), may hold values from 0.5 to 1.5
- w_qkv: float32 [2048, 3072], P(('wide', 'narrow')), may hold values from -0.125 to 0.125
- w_out: float32 [2048, 2048], P(('wide', 'narrow')), may hold values from -0.75 to 0.75
- w_gateup: float32 [2048, 11264], P(('wide', 'narrow')), may hold values from -0.125 to 0.125
- w_down: float32 [5632, 2048], P(('wide', 'narrow')), may hold values from -0.078125 to 0.078125
- moment_gains: float32 [2, 2048], P(None, ('wide', 'narrow')), may hold values from -192 to 192
- moment_qkv: float32 [2048, 3072], P(('wide', 'narrow')), may hold values from -192 to 192
- moment_out: float32 [2048, 2048], P(('wide', 'narrow')), may hold values from -192 to 192
- moment_gateup: float32 [2048, 11264], P(('wide', 'narrow')), may hold values from -192 to 192
- moment_down: float32 [5632, 2048], P(('wide', 'narrow')), may hold values from -192 to 192
- average_gains: float32 [2, 2048], P(None, ('wide', 'narrow')), may hold values from 0.5 to 1.5
- average_qkv: float32 [2048, 3072], P(('wide', 'narrow')), may hold values from -0.125 to 0.125
- average_out: float32 [2048, 2048], P(('wide', 'narrow')), may hold values from -0.75 to 0.75
- average_gateup: float32 [2048, 11264], P(('wide', 'narrow')), may hold values from -0.125 to 0.125
- average_down: float32 [5632, 2048], P(('wide', 'narrow')), may hold values from -0.078125 to 0.078125
Outputs:
- layer_out: bfloat16 [16, 1024, 2048], P('wide', 'narrow')
- grad_tokens: bfloat16 [16, 1024, 2048], P('wide', 'narrow')
- grad_gains: float32 [2, 2048], P(None, ('wide', 'narrow'))
- grad_qkv: float32 [2048, 3072], P(('wide', 'narrow'))
- grad_out: float32 [2048, 2048], P(('wide', 'narrow'))
- grad_gateup: float32 [2048, 11264], P(('wide', 'narrow'))
- grad_down: float32 [5632, 2048], P(('wide', 'narrow'))
- new_gains: float32 [2, 2048], P(None, ('wide', 'narrow'))
- new_qkv: float32 [2048, 3072], P(('wide', 'narrow'))
- new_out: float32 [2048, 2048], P(('wide', 'narrow'))
- new_gateup: float32 [2048, 11264], P(('wide', 'narrow'))
- new_down: float32 [5632, 2048], P(('wide', 'narrow'))
- next_moment_gains: float32 [2, 2048], P(None, ('wide', 'narrow'))
- next_moment_qkv: float32 [2048, 3072], P(('wide', 'narrow'))
- next_moment_out: float32 [2048, 2048], P(('wide', 'narrow'))
- next_moment_gateup: float32 [2048, 11264], P(('wide', 'narrow'))
- next_moment_down: float32 [5632, 2048], P(('wide', 'narrow'))
- next_average_gains: float32 [2, 2048], P(None, ('wide', 'narrow'))
- next_average_qkv: float32 [2048, 3072], P(('wide', 'narrow'))
- next_average_out: float32 [2048, 2048], P(('wide', 'narrow'))
- next_average_gateup: float32 [2048, 11264], P(('wide', 'narrow'))
- next_average_down: float32 [5632, 2048], P(('wide', 'narrow'))
Inputs may be any that keep to these rules, and one draw needn't show every extreme that they name: `active`: 1 marks a token that the layer processes, 0 one that keeps its input; each sequence has its own share of skipped tokens.
All inputs are finite; a program needn't handle non-finite values.
Results may differ from a plain program's by a relative error of at most 0.015.
Values may be sent and summed in bfloat16 or wider, within the bound.
A program may use at most 448 MiB of HBM per device.

v0:
```python
import jax
import jax.numpy as jnp
from jax import lax
from jax.sharding import PartitionSpec as P

HEADS = 16
KV_HEADS = 4
HEAD_DIM = 128
FF = 5632


EPSILON = 1e-05
MOMENTUM = 0.5
AVERAGING = 0.5
STEP_RATE = 0.0003


def rotary_tables(positions):
    half_dim = HEAD_DIM // 2
    frequency = jnp.power(10000.0, -2.0 * jnp.arange(half_dim, dtype=jnp.float32) / HEAD_DIM)
    angles = positions[:, None] * frequency[None, :]
    return (jnp.cos(angles)[:, None, :], jnp.sin(angles)[:, None, :])


def rotate_heads(head_values, cosine_table, sine_table):
    half_dim = head_values.shape[-1] // 2
    first_half = head_values[..., :half_dim]
    second_half = head_values[..., half_dim:]
    return jnp.concatenate(
        [
            first_half * cosine_table - second_half * sine_table,
            second_half * cosine_table + first_half * sine_table,
        ],
        axis=-1,
    )


def unrotate_heads(head_grads, cosine_table, sine_table):
    half_dim = head_grads.shape[-1] // 2
    first_half = head_grads[..., :half_dim]
    second_half = head_grads[..., half_dim:]
    return jnp.concatenate(
        [
            first_half * cosine_table + second_half * sine_table,
            second_half * cosine_table - first_half * sine_table,
        ],
        axis=-1,
    )


def norm_forward(values_in, gain_row):
    inverse = lax.rsqrt(jnp.mean(values_in * values_in, axis=-1, keepdims=True) + EPSILON)
    return (values_in * inverse * gain_row, inverse)


def norm_backward(values_in, inverse, gain_row, incoming):
    scaled_grad = incoming * gain_row
    grad_values = inverse * scaled_grad - values_in * inverse * inverse * inverse * jnp.mean(
        scaled_grad * values_in, axis=-1, keepdims=True
    )
    grad_gain = jnp.sum(incoming * values_in * inverse, axis=0)
    return (grad_values, grad_gain)


def advance_state(weight, moment, average, gradient):
    moment_next = MOMENTUM * moment + gradient
    weight_next = weight - STEP_RATE * (gradient + MOMENTUM * moment_next)
    average_next = AVERAGING * average + (1.0 - AVERAGING) * weight_next
    return (weight_next, moment_next, average_next)


def on_device(
    tokens,
    active,
    cotangent,
    gain_rows,
    w_qkv,
    w_out,
    w_gateup,
    w_down,
    moment_gains,
    moment_qkv,
    moment_out,
    moment_gateup,
    moment_down,
    average_gains,
    average_qkv,
    average_out,
    average_gateup,
    average_down,
):
    seq_count, span_len, width = tokens.shape
    seq_len = span_len * lax.axis_size("narrow")
    row_count = seq_count * span_len
    kv_width = KV_HEADS * HEAD_DIM
    group_size = HEADS // KV_HEADS
    score_scale = HEAD_DIM ** (-0.5)
    first_row = lax.axis_index("narrow") * span_len
    query_places = first_row + jnp.arange(span_len, dtype=jnp.int32)
    key_places = jnp.arange(seq_len, dtype=jnp.int32)
    own_mask = lax.dynamic_slice_in_dim(active, first_row, span_len, 1)
    allowed = (key_places[None, None, :] <= query_places[None, :, None]) & (
        (active[:, None, :] == 1) | (key_places[None, None, :] == query_places[None, :, None])
    )
    allowed = allowed[:, None, None]
    live_rows = own_mask.astype(jnp.float32).reshape(row_count, 1)
    inputs = tokens.reshape(row_count, width).astype(jnp.float32)
    cosine_table, sine_table = rotary_tables(query_places.astype(jnp.float32))
    gains_low, qkv_low, out_low = (
        lax.all_gather(gain_rows.astype(jnp.bfloat16), ("wide", "narrow"), axis=1, tiled=True),
        lax.all_gather(w_qkv.astype(jnp.bfloat16), ("wide", "narrow"), axis=0, tiled=True),
        lax.all_gather(w_out.astype(jnp.bfloat16), ("wide", "narrow"), axis=0, tiled=True),
    )
    gain_full = gains_low.astype(jnp.float32)
    normed, inverse_one = norm_forward(inputs, gain_full[0])
    normed_low = normed.astype(jnp.bfloat16)
    projected = jnp.dot(normed_low, qkv_low, preferred_element_type=jnp.float32)
    query_low = rotate_heads(
        projected[:, :width].reshape(seq_count, span_len, HEADS, HEAD_DIM), cosine_table, sine_table
    ).astype(jnp.bfloat16)
    key_low = rotate_heads(
        projected[:, width : width + kv_width].reshape(seq_count, span_len, KV_HEADS, HEAD_DIM),
        cosine_table,
        sine_table,
    ).astype(jnp.bfloat16)
    value_low = projected[:, width + kv_width :].astype(jnp.bfloat16)
    key_all, value_all = (
        lax.all_gather(
            key_low.reshape(seq_count, span_len, kv_width), "narrow", axis=1, tiled=True
        ),
        lax.all_gather(
            value_low.reshape(seq_count, span_len, kv_width), "narrow", axis=1, tiled=True
        ),
    )
    key_heads = key_all.reshape(seq_count, seq_len, KV_HEADS, HEAD_DIM)
    value_heads = value_all.reshape(seq_count, seq_len, KV_HEADS, HEAD_DIM)
    query_groups = query_low.reshape(seq_count, span_len, KV_HEADS, group_size, HEAD_DIM)

    def scores_for(query_part):
        raw_scores = (
            jnp.einsum(
                "bqkgd,bskd->bkgqs", query_part, key_heads, preferred_element_type=jnp.float32
            )
            * score_scale
        )
        return jnp.where(allowed, raw_scores, -1e30)

    scores = scores_for(query_groups)
    row_peak = jnp.max(scores, axis=-1, keepdims=True)
    shifted = jnp.exp(scores - row_peak)
    row_total = jnp.sum(shifted, axis=-1, keepdims=True)
    soft_probs = shifted / row_total
    log_total = row_peak + jnp.log(row_total)
    mixed_values = jnp.einsum(
        "bkgqs,bskd->bqkgd",
        soft_probs.astype(jnp.bfloat16),
        value_heads,
        preferred_element_type=jnp.float32,
    )
    attended_low = mixed_values.reshape(row_count, width).astype(jnp.bfloat16)
    branch = jnp.dot(attended_low, out_low, preferred_element_type=jnp.float32)
    middle = inputs + live_rows * branch
    normed_mid, inverse_two = norm_forward(middle, gain_full[1])
    normed_mid_low = normed_mid.astype(jnp.bfloat16)
    gateup_low, down_low = (
        lax.all_gather(w_gateup.astype(jnp.bfloat16), ("wide", "narrow"), axis=0, tiled=True),
        lax.all_gather(w_down.astype(jnp.bfloat16), ("wide", "narrow"), axis=0, tiled=True),
    )
    gate_up = jnp.dot(normed_mid_low, gateup_low, preferred_element_type=jnp.float32)
    gate_part = gate_up[:, :FF]
    upper_part = gate_up[:, FF:]
    hidden_low = (jax.nn.silu(gate_part) * upper_part).astype(jnp.bfloat16)
    down_proj = jnp.dot(hidden_low, down_low, preferred_element_type=jnp.float32)
    layer_out = (middle + live_rows * down_proj).astype(jnp.bfloat16).reshape(tokens.shape)
    upstream = cotangent.reshape(row_count, width).astype(jnp.float32)
    down_grad_low = (live_rows * upstream).astype(jnp.bfloat16)
    gateup_back, down_back = (
        lax.all_gather(w_gateup.astype(jnp.bfloat16), ("wide", "narrow"), axis=0, tiled=True),
        lax.all_gather(w_down.astype(jnp.bfloat16), ("wide", "narrow"), axis=0, tiled=True),
    )
    term_down = jnp.dot(hidden_low.T, down_grad_low, preferred_element_type=jnp.float32)
    grad_hidden = jnp.dot(down_grad_low, down_back.T, preferred_element_type=jnp.float32)
    gate_sigmoid = jax.nn.sigmoid(gate_part)
    grad_gate = grad_hidden * upper_part * gate_sigmoid * (1.0 + gate_part * (1.0 - gate_sigmoid))
    grad_upper = grad_hidden * gate_part * gate_sigmoid
    grad_gateup_low = jnp.concatenate([grad_gate, grad_upper], axis=1).astype(jnp.bfloat16)
    term_gateup = jnp.dot(normed_mid_low.T, grad_gateup_low, preferred_element_type=jnp.float32)
    grad_gateup, grad_down = (
        lax.psum_scatter(term_gateup, ("wide", "narrow"), scatter_dimension=0, tiled=True),
        lax.psum_scatter(term_down, ("wide", "narrow"), scatter_dimension=0, tiled=True),
    )
    grad_normed_mid = jnp.dot(grad_gateup_low, gateup_back.T, preferred_element_type=jnp.float32)
    grad_middle_norm, grad_gain_two = norm_backward(
        middle, inverse_two, gain_full[1], grad_normed_mid
    )
    grad_middle = upstream + grad_middle_norm
    branch_grad_low = (live_rows * grad_middle).astype(jnp.bfloat16)
    qkv_back, out_back = (
        lax.all_gather(w_qkv.astype(jnp.bfloat16), ("wide", "narrow"), axis=0, tiled=True),
        lax.all_gather(w_out.astype(jnp.bfloat16), ("wide", "narrow"), axis=0, tiled=True),
    )
    term_out = jnp.dot(attended_low.T, branch_grad_low, preferred_element_type=jnp.float32)
    grad_attended_low = jnp.dot(
        branch_grad_low, out_back.T, preferred_element_type=jnp.float32
    ).astype(jnp.bfloat16)
    grad_heads = grad_attended_low.reshape(seq_count, span_len, KV_HEADS, group_size, HEAD_DIM)
    probs_again = jnp.exp(scores_for(query_groups) - log_total)
    grad_probs = jnp.einsum(
        "bqkgd,bskd->bkgqs", grad_heads, value_heads, preferred_element_type=jnp.float32
    )
    row_inner = jnp.sum(grad_probs * probs_again, axis=-1, keepdims=True)
    grad_scores_low = (probs_again * (grad_probs - row_inner)).astype(jnp.bfloat16)
    grad_query = (
        jnp.einsum(
            "bkgqs,bskd->bqkgd", grad_scores_low, key_heads, preferred_element_type=jnp.float32
        )
        * score_scale
    )
    key_term = (
        jnp.einsum(
            "bkgqs,bqkgd->bskd", grad_scores_low, query_groups, preferred_element_type=jnp.float32
        )
        * score_scale
    )
    value_term = jnp.einsum(
        "bkgqs,bqkgd->bskd",
        probs_again.astype(jnp.bfloat16),
        grad_heads,
        preferred_element_type=jnp.float32,
    )
    grad_key, grad_value = (
        lax.psum_scatter(
            key_term.reshape(seq_count, seq_len, kv_width).astype(jnp.bfloat16),
            "narrow",
            scatter_dimension=1,
            tiled=True,
        ).astype(jnp.float32),
        lax.psum_scatter(
            value_term.reshape(seq_count, seq_len, kv_width).astype(jnp.bfloat16),
            "narrow",
            scatter_dimension=1,
            tiled=True,
        ).astype(jnp.float32),
    )
    grad_query_pre = unrotate_heads(
        grad_query.reshape(seq_count, span_len, HEADS, HEAD_DIM), cosine_table, sine_table
    ).reshape(row_count, width)
    grad_key_pre = unrotate_heads(
        grad_key.reshape(seq_count, span_len, KV_HEADS, HEAD_DIM), cosine_table, sine_table
    ).reshape(row_count, kv_width)
    grad_projected_low = jnp.concatenate(
        [grad_query_pre, grad_key_pre, grad_value.reshape(row_count, kv_width)], axis=1
    ).astype(jnp.bfloat16)
    term_qkv = jnp.dot(normed_low.T, grad_projected_low, preferred_element_type=jnp.float32)
    grad_normed = jnp.dot(grad_projected_low, qkv_back.T, preferred_element_type=jnp.float32)
    grad_input_norm, grad_gain_one = norm_backward(inputs, inverse_one, gain_full[0], grad_normed)
    grad_tokens = (grad_middle + grad_input_norm).astype(jnp.bfloat16).reshape(tokens.shape)
    gain_term = jnp.stack([grad_gain_one, grad_gain_two])
    grad_gains, grad_qkv, grad_out = (
        lax.psum_scatter(gain_term, ("wide", "narrow"), scatter_dimension=1, tiled=True),
        lax.psum_scatter(term_qkv, ("wide", "narrow"), scatter_dimension=0, tiled=True),
        lax.psum_scatter(term_out, ("wide", "narrow"), scatter_dimension=0, tiled=True),
    )
    state_gains = advance_state(gain_rows, moment_gains, average_gains, grad_gains)
    state_qkv = advance_state(w_qkv, moment_qkv, average_qkv, grad_qkv)
    state_out = advance_state(w_out, moment_out, average_out, grad_out)
    state_gateup = advance_state(w_gateup, moment_gateup, average_gateup, grad_gateup)
    state_down = advance_state(w_down, moment_down, average_down, grad_down)
    return (
        layer_out,
        grad_tokens,
        grad_gains,
        grad_qkv,
        grad_out,
        grad_gateup,
        grad_down,
        state_gains[0],
        state_qkv[0],
        state_out[0],
        state_gateup[0],
        state_down[0],
        state_gains[1],
        state_qkv[1],
        state_out[1],
        state_gateup[1],
        state_down[1],
        state_gains[2],
        state_qkv[2],
        state_out[2],
        state_gateup[2],
        state_down[2],
    )


def solution(mesh):
    in_specs = (
        P("wide", "narrow", None),
        P("wide", None),
        P("wide", "narrow", None),
        P(None, ("wide", "narrow")),
        P(("wide", "narrow"), None),
        P(("wide", "narrow"), None),
        P(("wide", "narrow"), None),
        P(("wide", "narrow"), None),
        P(None, ("wide", "narrow")),
        P(("wide", "narrow"), None),
        P(("wide", "narrow"), None),
        P(("wide", "narrow"), None),
        P(("wide", "narrow"), None),
        P(None, ("wide", "narrow")),
        P(("wide", "narrow"), None),
        P(("wide", "narrow"), None),
        P(("wide", "narrow"), None),
        P(("wide", "narrow"), None),
    )
    out_specs = (
        P("wide", "narrow", None),
        P("wide", "narrow", None),
        P(None, ("wide", "narrow")),
        P(("wide", "narrow"), None),
        P(("wide", "narrow"), None),
        P(("wide", "narrow"), None),
        P(("wide", "narrow"), None),
        P(None, ("wide", "narrow")),
        P(("wide", "narrow"), None),
        P(("wide", "narrow"), None),
        P(("wide", "narrow"), None),
        P(("wide", "narrow"), None),
        P(None, ("wide", "narrow")),
        P(("wide", "narrow"), None),
        P(("wide", "narrow"), None),
        P(("wide", "narrow"), None),
        P(("wide", "narrow"), None),
        P(None, ("wide", "narrow")),
        P(("wide", "narrow"), None),
        P(("wide", "narrow"), None),
        P(("wide", "narrow"), None),
        P(("wide", "narrow"), None),
    )
    return jax.shard_map(
        on_device, mesh=mesh, in_specs=in_specs, out_specs=out_specs, check_vma=False
    )
```

profile of v0, /device:TPU:0, one launch (start us, length us, event | category | flops | bytes accessed | tf_op | source)
XLA Modules:
  0.0 4626.1 jit_solution(4949357317963044455)
XLA Ops:
  12.2 69.9 %all-gather = bf16[32,64,2]{1,2,0:T(2,128)(2,1)S(1)} all-gather(bf16[1,64,2]{1,2,0:T(2,128)(2,1)S(1)} %convert_bitcast_fusion.2), channel_id=1, replica_groups=mesh['wide'=8,'narrow'=4] {'wide','narrow'}, dimensions={0}, use_global_device_ids=true | all-gather | bytes 8448 | tf_op jit(solution)/shard_map/all_gather | solution.py:110
  84.7 25.9 all-gather.8.cloned.1.call-done
  172.2 43.2 all-gather.12.cloned.1.call-done
  215.4 17.0 fusion.41
  245.9 15.1 convert_bitcast_fusion
  270.2 24.3 all-gather.14.cloned.1.call-done
  305.3 246.3 %all-gather.16.cloned.1.call-done = bf16[2048,11264]{1,0:T(8,128)(2,1)} async-done(((bf16[64,11264]{1,0:T(8,128)(2,1)}), bf16[2048,11264]{1,0:T(8,128)(2,1)}) %all-gather.16.cloned.1.call-update) | async-done | bytes 46137360 | tf_op jit(solution)/shard_map/all_gather | solution.py:166
  551.6 33.3 fusion.37
  584.9 112.8 %all-gather.18.cloned.1.call-done = bf16[5632,2048]{1,0:T(8,128)(2,1)} async-done(((bf16[176,2048]{1,0:T(8,128)(2,1)}), bf16[5632,2048]{1,0:T(8,128)(2,1)}) %all-gather.18.cloned.1.call-update) | async-done | bytes 23068688 | tf_op jit(solution)/shard_map/all_gather | solution.py:167
  697.7 26.7 multiply_convert_fusion.1
  724.4 34.4 multiply_reduce_fusion
  779.8 23.6 fusion
  803.4 27.9 fusion.2
  842.4 16.0 bitcast_convert_fusion
  896.5 34.2 reduce-scatter.12.cloned.1.call-done
  930.7 14.6 fusion.24
  976.8 21.0 fusion.43
  998.5 40.2 fusion.9
  1038.9 20.2 add_convert_fusion.1
  1062.0 19.4 reduce-scatter.22.cloned.1.call-done
  1082.9 362.2 %reduce-scatter.16.cloned.1.call-done = f32[64,2048]{1,0:T(8,128)} async-done(((f32[2048,2048]{1,0:T(8,128)}), f32[64,2048]{1,0:T(8,128)}) %reduce-scatter.16.cloned.1.call-update) | async-done | bytes 524304 | tf_op jit(solution)/shard_map/reduce_scatter | solution.py:262
  1447.8 248.9 %reduce-scatter.14.cloned.1.call-done = f32[64,3072]{1,0:T(8,128)} async-done(((f32[2048,3072]{1,0:T(8,128)}), f32[64,3072]{1,0:T(8,128)}) %reduce-scatter.14.cloned.1.call-update) | async-done | bytes 786448 | tf_op jit(solution)/shard_map/reduce_scatter | solution.py:261
  1699.9 971.5 %reduce-scatter.20.cloned.1.call-done = f32[176,2048]{1,0:T(8,128)} async-done(((f32[5632,2048]{1,0:T(8,128)}), f32[176,2048]{1,0:T(8,128)}) %reduce-scatter.20.cloned.1.call-update) | async-done | bytes 1441808 | tf_op jit(solution)/shard_map/reduce_scatter | solution.py:190
  2676.4 1933.9 %reduce-scatter.18.cloned.1.call-done = f32[64,11264]{1,0:T(8,128)} async-done(((f32[2048,11264]{1,0:T(8,128)}), f32[64,11264]{1,0:T(8,128)}) %reduce-scatter.18.cloned.1.call-update) | async-done | bytes 2883600 | tf_op jit(solution)/shard_map/reduce_scatter | solution.py:189
  (184 shorter events, 228.4 us)
Async XLA Ops:
  7.2 75.6 %copy-start = (bf16[2,256,2048]{2,1,0:T(8,128)(2,1)S(1)}, bf16[2,256,2048]{2,1,0:T(8,128)(2,1)}, u32[]{:S(2)}) copy-start(bf16[2,256,2048]{2,1,0:T(8,128)(2,1)} %param.18) | copy-start | bytes 6291460
  7.2 103.3 %all-gather.8.cloned.1.call-start = ((), (), s32[]{:S(2)}) async-start(), calls=%async_computation.7 | async-start | bytes 12976128 | tf_op jit(solution)/shard_map/all_gather | solution.py:111
  9.3 159.0 %all-gather.10.cloned.1.call-start = ((), (), s32[]{:S(2)}) async-start(), calls=%async_computation.8 | async-start | bytes 2621440 | tf_op jit(solution)/shard_map/all_gather | solution.py:131
  11.5 109.0 %copy-start.32 = (f32[1,2,2,128]{3,1,2,0:T(2,128)}, f32[1,2,2,128]{3,1,2,0:T(2,128)S(1)}, u32[]{:S(2)}) copy-start(f32[1,2,2,128]{3,1,2,0:T(2,128)S(1)} %copy.135) | copy-start | bytes 6148
  82.2 676.6 %copy-start.25 = (f32[1,2048]{1,0:T(1,128)}, f32[1,2048]{1,0:T(1,128)S(1)}, u32[]{:S(2)}) copy-start(f32[1,2048]{1,0:T(1,128)S(1)} %get-tuple-element.56) | copy-start | bytes 24580
  124.0 91.5 %all-gather.12.cloned.1.call-start = ((), (), s32[]{:S(2)}) async-start(), calls=%async_computation.9 | async-start | bytes 2621440 | tf_op jit(solution)/shard_map/all_gather | solution.py:128
  133.6 160.9 %all-gather.14.cloned.1.call-start = ((), (), s32[]{:S(2)}) async-start(), calls=%async_computation.10 | async-start | bytes 8650752 | tf_op jit(solution)/shard_map/all_gather | solution.py:112
  135.4 416.2 %all-gather.16.cloned.1.call-start = ((), (), s32[]{:S(2)}) async-start(), calls=%async_computation.11 | async-start | bytes 47579136 | tf_op jit(solution)/shard_map/all_gather | solution.py:166
  138.6 559.1 %all-gather.18.cloned.1.call-start = ((), (), s32[]{:S(2)}) async-start(), calls=%async_computation.12 | async-start | bytes 23789568 | tf_op jit(solution)/shard_map/all_gather | solution.py:167
  139.6 749.4 %reduce-scatter.10.cloned.1.call-start = ((), (), s32[]{:S(2)}) async-start(), calls=%async_computation.13 | async-start | bytes 2621440 | tf_op jit(solution)/shard_map/reduce_scatter | solution.py:232
  305.3 453.5 %copy-start.27 = (f32[512]{0:T(512)}, f32[512]{0:T(512)S(1)}, u32[]{:S(2)}) copy-start(f32[512]{0:T(512)S(1)} %add_rsqrt_fusion) | copy-start | bytes 6148
  551.6 146.1 %copy-start.23 = (bf16[512,2048]{1,0:T(8,128)(2,1)S(1)}, bf16[512,2048]{1,0:T(8,128)(2,1)}, u32[]{:S(2)}) copy-start(bf16[512,2048]{1,0:T(8,128)(2,1)} %fusion.11) | copy-start | bytes 6291460
  842.3 88.4 %reduce-scatter.12.cloned.1.call-start = ((), (), s32[]{:S(2)}) async-start(), calls=%async_computation.14 | async-start | bytes 2621440 | tf_op jit(solution)/shard_map/reduce_scatter | solution.py:238
  862.4 219.0 %reduce-scatter.22.cloned.1.call-start = ((), (), s32[]{:S(2)}) async-start(), calls=%async_computation.19 | async-start | bytes 1081344
  891.4 39.3 copy-start.1
  891.4 39.3 copy-start.30
  946.6 498.5 %reduce-scatter.16.cloned.1.call-start = ((), (), s32[]{:S(2)}) async-start(), calls=%async_computation.16 | async-start | bytes 17301504 | tf_op jit(solution)/shard_map/reduce_scatter | solution.py:262
  960.1 736.6 %reduce-scatter.14.cloned.1.call-start = ((), (), s32[]{:S(2)}) async-start(), calls=%async_computation.15 | async-start | bytes 25952256 | tf_op jit(solution)/shard_map/reduce_scatter | solution.py:261
  975.3 1696.2 %reduce-scatter.20.cloned.1.call-start = ((), (), s32[]{:S(2)}) async-start(), calls=%async_computation.18 | async-start | bytes 47579136 | tf_op jit(solution)/shard_map/reduce_scatter | solution.py:190
  997.9 3612.5 %reduce-scatter.18.cloned.1.call-start = ((), (), s32[]{:S(2)}) async-start(), calls=%async_computation.17 | async-start | bytes 95158272 | tf_op jit(solution)/shard_map/reduce_scatter | solution.py:189
  1059.2 385.9 %copy-start.21 = (f32[64,2048]{1,0:T(8,128)S(1)}, f32[64,2048]{1,0:T(8,128)}, u32[]{:S(2)}) copy-start(f32[64,2048]{1,0:T(8,128)} %param.23) | copy-start | bytes 1572868
  1062.0 634.7 %copy-start.20 = (f32[64,3072]{1,0:T(8,128)S(1)}, f32[64,3072]{1,0:T(8,128)}, u32[]{:S(2)}) copy-start(f32[64,3072]{1,0:T(8,128)} %param.22) | copy-start | bytes 2359300
  1082.3 617.6 %copy-start.36 = (f32[2,64]{1,0:T(2,128)}, f32[2,64]{1,0:T(2,128)S(1)}, u32[]{:S(2)}) copy-start(f32[2,64]{1,0:T(2,128)S(1)} %copy.129) | copy-start | bytes 1540
  1082.9 1588.5 %copy-start.11 = (f32[176,2048]{1,0:T(8,128)S(1)}, f32[176,2048]{1,0:T(8,128)}, u32[]{:S(2)}) copy-start(f32[176,2048]{1,0:T(8,128)} %param.25) | copy-start | bytes 4325380
  (31 other events, 376.6 us)
Sparse Core Ops, SparseCore 0:
  11.5 98.9 all-gather.7
  124.1 44.1 all-gather.9
  170.4 44.9 all-gather.11
  218.8 75.6 all-gather.13
  297.7 253.8 all-gather.15
  554.9 142.7 all-gather.17
  842.4 42.0 reduce-scatter.9
  887.5 43.1 reduce-scatter.11
  946.8 134.6 reduce-scatter.21
  1084.3 360.8 reduce-scatter.15
  1453.3 243.3 reduce-scatter.13
  1699.4 971.9 reduce-scatter.19
  2674.4 1935.9 reduce-scatter.17
where the time goes:
time: 4630 us
  waiting for transfers between devices  4040 us (87%)
  matrix products  337 us (7%)
  other arithmetic  99.8 us (2%)
  blocking collectives  69.9 us (2%)
  local copies, waits for them, and re-layouts  65.5 us (1%)
    reduce_scatter x1, waiting for transfers between devices, on_device(): lax.psum_scatter(term_gateup, ('wide', 'narrow'), scatter_dimension=0, ti...  1930 us
    reduce_scatter x1, waiting for transfers between devices, on_device(): lax.psum_scatter(term_down, ('wide', 'narrow'), scatter_dimension=0, tile...  972 us
    reduce_scatter x1, waiting for transfers between devices, on_device(): lax.psum_scatter(term_out, ('wide', 'narrow'), scatter_dimension=0, tiled...  362 us
    reduce_scatter x1, waiting for transfers between devices, on_device(): lax.psum_scatter(term_qkv, ('wide', 'narrow'), scatter_dimension=0, tiled...  249 us
    all_gather x1, waiting for transfers between devices, on_device(): lax.all_gather(w_gateup.astype(jnp.bfloat16), ('wide', 'narrow'), axis=0,...  246 us
    all_gather x1, waiting for transfers between devices, on_device(): lax.all_gather(w_down.astype(jnp.bfloat16), ('wide', 'narrow'), axis=0, t...  113 us
  transfers between devices with their start and end apart: 13, of which 12 were waited for; matrix products, arithmetic and copies ran while one was open for 7% of the time, Pallas kernels for 0%

commit v1 on v0

v1 whole, which is shorter than its diff:
```python
import functools

import jax
import jax.numpy as jnp
from jax import lax
from jax.experimental import pallas as pl
from jax.experimental.pallas import tpu as pltpu
from jax.sharding import PartitionSpec as P

HEADS = 16
KV_HEADS = 4
HEAD_DIM = 128
GROUP = HEADS // KV_HEADS
FF = 5632


EPSILON = 1e-05
MOMENTUM = 0.5
AVERAGING = 0.5
STEP_RATE = 0.0003

MESH = pl.DeviceIdType.MESH
MESH_AXES = ("wide", "narrow")
SCORE_SCALE = HEAD_DIM ** (-0.5)
LOG2_E = 1.4426950408889634
MASKED = -1e30


def dot_nt(a, b):
    return lax.dot_general(a, b, (((1,), (1,)), ((), ())), preferred_element_type=jnp.float32)


def dot_tn(a, b):
    return lax.dot_general(a, b, (((0,), (0,)), ((), ())), preferred_element_type=jnp.float32)


def fill_bias(key_code, query_code, query_base, bias):
    rows = query_code.shape[1]

    def chunk(r, carry):
        at = pl.ds(pl.multiple_of(r * rows, 128), rows)
        code = key_code[at, :]
        seen = (code <= query_code[...]) & (code >= query_base[...])
        bias[at, :] = jnp.where(seen, 0.0, MASKED)
        return carry

    lax.fori_loop(0, key_code.shape[0] // rows, chunk, 0)


def attend_kernel(q_ref, k_ref, v_ref, key_code, query_code, query_base, o_ref, total_ref, bias):
    rows = q_ref.shape[0]
    blocks = k_ref.shape[0] // rows

    @pl.when(pl.program_id(0) == 0)
    def _():
        fill_bias(key_code, query_code, query_base, bias)

    def chunk(r, carry):
        at = pl.ds(pl.multiple_of(r * rows, 128), rows)
        keys, values, hidden = k_ref[at, :], v_ref[at, :], bias[at, :]
        out = []
        for h in range(GROUP):
            peak, total, mixed = carry[h]
            query = q_ref[:, h * HEAD_DIM : (h + 1) * HEAD_DIM]
            scores = dot_nt(keys, query) * (SCORE_SCALE * LOG2_E) + hidden
            new_peak = jnp.maximum(peak, jnp.max(scores, axis=0, keepdims=True))
            weights = jnp.exp2(scores - new_peak)
            shrink = jnp.exp2(peak - new_peak)
            total = total * shrink + jnp.sum(weights, axis=0, keepdims=True)
            mixed = mixed * shrink + dot_tn(values, weights.astype(jnp.bfloat16))
            out.append((new_peak, total, mixed))
        return tuple(out)

    start = (
        jnp.full((1, rows), MASKED, jnp.float32),
        jnp.zeros((1, rows), jnp.float32),
        jnp.zeros((HEAD_DIM, rows), jnp.float32),
    )
    done = lax.fori_loop(0, blocks, chunk, (start,) * GROUP)
    for h, (peak, total, mixed) in enumerate(done):
        o_ref[:, h * HEAD_DIM : (h + 1) * HEAD_DIM] = (mixed / total).T.astype(jnp.bfloat16)
        total_ref[0, h : h + 1, :] = peak + jnp.log2(total)


def attend(query, kv, key_code, query_code, query_base):
    rows, width = query.shape
    length = kv.shape[0]
    whole = lambda g: (0, 0)
    return pl.pallas_call(
        attend_kernel,
        grid=(KV_HEADS,),
        in_specs=[
            pl.BlockSpec((rows, GROUP * HEAD_DIM), lambda g: (0, g)),
            pl.BlockSpec((length, HEAD_DIM), lambda g: (0, g)),
            pl.BlockSpec((length, HEAD_DIM), lambda g: (0, KV_HEADS + g)),
            pl.BlockSpec((length, 1), whole),
            pl.BlockSpec((1, rows), whole),
            pl.BlockSpec((1, rows), whole),
        ],
        out_specs=(
            pl.BlockSpec((rows, GROUP * HEAD_DIM), lambda g: (0, g)),
            pl.BlockSpec((1, GROUP, rows), lambda g: (g, 0, 0)),
        ),
        out_shape=(
            jax.ShapeDtypeStruct((rows, width), jnp.bfloat16),
            jax.ShapeDtypeStruct((KV_HEADS, GROUP, rows), jnp.float32),
        ),
        scratch_shapes=[pltpu.VMEM((length, rows), jnp.float32)],
        compiler_params=pltpu.CompilerParams(vmem_limit_bytes=48 * 1024 * 1024),
        cost_estimate=pl.CostEstimate(
            flops=4 * rows * length * width, bytes_accessed=8 * rows * width, transcendentals=HEADS * rows * length
        ),
        name="attend",
    )(query, kv, kv, key_code, query_code, query_base)


def attend_back_kernel(
    q_ref, k_ref, v_ref, do_ref, total_ref, inner_ref, key_code, query_code, query_base,
    dq_ref, dk_ref, dv_ref, bias, dk_sum, dv_sum, dq_sum,
):
    rows = q_ref.shape[0]
    blocks = k_ref.shape[0] // rows

    @pl.when(pl.program_id(0) == 0)
    def _():
        fill_bias(key_code, query_code, query_base, bias)

    for h in range(GROUP):
        lanes = slice(h * HEAD_DIM, (h + 1) * HEAD_DIM)
        query = q_ref[:, lanes]
        grad = do_ref[:, lanes]
        total = total_ref[0, h : h + 1, :]
        inner = inner_ref[0, h : h + 1, :]
        dq_sum[...] = jnp.zeros_like(dq_sum)

        def chunk(r, carry):
            at = pl.ds(pl.multiple_of(r * rows, 128), rows)
            keys = k_ref[at, :]
            scores = dot_nt(keys, query) * (SCORE_SCALE * LOG2_E) + bias[at, :]
            weights = jnp.exp2(scores - total)
            grad_weights = dot_nt(v_ref[at, :], grad)
            grad_scores = (weights * (grad_weights - inner)).astype(jnp.bfloat16)
            dv = jnp.dot(weights.astype(jnp.bfloat16), grad, preferred_element_type=jnp.float32)
            dk = jnp.dot(grad_scores, query, preferred_element_type=jnp.float32)
            if h == 0:
                dv_sum[at, :] = dv
                dk_sum[at, :] = dk
            elif h < GROUP - 1:
                dv_sum[at, :] += dv
                dk_sum[at, :] += dk
            else:
                dv_ref[at, :] = (dv_sum[at, :] + dv).astype(dv_ref.dtype)
                dk_ref[at, :] = ((dk_sum[at, :] + dk) * SCORE_SCALE).astype(dk_ref.dtype)
            dq_sum[...] += dot_tn(keys, grad_scores)
            return carry

        lax.fori_loop(0, blocks, chunk, 0)
        dq_ref[:, lanes] = dq_sum[...].T * SCORE_SCALE


def attend_back(query, kv, grad, total, inner, key_code, query_code, query_base):
    rows, width = query.shape
    length = kv.shape[0]
    whole = lambda g: (0, 0)
    heads = pl.BlockSpec((rows, GROUP * HEAD_DIM), lambda g: (0, g))
    kv_heads = pl.BlockSpec((length, HEAD_DIM), lambda g: (0, g))
    values = pl.BlockSpec((length, HEAD_DIM), lambda g: (0, KV_HEADS + g))
    per_head = pl.BlockSpec((1, GROUP, rows), lambda g: (g, 0, 0))
    return pl.pallas_call(
        attend_back_kernel,
        grid=(KV_HEADS,),
        in_specs=[
            heads, kv_heads, values, heads, per_head, per_head,
            pl.BlockSpec((length, 1), whole),
            pl.BlockSpec((1, rows), whole),
            pl.BlockSpec((1, rows), whole),
        ],
        out_specs=(heads, kv_heads, kv_heads),
        out_shape=(
            jax.ShapeDtypeStruct((rows, width), jnp.float32),
            jax.ShapeDtypeStruct((length, KV_HEADS * HEAD_DIM), jnp.float32),
            jax.ShapeDtypeStruct((length, KV_HEADS * HEAD_DIM), jnp.float32),
        ),
        scratch_shapes=[
            pltpu.VMEM((length, rows), jnp.float32),
            pltpu.VMEM((length, HEAD_DIM), jnp.float32),
            pltpu.VMEM((length, HEAD_DIM), jnp.float32),
            pltpu.VMEM((HEAD_DIM, rows), jnp.float32),
        ],
        compiler_params=pltpu.CompilerParams(vmem_limit_bytes=48 * 1024 * 1024),
        cost_estimate=pl.CostEstimate(
            flops=10 * rows * length * width, bytes_accessed=16 * rows * width, transcendentals=HEADS * rows * length
        ),
        name="attend_back",
    )(query, kv, kv, grad, total, inner, key_code, query_code, query_base)


def gather_kernel(n, qkv_ref, out_ref, ext_ref, trade_ref, qkv_all, out_line, ext_all, came, *sems):
    wide = lax.axis_index("wide")
    z = lax.axis_index("narrow")
    t, core = wide // 2, wide % 2
    send_sems, recv_sems, local_sems = sems
    t_x, t_y, t_d = t ^ 1, t ^ 2, t ^ 3

    def device(place, c=None, along=None):
        return (place * 2 + (core if c is None else c), z if along is None else along)

    by_x, by_y, by_d, sibling = device(t_x), device(t_y), device(t_d), device(t, 1 - core)

    barrier = pltpu.get_barrier_semaphore()
    for other in (by_x, by_y, by_d, sibling):
        pl.semaphore_signal(barrier, inc=1, device_id=other, device_id_type=MESH)

    @pl.when(z > 0)
    def _():
        pl.semaphore_signal(barrier, inc=1, device_id=device(t, along=z - 1), device_id_type=MESH)

    @pl.when(z < n - 1)
    def _():
        pl.semaphore_signal(barrier, inc=1, device_id=device(t, along=z + 1), device_id_type=MESH)

    peers = 4 + (z > 0).astype(jnp.int32) + (z < n - 1).astype(jnp.int32)
    pl.semaphore_wait(barrier, peers)

    count = [0]
    started = []

    def copy(src, dst, to):
        k = count[0]
        count[0] += 1
        return pltpu.make_async_remote_copy(
            src_ref=src, dst_ref=dst, send_sem=send_sems.at[k], recv_sem=recv_sems.at[k],
            device_id=to, device_id_type=MESH,
        )

    def go(moves, when=None):
        if when is None:
            for m in moves:
                m.start()
        else:
            @pl.when(when)
            def _():
                for m in moves:
                    m.start()
        started.append((moves, when))

    def arrive(moves, when=None):
        if when is None:
            for m in moves:
                m.wait_recv()
        else:
            @pl.when(when)
            def _():
                for m in moves:
                    m.wait_recv()

    local = []

    def place(src, dst):
        c = pltpu.make_async_copy(src, dst, local_sems.at[len(local)])
        c.start()
        local.append(c)

    place(qkv_ref, qkv_all.at[t, core, z])
    place(ext_ref, ext_all.at[t, core, z])
    place(out_ref, out_line.at[z])
    place(trade_ref.at[t], came.at[t])
    class Line:
        def __init__(self, view, own=None):
            self.view, self.own = view, own
            self.up, self.down = {}, {}

        def send(self, step):
            zz = z - (step - 1)
            block = self.view(jnp.maximum(zz, 0))
            first = self.own if step == 1 and self.own is not None else None
            up = copy(block if first is None else first, block, device(t, along=jnp.minimum(z + 1, n - 1)))
            self.up[step] = up
            go([up], (zz >= 0) & (z < n - 1))
            zz = z + (step - 1)
            block = self.view(jnp.minimum(zz, n - 1))
            down = copy(block if first is None else first, block, device(t, along=jnp.maximum(z - 1, 0)))
            self.down[step] = down
            go([down], (zz <= n - 1) & (z > 0))

        def take(self, step):
            arrive([self.up[step]], z - step >= 0)
            arrive([self.down[step]], z + step <= n - 1)

    def same(ref, to):
        return copy(ref, ref, to)

    qa, qb, qc = pl.ds(0, 1152), pl.ds(1152, 1152), pl.ds(2304, 768)
    lines = [
        Line(lambda zz, cols=cols: qkv_all.at[t, core, zz, :, cols], qkv_ref.at[:, cols])
        for cols in (qa, qb)
    ]
    line_ext = Line(lambda zz: ext_all.at[t, core, zz], ext_ref)
    line_out = Line(lambda zz: out_line.at[zz], out_ref)
    line_c = Line(lambda zz: qkv_all.at[:, core, zz, :, qc])

    c_x = copy(qkv_ref.at[:, qc], qkv_all.at[t, core, z, :, qc], by_x)
    trade = [copy(trade_ref.at[p], came.at[t], to) for p, to in ((t_x, by_x), (t_y, by_y), (t_d, by_d))]
    for line in lines + [line_ext]:
        line.send(1)
    go([c_x])
    for step in range(1, n):
        for line in lines + [line_ext]:
            line.take(step)
            if step < n - 1:
                line.send(step + 1)
        if step == 1:
            arrive([c_x])
            c_y = [
                copy(qkv_ref.at[:, qc], qkv_all.at[t, core, z, :, qc], by_y),
                same(qkv_all.at[t_x, core, z, :, qc], by_y),
            ]
            go(c_y)
            go(trade[:2])
        if step == 2:
            arrive(c_y)
            for c in local:
                c.wait()
            line_c.send(1)
            go(trade[2:])
    a_y = same(qkv_all.at[t, core, :, :, qa], by_y)
    b_x = same(qkv_all.at[t, core, :, :, qb], by_x)
    e_x = same(ext_all.at[t, core], by_x)
    go([a_y, b_x, e_x])
    own = [same(qkv_all.at[t, core, :, :, pl.ds(0, 2304)], sibling), same(ext_all.at[t, core], sibling)]
    go(own)
    line_c.take(1)
    line_c.send(2)
    arrive([a_y])
    a_x = [same(qkv_all.at[p, core, :, :, qa], by_x) for p in (t, t_y)]
    go(a_x)
    arrive([b_x])
    b_y = [same(qkv_all.at[p, core, :, :, qb], by_y) for p in (t, t_x)]
    go(b_y)
    arrive([e_x])
    e_y = [same(ext_all.at[p, core], by_y) for p in (t, t_x)]
    go(e_y)
    near = [
        same(qkv_all.at[t_y, core, :, :, qa], sibling),
        same(qkv_all.at[t_x, core, :, :, qb], sibling),
        same(ext_all.at[t_x, core], sibling),
    ]
    go(near)
    line_c.take(2)
    line_c.send(3)
    line_out.send(1)
    arrive(e_y)
    far_e = [same(ext_all.at[p, core], sibling) for p in (t_y, t_d)]
    go(far_e)
    line_c.take(3)
    c_all = same(qkv_all.at[:, core, :, :, qc], sibling)
    go([c_all])
    for step in range(1, n):
        line_out.take(step)
        if step < n - 1:
            line_out.send(step + 1)
    arrive(a_x)
    far_a = [same(qkv_all.at[p, core, :, :, qa], sibling) for p in (t_x, t_d)]
    go(far_a)
    arrive(b_y)
    far_b = [same(qkv_all.at[p, core, :, :, qb], sibling) for p in (t_y, t_d)]
    go(far_b)
    arrive(trade)
    arrive(own + near + far_e + [c_all] + far_a + far_b)
    for moves, when in started:
        if when is None:
            for m in moves:
                m.wait_send()
        else:
            @pl.when(when)
            def _(moves=moves):
                for m in moves:
                    m.wait_send()


COPIES = 80


def gather_first(qkv, out, ext, trade, planes, n):
    any_spec = pl.BlockSpec(memory_space=pl.ANY)
    rows = qkv.shape[0]
    low = jnp.bfloat16
    return pl.pallas_call(
        functools.partial(gather_kernel, n),
        out_shape=(
            jax.ShapeDtypeStruct((planes, 2, n, rows, qkv.shape[1]), low),
            jax.ShapeDtypeStruct((n, rows, out.shape[1]), low),
            jax.ShapeDtypeStruct((planes, 2, n) + ext.shape, low),
            jax.ShapeDtypeStruct(trade.shape, low),
        ),
        in_specs=[pl.BlockSpec(memory_space=pltpu.VMEM)] * 4,
        out_specs=(any_spec,) * 4,
        scratch_shapes=[
            pltpu.SemaphoreType.DMA((COPIES,)),
            pltpu.SemaphoreType.DMA((COPIES,)),
            pltpu.SemaphoreType.DMA((4,)),
        ],
        compiler_params=pltpu.CompilerParams(collective_id=0, has_side_effects=True),
        name="gather_first",
    )(qkv, out, ext, trade)


def rotary_tables(positions):
    half_dim = HEAD_DIM // 2
    frequency = jnp.power(10000.0, -2.0 * jnp.arange(half_dim, dtype=jnp.float32) / HEAD_DIM)
    angles = positions[:, None] * frequency[None, :]
    return (jnp.cos(angles)[:, None, :], jnp.sin(angles)[:, None, :])


def rotate_heads(values, cosine_table, sine_table):
    half_dim = HEAD_DIM // 2
    cosine, sine = cosine_table[:, 0], sine_table[:, 0]
    cosine = jnp.concatenate([cosine, cosine], axis=1)
    sine = jnp.concatenate([-sine, sine], axis=1)
    done = []
    for start in range(0, values.shape[1], HEAD_DIM):
        head = values[:, start : start + HEAD_DIM]
        done.append(head * cosine + jnp.roll(head, half_dim, axis=1) * sine)
    return jnp.concatenate(done, axis=1)


def norm_forward(values_in, gain_row):
    inverse = lax.rsqrt(jnp.mean(values_in * values_in, axis=-1, keepdims=True) + EPSILON)
    return (values_in * inverse * gain_row, inverse)


def norm_backward(values_in, inverse, gain_row, incoming):
    scaled_grad = incoming * gain_row
    return inverse * scaled_grad - values_in * inverse * inverse * inverse * jnp.mean(
        scaled_grad * values_in, axis=-1, keepdims=True
    )


def advance_state(weight, moment, average, gradient):
    moment_next = MOMENTUM * moment + gradient
    weight_next = weight - STEP_RATE * (gradient + MOMENTUM * moment_next)
    average_next = AVERAGING * average + (1.0 - AVERAGING) * weight_next
    return (weight_next, moment_next, average_next)


class Links:
    def __init__(self):
        self.wide = lax.axis_size("wide")
        self.n = lax.axis_size("narrow")
        self.planes = self.wide // 2
        self.wide_at = lax.axis_index("wide")
        self.z_at = lax.axis_index("narrow")
        self.t_at = self.wide_at // 2
        self.core_at = self.wide_at % 2
        self.bits = [1 << k for k in range(self.planes.bit_length() - 1)]
        per_chip = 2 * self.n
        self.same_chip = [[t * per_chip + j for j in range(per_chip)] for t in range(self.planes)]
        self.same_plane = [
            [t * per_chip + j for t in range(self.planes)] for j in range(per_chip)
        ]

    def swap(self, values, flip):
        pairs = [(i, i ^ (flip * self.n)) for i in range(self.wide * self.n)]
        return lax.ppermute(values, MESH_AXES, pairs)

    def shift(self, values, step):
        pairs = [
            (w * self.n + z, w * self.n + z + step)
            for w in range(self.wide)
            for z in range(self.n)
            if 0 <= z + step < self.n
        ]
        return lax.ppermute(values, MESH_AXES, pairs)

    def column_cuts(self, cols):
        lanes = cols // 128
        count = len(self.bits)
        edges = [128 * (lanes * k // count) for k in range(count + 1)]
        orders = [self.bits[k:] + self.bits[:k] for k in range(count)]
        return list(zip(edges[:-1], edges[1:], orders))

    def gather_planes(self, line):
        rows, cols = line.shape
        whole = jnp.zeros((self.wide, rows, cols), line.dtype)
        for low, high, order in self.column_cuts(cols):
            held = {0: line[:, low:high]}
            for bit in order:
                held.update({d | bit: self.swap(v, 2 * bit) for d, v in list(held.items())})
            for d, v in held.items():
                for flip, piece in ((2 * d, v), (2 * d + 1, self.swap(v, 1))):
                    whole = lax.dynamic_update_slice(whole, piece[None], (self.wide_at ^ flip, 0, low))
        return whole.reshape(self.wide * rows, cols)

    def scatter_core(self, term):
        mine = lax.dynamic_index_in_dim(term, self.core_at, 1, keepdims=False)
        other = lax.dynamic_index_in_dim(term, 1 - self.core_at, 1, keepdims=False)
        got = self.swap(other, 1)
        return (mine.astype(jnp.float32) + got.astype(jnp.float32)).astype(jnp.bfloat16)

    def scatter_rows(self, term):
        rows, cols = term.shape
        term = term.reshape(self.planes, 2, rows // self.wide, cols)
        term = self.scatter_core(term)
        parts = []
        for low, high, order in self.column_cuts(cols):
            part = term[:, :, low:high]
            left = sorted(self.bits, reverse=True)
            part = part.reshape((2,) * len(left) + part.shape[1:])
            for bit in order:
                axis = left.index(bit)
                my_bit = (self.t_at // bit) % 2
                mine = lax.dynamic_index_in_dim(part, my_bit, axis, keepdims=False)
                other = lax.dynamic_index_in_dim(part, 1 - my_bit, axis, keepdims=False)
                got = self.swap(other, 2 * bit)
                part = (mine.astype(jnp.float32) + got.astype(jnp.float32)).astype(jnp.bfloat16)
                left.remove(bit)
            parts.append(part)
        total = jnp.concatenate(parts, axis=1)
        return lax.psum_scatter(total, "narrow", scatter_dimension=0, tiled=True)

    def gather_tokens(self, rows):
        if self.planes != 4:
            every = lax.all_gather(
                rows, MESH_AXES, axis=0, tiled=False, axis_index_groups=self.same_plane
            )
            return [every[k] for k in range(self.planes)]
        half = rows.shape[0] // 2
        by_x = self.swap(rows, 2)
        by_y = self.swap(rows, 4)
        corner = [self.swap(by_y[:half], 2), self.swap(by_x[half:], 4)]
        return [rows, by_x, by_y, jnp.concatenate(corner)]

    def scatter_tokens(self, blocks):
        if self.planes != 4:
            every = jnp.concatenate([b.astype(jnp.bfloat16) for b in blocks])
            total = lax.psum_scatter(
                every, MESH_AXES, scatter_dimension=0, tiled=True, axis_index_groups=self.same_plane
            )
            return total.astype(jnp.float32)
        own, by_x, by_y, corner = blocks
        half = own.shape[0] // 2
        corner = corner.astype(jnp.bfloat16)
        top = self.swap(corner[:half], 2).astype(jnp.float32)
        bottom = self.swap(corner[half:], 4).astype(jnp.float32)
        by_y = jnp.concatenate([by_y[:half] + top, by_y[half:]]).astype(jnp.bfloat16)
        by_x = jnp.concatenate([by_x[:half], by_x[half:] + bottom]).astype(jnp.bfloat16)
        return (
            own
            + self.swap(by_x, 2).astype(jnp.float32)
            + self.swap(by_y, 4).astype(jnp.float32)
        )

    def trade_columns(self, pieces):
        came = jnp.zeros_like(pieces)
        for d in range(self.planes):
            piece = lax.dynamic_index_in_dim(pieces, self.t_at ^ d, 0)
            if d:
                piece = self.swap(piece, 2 * d)
            came = lax.dynamic_update_slice(came, piece, (self.t_at ^ d, 0, 0))
        return came

    def keys_before(self, own):
        blocks = [own]
        for _ in range(self.n - 1):
            blocks.append(self.shift(blocks[-1], 1))
        return blocks

    def keys_back(self, terms):
        got = None
        for r in range(self.n - 1, 0, -1):
            term = terms[r] if got is None else terms[r] + got
            got = self.shift(term.astype(jnp.bfloat16), -1).astype(jnp.float32)
        return terms[0] if got is None else terms[0] + got

    def gather_first(self, qkv, out, gains, count, trade):
        rows = qkv.shape[0]
        if self.planes == 4 and self.n > 1:
            digits = jnp.stack([count // 16, count % 16]).astype(jnp.bfloat16)
            ext = jnp.concatenate([gains.reshape(1, 2 * rows), jnp.zeros((15, 2 * rows), gains.dtype)])
            ext = lax.dynamic_update_slice(ext, digits[None], (1, 0))
            qkv_all, out_line, ext_all, came = gather_first(qkv, out, ext, trade, self.planes, self.n)
            ext_all = ext_all.reshape(self.wide * self.n, 16, 2 * rows)
            gain_full = ext_all[:, 0].reshape(-1, 2, rows).transpose(1, 0, 2).reshape(2, -1)
            digits = ext_all[:, 1, :2].astype(jnp.int32)
            most = jnp.max(digits[:, 0] * 16 + digits[:, 1])
            return (
                qkv_all.reshape(self.wide * self.n * rows, -1),
                out_line.reshape(self.n * rows, -1),
                gain_full,
                most,
                came,
            )
        return (
            lax.all_gather(qkv, MESH_AXES, axis=0, tiled=True),
            lax.all_gather(out, "narrow", axis=0, tiled=True),
            lax.all_gather(gains, MESH_AXES, axis=1, tiled=True),
            lax.pmax(count, MESH_AXES),
            self.trade_columns(trade),
        )


def dot32(a, b):
    return jnp.dot(a, b, preferred_element_type=jnp.float32)


def dot_low(a, b):
    return jnp.dot(a, b, preferred_element_type=jnp.float32).astype(jnp.bfloat16)


def pick_live(mask, cap):
    flat = mask.reshape(-1)
    rows = flat.shape[0]
    at = jnp.arange(rows, dtype=jnp.int32)
    rank = jnp.sum(jnp.where(at[None, :] <= at[:, None], flat[None, :], 0), axis=1) - 1
    slot = jnp.arange(cap, dtype=jnp.int32)
    chosen = (rank[None, :] == slot[:, None]) & (flat[None, :] == 1)
    return chosen, slot < jnp.sum(flat)


def layer(links, cap, given):
    (
        tokens,
        active,
        cotangent,
        gain_full,
        qkv_low,
        out_line,
        pieces,
        w_down,
    ) = given
    n, planes = links.n, links.planes
    seq_count, span_len, width = tokens.shape
    row_count = seq_count * span_len
    seq_len = n * span_len
    kv_width = KV_HEADS * HEAD_DIM
    ff_part = FF // planes
    shard_rows = pieces.shape[1]
    low = jnp.bfloat16

    gateup_low = lax.all_gather(
        pieces, MESH_AXES, axis=1, tiled=True, axis_index_groups=links.same_chip
    ).reshape(width, 2 * ff_part)
    down_low = lax.all_gather(
        w_down, MESH_AXES, axis=0, tiled=True, axis_index_groups=links.same_chip
    )
    out_low = links.gather_planes(out_line)

    def codes_of(block):
        mask = lax.dynamic_slice_in_dim(active, jnp.maximum(block, 0) * span_len, span_len, 1)
        chosen, live = pick_live(mask, cap)
        code = jnp.arange(seq_count, dtype=jnp.int32)[:, None] * seq_len + jnp.arange(span_len, dtype=jnp.int32)
        code = jnp.sum(jnp.where(chosen, code.reshape(1, -1), 0), axis=1) + block * span_len
        return chosen, live & (block >= 0), code

    chosen, live, own_code = codes_of(links.z_at)
    key_codes = []
    for r in range(n):
        _, there, code = codes_of(links.z_at - r)
        key_codes.append(jnp.where(there, code, seq_count * seq_len))
    key_code = jnp.concatenate(key_codes)[:, None]
    query_code = jnp.where(live, own_code, -1)[None]
    query_base = jnp.where(live, own_code // seq_len * seq_len, 0)[None]
    places = jnp.where(live, own_code % seq_len, 0).astype(jnp.float32)
    cosine_table, sine_table = rotary_tables(places)
    picker = chosen.astype(low)
    live_rows = live.astype(jnp.float32)[:, None]

    inputs = dot32(picker, tokens.reshape(row_count, width))
    down_grad = dot_low(picker, cotangent.reshape(row_count, width))
    upstream = down_grad.astype(jnp.float32)
    down_grad_blocks = links.gather_tokens(down_grad)

    normed, inverse_one = norm_forward(inputs, gain_full[0])
    normed_low = normed.astype(low)
    kv_part = dot32(normed_low, qkv_low[:, width:])
    kv_low = jnp.concatenate(
        [rotate_heads(kv_part[:, :kv_width], cosine_table, sine_table), kv_part[:, kv_width:]], axis=1
    ).astype(low)
    kv_all = jnp.concatenate(links.keys_before(kv_low))
    query_low = rotate_heads(dot32(normed_low, qkv_low[:, :width]), cosine_table, sine_table).astype(low)
    attended_low, totals = attend(query_low, kv_all, key_code, query_code, query_base)
    middle = inputs + live_rows * dot32(attended_low, out_low)
    normed_mid, inverse_two = norm_forward(middle, gain_full[1])
    blocks = links.gather_tokens(normed_mid.astype(low))

    down_terms, mid_terms, hidden_blocks, gateup_grad_blocks = [], [], [], []
    for block, down_grad_block in zip(blocks, down_grad_blocks):
        gate_part = dot32(block, gateup_low[:, :ff_part])
        upper_part = dot32(block, gateup_low[:, ff_part:])
        gate_sigmoid = jax.nn.sigmoid(gate_part)
        hidden = (gate_part * gate_sigmoid * upper_part).astype(low)
        grad_hidden = dot32(down_grad_block, down_low.T)
        grad_gate = grad_hidden * upper_part * gate_sigmoid * (1.0 + gate_part * (1.0 - gate_sigmoid))
        grad_upper = grad_hidden * gate_part * gate_sigmoid
        grad_gateup_low = jnp.concatenate([grad_gate, grad_upper], axis=1).astype(low)
        hidden_blocks.append(hidden)
        gateup_grad_blocks.append(grad_gateup_low)
        down_terms.append(dot32(hidden, down_low))
        mid_terms.append(dot32(grad_gateup_low, gateup_low.T))
    grad_normed_mid = links.scatter_tokens(mid_terms)

    term_down = dot_low(jnp.concatenate(hidden_blocks).T, jnp.concatenate(down_grad_blocks))
    term_gateup = dot_low(jnp.concatenate(blocks).T, jnp.concatenate(gateup_grad_blocks))
    down_half = links.scatter_core(term_down.reshape(1, 2, ff_part // 2, width))[0]
    gateup_half = links.scatter_core(term_gateup.reshape(planes, 2, n * shard_rows, 2 * ff_part))
    grad_down = lax.psum_scatter(down_half, "narrow", scatter_dimension=0, tiled=True)
    grad_pieces = lax.psum_scatter(gateup_half, "narrow", scatter_dimension=1, tiled=True)
    down_proj = links.scatter_tokens(down_terms)
    layer_out = (middle + down_proj).astype(low)

    grad_middle = upstream + norm_backward(middle, inverse_two, gain_full[1], grad_normed_mid)
    branch_grad_low = grad_middle.astype(low)
    branch_grad_low, down_half, gateup_half = lax.optimization_barrier(
        (branch_grad_low, down_half, gateup_half)
    )
    grad_attended_low = dot_low(branch_grad_low, out_low.T)
    grad_out = links.scatter_rows(dot_low(attended_low.T, branch_grad_low))
    inner = jnp.sum(
        (grad_attended_low.astype(jnp.float32) * attended_low.astype(jnp.float32)).reshape(
            cap, HEADS, HEAD_DIM
        ),
        axis=-1,
    )
    inner = inner.T.reshape(KV_HEADS, GROUP, cap)
    grad_query, key_term, value_term = attend_back(
        query_low, kv_all, grad_attended_low, totals, inner, key_code, query_code, query_base
    )
    kv_terms = [
        jnp.concatenate([key_term[r * cap : (r + 1) * cap], value_term[r * cap : (r + 1) * cap]], axis=1)
        for r in range(n)
    ]
    grad_kv = links.keys_back(kv_terms)
    grad_query_low = rotate_heads(grad_query, cosine_table, -sine_table).astype(low)
    grad_q_rows = links.scatter_rows(dot_low(normed_low.T, grad_query_low))
    grad_kv_low = jnp.concatenate(
        [rotate_heads(grad_kv[:, :kv_width], cosine_table, -sine_table), grad_kv[:, kv_width:]], axis=1
    ).astype(low)
    grad_kv_rows = links.scatter_rows(dot_low(normed_low.T, grad_kv_low))
    grad_normed = dot32(grad_query_low, qkv_low[:, :width].T) + dot32(grad_kv_low, qkv_low[:, width:].T)
    grad_tokens = (
        grad_middle + norm_backward(inputs, inverse_one, gain_full[0], grad_normed)
    ).astype(low)

    def spread(packed, skipped):
        back = lax.dot_general(
            picker, packed, (((0,), (0,)), ((), ())), preferred_element_type=jnp.float32
        ).astype(low)
        mask = lax.dynamic_slice_in_dim(active, links.z_at * span_len, span_len, 1)
        return jnp.where(mask[:, :, None] == 1, back.reshape(skipped.shape), skipped)

    layer_out, grad_tokens = spread(layer_out, tokens), spread(grad_tokens, cotangent)
    grad_pieces = links.trade_columns(grad_pieces).reshape(planes, shard_rows, 2, ff_part)
    grad_gateup = grad_pieces.transpose(1, 2, 0, 3).reshape(shard_rows, 2 * FF)
    grad_qkv = jnp.concatenate([grad_q_rows, grad_kv_rows], axis=1)
    return layer_out, grad_tokens, grad_qkv, grad_out, grad_gateup, grad_down


def on_device(
    tokens,
    active,
    cotangent,
    gain_rows,
    w_qkv,
    w_out,
    w_gateup,
    w_down,
    moment_gains,
    moment_qkv,
    moment_out,
    moment_gateup,
    moment_down,
    average_gains,
    average_qkv,
    average_out,
    average_gateup,
    average_down,
):
    links = Links()
    planes = links.planes
    seq_count, span_len, _ = tokens.shape
    row_count = seq_count * span_len
    ff_part = FF // planes
    low = jnp.bfloat16

    gains_low = gain_rows.astype(low)
    shard_rows = w_gateup.shape[0]
    gateup_shard = w_gateup.astype(low)
    pieces = gateup_shard.reshape(shard_rows, 2, planes, ff_part)
    pieces = pieces.transpose(2, 0, 1, 3).reshape(planes, shard_rows, 2 * ff_part)
    qkv_shard = w_qkv.astype(low)
    own_mask = lax.dynamic_slice_in_dim(active, links.z_at * span_len, span_len, 1)
    qkv_low, out_line, gain_full, most, pieces = links.gather_first(
        qkv_shard, w_out.astype(low), gains_low, jnp.sum(own_mask), pieces
    )
    gain_full = gain_full.astype(jnp.float32)
    given = (tokens, active, cotangent, gain_full, qkv_low, out_line, pieces, w_down.astype(low))
    few = -(-3 * row_count // 4 // 128) * 128
    if few < row_count:
        found = lax.cond(
            most <= few,
            lambda *g: layer(links, few, g),
            lambda *g: layer(links, row_count, g),
            *given,
        )
    else:
        found = layer(links, row_count, given)
    layer_out, grad_tokens, grad_qkv, grad_out, grad_gateup, grad_down = found
    grad_qkv, grad_out, grad_gateup, grad_down = (
        g.astype(jnp.float32) for g in (grad_qkv, grad_out, grad_gateup, grad_down)
    )

    def gain_grad(shard, gradient, row):
        return jnp.sum(shard.astype(jnp.float32) * gradient, axis=1) / gains_low[row].astype(jnp.float32)

    grad_gains = jnp.stack([gain_grad(qkv_shard, grad_qkv, 0), gain_grad(gateup_shard, grad_gateup, 1)])
    state_gains = advance_state(gain_rows, moment_gains, average_gains, grad_gains)
    state_qkv = advance_state(w_qkv, moment_qkv, average_qkv, grad_qkv)
    state_out = advance_state(w_out, moment_out, average_out, grad_out)
    state_gateup = advance_state(w_gateup, moment_gateup, average_gateup, grad_gateup)
    state_down = advance_state(w_down, moment_down, average_down, grad_down)
    return (
        layer_out,
        grad_tokens,
        grad_gains,
        grad_qkv,
        grad_out,
        grad_gateup,
        grad_down,
        state_gains[0],
        state_qkv[0],
        state_out[0],
        state_gateup[0],
        state_down[0],
        state_gains[1],
        state_qkv[1],
        state_out[1],
        state_gateup[1],
        state_down[1],
        state_gains[2],
        state_qkv[2],
        state_out[2],
        state_gateup[2],
        state_down[2],
    )


def solution(mesh):
    in_specs = (
        P("wide", "narrow", None),
        P("wide", None),
        P("wide", "narrow", None),
        P(None, ("wide", "narrow")),
        P(("wide", "narrow"), None),
        P(("wide", "narrow"), None),
        P(("wide", "narrow"), None),
        P(("wide", "narrow"), None),
        P(None, ("wide", "narrow")),
        P(("wide", "narrow"), None),
        P(("wide", "narrow"), None),
        P(("wide", "narrow"), None),
        P(("wide", "narrow"), None),
        P(None, ("wide", "narrow")),
        P(("wide", "narrow"), None),
        P(("wide", "narrow"), None),
        P(("wide", "narrow"), None),
        P(("wide", "narrow"), None),
    )
    out_specs = (
        P("wide", "narrow", None),
        P("wide", "narrow", None),
        P(None, ("wide", "narrow")),
        P(("wide", "narrow"), None),
        P(("wide", "narrow"), None),
        P(("wide", "narrow"), None),
        P(("wide", "narrow"), None),
        P(None, ("wide", "narrow")),
        P(("wide", "narrow"), None),
        P(("wide", "narrow"), None),
        P(("wide", "narrow"), None),
        P(("wide", "narrow"), None),
        P(None, ("wide", "narrow")),
        P(("wide", "narrow"), None),
        P(("wide", "narrow"), None),
        P(("wide", "narrow"), None),
        P(("wide", "narrow"), None),
        P(None, ("wide", "narrow")),
        P(("wide", "narrow"), None),
        P(("wide", "narrow"), None),
        P(("wide", "narrow"), None),
        P(("wide", "narrow"), None),
    )
    return jax.shard_map(
        on_device, mesh=mesh, in_specs=in_specs, out_specs=out_specs, check_vma=False
    )
```

time: 4630 us -> 1040 us (0.22)
  waiting for transfers between devices: 4040 us -> 304 us
  Pallas kernels: 0 us -> 163 us
  matrix products: 337 us -> 230 us
  starting transfers between devices: 1.53 us -> 72.7 us
  blocking collectives: 69.9 us -> 0 us
  local copies, waits for them, and re-layouts: 65.5 us -> 124 us
    reduce_scatter x6 -> x5, waiting for transfers between devices: 3550 us -> 12.6 us  [the longest x3 12.6 us: scatter_rows(): return lax.psum_scatter(total, 'narrow', scatter_dimension=0, tiled=True)]
    all_gather x6 -> x2, waiting for transfers between devices: 467 us -> 0.01 us  [the longest x1 0.01 us: layer(): lax.all_gather(pieces, MESH_AXES, axis=1, tiled=True, axis_index_groups=l...]
    ppermute x0 -> x56, waiting for transfers between devices: none -> 290 us  [the longest x6 164 us: shift(): return lax.ppermute(values, MESH_AXES, pairs)]
    pallas_call x0 -> x3, Pallas kernels: none -> 163 us  [the longest x1 91.6 us: gather_first(): pl.pallas_call(functools.partial(gather_kernel, n), out_shape=(jax.ShapeD...]
    dot_general x18 -> x34, matrix products: 337 us -> 230 us  [the longest x25 143 us: dot32(): return jnp.dot(a, b, preferred_element_type=jnp.float32)]
    ppermute x0 -> x56, starting transfers between devices: none -> 72.3 us  [the longest x50 41.6 us: swap(): return lax.ppermute(values, MESH_AXES, pairs)]
    all_gather x1 -> x0, blocking collectives: 69.9 us -> none  [on_device(): lax.all_gather(gain_rows.astype(jnp.bfloat16), ('wide', 'narrow'), axis=1...]
  transfers between devices with their start and end apart: 13 -> 63, of which waited for: 12 -> 22; matrix products, arithmetic and copies ran while one was open for 7% -> 30% of each run, Pallas kernels for 0% -> 7%
where the time goes in v1:
time: 1040 us; the launch traced here: 1030 us
  waiting for transfers between devices  304 us (29%)
  matrix products  230 us (22%)
  Pallas kernels  163 us (16%)
  local copies, waits for them, and re-layouts  124 us (12%)
  other arithmetic  112 us (11%)
  starting transfers between devices  72.7 us (7%)
  between operations  17.8 us (2%)
    ppermute x6, waiting for transfers between devices, shift(): return lax.ppermute(values, MESH_AXES, pairs)  164 us
    dot_general x25, matrix products, dot32(): return jnp.dot(a, b, preferred_element_type=jnp.float32)  143 us
    ppermute x50, waiting for transfers between devices, swap(): return lax.ppermute(values, MESH_AXES, pairs)  126 us
    pallas_call x1, Pallas kernels, gather_first(): pl.pallas_call(functools.partial(gather_kernel, n), out_shape=(jax.ShapeD...  91.6 us
    dot_general x7, matrix products, dot_low(): jnp.dot(a, b, preferred_element_type=jnp.float32).astype(jnp.bfloat16)  70.2 us
    ppermute x50, starting transfers between devices, swap(): return lax.ppermute(values, MESH_AXES, pairs)  41.6 us
    pallas_call x1, Pallas kernels, attend_back(): pl.pallas_call(attend_back_kernel, grid=(KV_HEADS,), in_specs=[heads, kv_...  40.7 us
    unnamed x250, local copies, waits for them, and re-layouts  35.2 us
  transfers between devices with their start and end apart: 63, of which 22 were waited for; matrix products, arithmetic and copies ran while one was open for 30% of the time, Pallas kernels for 7%

profile of v1, /device:TPU:0, one launch (start us, length us, event | category | flops | bytes accessed | tf_op | source)
XLA Modules:
  0.0 1030.6 jit_solution(14209923708474416325)
XLA Ops:
  25.6 91.6 %gather_first.1 = (bf16[4,2,4,64,3072]{4,3,2,1,0:T(8,128)(2,1)}, bf16[4,64,2048]{2,1,0:T(8,128)(2,1)S(1)}, bf16[4,2,4,16,128]{4,3,2,1,0:T(8,128)(2,1)}, bf16[4,64,2816]{2,1,0:T(8,128)(2,1)}) custom-call(bf16[64,3072]{1,0:T(8,128)(2,1)} %convert_element_type.809.qkv_ref, bf16[64,2048]{1,0:T(8,128)(2,1)} %convert_element_type.810.out_ref, ...), custom_call_target="tpu_custom_call" | custom-call | tf_op jit(solution)/shard_map/gather_first/pallas_call | solution.py:388
  120.4 884.4 %conditional.3 = (bf16[2,256,2048]{2,1,0:T(8,128)(2,1)}, bf16[2,256,2048]{2,1,0:T(8,128)(2,1)}, f32[64,3072]{1,0:T(8,128)}, f32[64,2048]{1,0:T(8,128)S(1)}, f32[...) conditional(s32[]{:T(128)} %convert_element_type.815, (s32[]{:T(128)}, s32[2,1024]{1,0:T(2,128)S(1)}, ...), branch_computations={%region_2.25_spmd, %region_25.48_spmd} | conditional | flops 173283475456 | bytes 2316326400
  185.1 13.2 %collective-permute-done.56 = bf16[384,1024]{1,0:T(8,128)(2,1)S(1)} collective-permute-done((bf16[384,1024]{1,0:T(8,128)(2,1)S(1)}, bf16[384,1024]{1,0:T(8,128)(2,1)S(1)}, u32[]{:S(2)}, u32[]{:S(2)}) %collective-permute-start.56) | collective-permute-done | bytes 786464 | tf_op jit(solution)/shard_map/cond/branch_1_fun/ppermute | solution.py:473
  211.5 25.7 %collective-permute-done.57 = bf16[384,1024]{1,0:T(8,128)(2,1)S(1)} collective-permute-done((bf16[384,1024]{1,0:T(8,128)(2,1)S(1)}, bf16[384,1024]{1,0:T(8,128)(2,1)S(1)}, u32[]{:S(2)}, u32[]{:S(2)}) %collective-permute-start.57) | collective-permute-done | bytes 786464 | tf_op jit(solution)/shard_map/cond/branch_1_fun/ppermute | solution.py:473
  237.3 20.9 %collective-permute-start.58 = (bf16[384,1024]{1,0:T(8,128)(2,1)S(1)}, bf16[384,1024]{1,0:T(8,128)(2,1)S(1)}, u32[]{:S(2)}, u32[]{:S(2)}) collective-permute-start(bf16[384,1024]{1,0:T(8,128)(2,1)S(1)} %collective-permute-done.57), channel_id=1, source_target_pairs={{0,1},{1,2},{2,3},{4,5},{5,6},{6,7},{8,9},{9,10},{10,11},{12,13},{... | collective-permute-start | bytes 2359304 | tf_op jit(solution)/shard_map/cond/branch_1_fun/ppermute | solution.py:473
  261.6 30.9 %collective-permute-done.58 = bf16[384,1024]{1,0:T(8,128)(2,1)S(1)} collective-permute-done((bf16[384,1024]{1,0:T(8,128)(2,1)S(1)}, bf16[384,1024]{1,0:T(8,128)(2,1)S(1)}, u32[]{:S(2)}, u32[]{:S(2)}) %collective-permute-start.58) | collective-permute-done | bytes 786464 | tf_op jit(solution)/shard_map/cond/branch_1_fun/ppermute | solution.py:473
  294.4 30.5 %attend.3 = (bf16[384,2048]{1,0:T(8,128)(2,1)S(1)}, f32[4,4,384]{2,1,0:T(4,128)S(1)}) custom-call(bf16[384,2048]{1,0:T(8,128)(2,1)S(1)} %get-tuple-element.682.q_ref, bf16[1536,1024]{1,0:T(8,128)(2,1)} %pad_maximum_fusion.12.k_ref.v_ref, bf16[1536,1024]{1,0:T(8,128)(2,1)} %pad_maximum_fusion.12.k_ref.v_ref, s32[1536,1]{1,0:T(8,128)S(1)} %broadcast_in_dim.371.key_code, ...), custom_call_target="tpu_custom_call" | custom-call | flops 4831838208 | bytes 6291456 | tf_op jit(solution)/shard_map/cond/branch_1_fun/attend/pallas_call | solution.py:89
  345.5 23.3 %collective-permute-done.74 = bf16[384,2048]{1,0:T(8,128)(2,1)S(1)} collective-permute-done((bf16[384,2048]{1,0:T(8,128)(2,1)}, bf16[384,2048]{1,0:T(8,128)(2,1)S(1)}, u32[]{:S(2)}, u32[]{:S(2)}) %collective-permute-start.74) | collective-permute-done | bytes 1572896 | tf_op jit(solution)/shard_map/cond/branch_1_fun/ppermute | solution.py:464
  370.5 16.8 %collective-permute-done.83 = bf16[192,2048]{1,0:T(8,128)(2,1)} collective-permute-done((bf16[192,2048]{1,0:T(8,128)(2,1)}, bf16[192,2048]{1,0:T(8,128)(2,1)}, u32[]{:S(2)}, u32[]{:S(2)}) %collective-permute-start.83) | collective-permute-done | bytes 786464 | tf_op jit(solution)/shard_map/cond/branch_1_fun/ppermute | solution.py:464
  448.8 10.9 %convolution_convert_fusion.18 = bf16[384,2048]{1,0:T(8,128)(2,1)} fusion(bf16[2048,2816]{1,0:T(8,128)(2,1)} %bitcast.558, bf16[384,1408]{1,0:T(8,128)(2,1)} %get-tuple-element.565, bf16[384,1408]{1,0:T(8,128)(2,1)} %get-tuple-element.563), kind=kOutput, calls=%fused_computation.595 | convolution fusion | flops 4434296832 | bytes 15269888 | tf_op jit(solution)/shard_map/cond/branch_1_fun/dot_general | solution.py:603
  459.7 9.6 multiply_convert_fusion.23
  484.1 29.6 %convolution_convert_fusion.10 = bf16[2048,2816]{1,0:T(8,128)(2,1)} fusion(bf16[1536,2048]{1,0:T(8,128)(2,1)} %get-tuple-element.671, bf16[384,1408]{1,0:T(8,128)(2,1)} %get-tuple-element.565, bf16[384,1408]{1,0:T(8,128)(2,1)} %get-tuple-element.563, bf16[384,1408]{1,0:T(8,128)(2,1)} %get-tuple-element.568, bf16[384,1408]{1,0:T(8,128)(2,1)} %get-tuple-element.566, ...), kind=kOutput, calls=%fused_computation.514 | convolution fusion | flops 17791713280 | bytes 26476544 | tf_op jit(solution)/shard_map/cond/branch_1_fun/dot_general | solution.py:607
  544.0 15.2 %convolution_convert_fusion.13 = bf16[1408,2048]{1,0:T(8,128)(2,1)} fusion(bf16[1536,2048]{1,0:T(8,128)(2,1)} %constant_dynamic-update-slice_fusion.37, bf16[384,1408]{1,0:T(8,128)(2,1)} %get-tuple-element.564, bf16[384,1408]{1,0:T(8,128)(2,1)} %get-tuple-element.567, bf16[384,1408]{1,0:T(8,128)(2,1)} %get-tuple-element.561, ...), kind=kOutput, calls=%fused_computation.536 | convolution fusion | flops 8878555136 | bytes 16384000 | tf_op jit(solution)/shard_map/cond/branch_1_fun/dot_general | solution.py:607
  592.9 18.7 %collective-permute-done.88 = bf16[384,2048]{1,0:T(8,128)(2,1)S(1)} collective-permute-done((bf16[384,2048]{1,0:T(8,128)(2,1)S(1)}, bf16[384,2048]{1,0:T(8,128)(2,1)S(1)}, u32[]{:S(2)}, u32[]{:S(2)}) %collective-permute-start.88) | collective-permute-done | bytes 1572896 | tf_op jit(solution)/shard_map/cond/branch_1_fun/ppermute | solution.py:464
  616.3 11.0 %multiply_reduce_fusion.5 = (f32[384]{0:T(512)S(1)}, f32[384,2048]{1,0:T(8,128)S(1)}) fusion(f32[384,2048]{1,0:T(8,128)S(1)} %copy-done.36, f32[2048]{0:T(1024)S(1)} %copy-done.151, bf16[384,2048]{1,0:T(8,128)(2,1)} %copy-done.184, bf16[384,2048]{1,0:T(8,128)(2,1)} %collective-permute-done.86, bf16[2048,2816]{1,0:T(8,128)(2,1)} %bitcast.562, ...), kind=kOutput, calls=%fused_computation.582 | convolution fusion | flops 4439014912 | bytes 23143936 | tf_op jit(solution)/shard_map/cond/branch_1_fun/dot_general | solution.py:603
  653.7 40.7 %attend_back.3 = (f32[384,2048]{1,0:T(8,128)}, f32[1536,512]{1,0:T(8,128)}, f32[1536,512]{1,0:T(8,128)}) custom-call(bf16[384,2048]{1,0:T(8,128)(2,1)S(1)} %copy-done.13, bf16[1536,1024]{1,0:T(8,128)(2,1)} %pad_maximum_fusion.12.k_ref.v_ref, bf16[1536,1024]{1,0:T(8,128)(2,1)} %pad_maximum_fusion.12.k_ref.v_ref, ...), custom_call_target="tpu_custom_call" | custom-call | flops 12079595520 | bytes 12582912 | tf_op jit(solution)/shard_map/cond/branch_1_fun/attend_back/pallas_call | solution.py:169
  703.1 31.6 %collective-permute-done.91 = bf16[384,1024]{1,0:T(8,128)(2,1)S(1)} collective-permute-done((bf16[384,1024]{1,0:T(8,128)(2,1)S(1)}, bf16[384,1024]{1,0:T(8,128)(2,1)S(1)}, u32[]{:S(2)}, u32[]{:S(2)}) %collective-permute-start.91) | collective-permute-done | bytes 786464 | tf_op jit(solution)/shard_map/cond/branch_1_fun/ppermute | solution.py:473
  745.7 20.7 %collective-permute-done.92 = bf16[384,1024]{1,0:T(8,128)(2,1)} collective-permute-done((bf16[384,1024]{1,0:T(8,128)(2,1)}, bf16[384,1024]{1,0:T(8,128)(2,1)}, u32[]{:S(2)}, u32[]{:S(2)}) %collective-permute-start.92) | collective-permute-done | bytes 786464 | tf_op jit(solution)/shard_map/cond/branch_1_fun/ppermute | solution.py:473
  773.8 41.6 %collective-permute-done.93 = bf16[384,1024]{1,0:T(8,128)(2,1)S(1)} collective-permute-done((bf16[384,1024]{1,0:T(8,128)(2,1)S(1)}, bf16[384,1024]{1,0:T(8,128)(2,1)S(1)}, u32[]{:S(2)}, u32[]{:S(2)}) %collective-permute-start.93) | collective-permute-done | bytes 786464 | tf_op jit(solution)/shard_map/cond/branch_1_fun/ppermute | solution.py:473
  850.8 9.2 convolution_convert_fusion.16
  862.7 15.4 %collective-permute-done.100 = bf16[2,256,512]{2,1,0:T(8,128)(2,1)} collective-permute-done((bf16[2,256,512]{2,1,0:T(8,128)(2,1)}, bf16[2,256,512]{2,1,0:T(8,128)(2,1)}, u32[]{:S(2)}, u32[]{:S(2)}) %collective-permute-start.100) | collective-permute-done | bytes 524320 | tf_op jit(solution)/shard_map/cond/branch_1_fun/ppermute | solution.py:464
  888.0 10.1 collective-permute-done.106
  919.9 10.6 %collective-permute-done.95 = bf16[2,256,1024]{2,1,0:T(8,128)(2,1)} collective-permute-done((bf16[2,256,1024]{2,1,0:T(8,128)(2,1)}, bf16[2,256,1024]{2,1,0:T(8,128)(2,1)}, u32[]{:S(2)}, u32[]{:S(2)}) %collective-permute-start.95) | collective-permute-done | bytes 1048608 | tf_op jit(solution)/shard_map/cond/branch_1_fun/ppermute | solution.py:464
  967.7 12.6 %reduce-scatter.21.cloned.1.call-done = bf16[64,2048]{1,0:T(8,128)(2,1)} async-done(((bf16[256,2048]{1,0:T(8,128)(2,1)}), bf16[64,2048]{1,0:T(8,128)(2,1)}) %reduce-scatter.21.cloned.1.call-update) | async-done | bytes 262160 | tf_op jit(solution)/shard_map/cond/branch_1_fun/reduce_scatter | solution.py:519
  (609 shorter events, 465.2 us)
Async XLA Ops:
  125.4 282.1 %all-gather.11.cloned.1.call-start = ((), (), s32[]{:S(2)}) async-start(), calls=%async_computation.18 | async-start | bytes 6488064 | tf_op jit(solution)/shard_map/cond/branch_1_fun/all_gather | solution.py:643
  126.1 305.0 %all-gather.9.cloned.1.call-start = ((), (), s32[]{:S(2)}) async-start(), calls=%async_computation.17 | async-start | bytes 12976128 | tf_op jit(solution)/shard_map/cond/branch_1_fun/all_gather | solution.py:640
  129.4 50.9 %collective-permute-start.67 = (bf16[256,1024]{1,0:T(8,128)(2,1)}, bf16[256,1024]{1,0:T(8,128)(2,1)}, u32[]{:S(2)}, u32[]{:S(2)}) collective-permute-start(bf16[256,1024]{1,0:T(8,128)(2,1)} %get-tuple-element.669), channel_id=1, source_target_pairs={{0,16},{1,17},{2,18},{3,19},{4,20},{5,21},{6,22},{7,23},{8,24},{9,... | collective-permute-start | bytes 1572872 | tf_op jit(solution)/shard_map/cond/branch_1_fun/ppermute | solution.py:464
  130.1 824.2 %reduce-scatter.27.cloned.1.call-start = ((), (), s32[]{:S(2)}) async-start(), calls=%async_computation.22 | async-start | bytes 7208960 | tf_op jit(solution)/shard_map/cond/branch_1_fun/reduce_scatter | solution.py:707
  204.5 129.7 %collective-permute-start.82 = (bf16[384,2048]{1,0:T(8,128)(2,1)}, bf16[384,2048]{1,0:T(8,128)(2,1)}, u32[]{:S(2)}, u32[]{:S(2)}) collective-permute-start(bf16[384,2048]{1,0:T(8,128)(2,1)} %get-tuple-element.711), channel_id=1, source_target_pairs={{0,16},{1,17},{2,18},{3,19},{4,20},{5,21},{6,22},{7,23},{8,24},{9,... | collective-permute-start | bytes 4718600 | tf_op jit(solution)/shard_map/cond/branch_1_fun/ppermute | solution.py:464
  206.2 52.8 %collective-permute-start.70 = (bf16[256,1024]{1,0:T(8,128)(2,1)S(1)}, bf16[256,1024]{1,0:T(8,128)(2,1)S(1)}, u32[]{:S(2)}, u32[]{:S(2)}) collective-permute-start(bf16[256,1024]{1,0:T(8,128)(2,1)S(1)} %collective-permute-done.69), channel_id=1, source_target_pairs={{0,4},{1,5},{2,6},{3,7},{4,0},{5,1},{6,2},{7,3},{8,12},{9,13},{10,... | collective-permute-start | bytes 1572872 | tf_op jit(solution)/shard_map/cond/branch_1_fun/ppermute | solution.py:464
  209.0 127.9 %collective-permute-start.81 = (bf16[384,2048]{1,0:T(8,128)(2,1)}, bf16[384,2048]{1,0:T(8,128)(2,1)}, u32[]{:S(2)}, u32[]{:S(2)}) collective-permute-start(bf16[384,2048]{1,0:T(8,128)(2,1)} %get-tuple-element.711), channel_id=1, source_target_pairs={{0,8},{1,9},{2,10},{3,11},{4,12},{5,13},{6,14},{7,15},{8,0},{9,1},... | collective-permute-start | bytes 4718600 | tf_op jit(solution)/shard_map/cond/branch_1_fun/ppermute | solution.py:464
  210.4 50.3 %collective-permute-start.72 = (bf16[256,1024]{1,0:T(8,128)(2,1)S(1)}, bf16[256,1024]{1,0:T(8,128)(2,1)S(1)}, u32[]{:S(2)}, u32[]{:S(2)}) collective-permute-start(bf16[256,1024]{1,0:T(8,128)(2,1)S(1)} %collective-permute-done.71), channel_id=1, source_target_pairs={{0,4},{1,5},{2,6},{3,7},{4,0},{5,1},{6,2},{7,3},{8,12},{9,13},{10,... | collective-permute-start | bytes 1572872 | tf_op jit(solution)/shard_map/cond/branch_1_fun/ppermute | solution.py:464
  237.3 55.3 %collective-permute-start.58 = (bf16[384,1024]{1,0:T(8,128)(2,1)S(1)}, bf16[384,1024]{1,0:T(8,128)(2,1)S(1)}, u32[]{:S(2)}, u32[]{:S(2)}) collective-permute-start(bf16[384,1024]{1,0:T(8,128)(2,1)S(1)} %collective-permute-done.57), channel_id=1, source_target_pairs={{0,1},{1,2},{2,3},{4,5},{5,6},{6,7},{8,9},{9,10},{10,11},{12,13},{... | collective-permute-start | bytes 2359304 | tf_op jit(solution)/shard_map/cond/branch_1_fun/ppermute | solution.py:473
  332.8 58.7 %collective-permute-start.73 = (bf16[384,2048]{1,0:T(8,128)(2,1)}, bf16[384,2048]{1,0:T(8,128)(2,1)S(1)}, u32[]{:S(2)}, u32[]{:S(2)}) collective-permute-start(bf16[384,2048]{1,0:T(8,128)(2,1)} %get-tuple-element.375), channel_id=1, source_target_pairs={{0,8},{1,9},{2,10},{3,11},{4,12},{5,13},{6,14},{7,15},{8,0},{9,1},... | collective-permute-start | bytes 4718600 | tf_op jit(solution)/shard_map/cond/branch_1_fun/ppermute | solution.py:464
  336.4 50.9 %collective-permute-start.83 = (bf16[192,2048]{1,0:T(8,128)(2,1)}, bf16[192,2048]{1,0:T(8,128)(2,1)}, u32[]{:S(2)}, u32[]{:S(2)}) collective-permute-start(bf16[192,2048]{1,0:T(8,128)(2,1)} %slice.1393), channel_id=1, source_target_pairs={{0,8},{1,9},{2,10},{3,11},{4,12},{5,13},{6,14},{7,15},{8,0},{9,1},... | collective-permute-start | bytes 2359304 | tf_op jit(solution)/shard_map/cond/branch_1_fun/ppermute | solution.py:464
  339.0 50.4 %collective-permute-start.84 = (bf16[192,2048]{1,0:T(8,128)(2,1)}, bf16[192,2048]{1,0:T(8,128)(2,1)}, u32[]{:S(2)}, u32[]{:S(2)}) collective-permute-start(bf16[192,2048]{1,0:T(8,128)(2,1)} %slice.1394), channel_id=1, source_target_pairs={{0,16},{1,17},{2,18},{3,19},{4,20},{5,21},{6,22},{7,23},{8,24},{9,... | collective-permute-start | bytes 2359304 | tf_op jit(solution)/shard_map/cond/branch_1_fun/ppermute | solution.py:464
  520.6 56.7 %collective-permute-start.85 = (bf16[192,2048]{1,0:T(8,128)(2,1)}, bf16[192,2048]{1,0:T(8,128)(2,1)}, u32[]{:S(2)}, u32[]{:S(2)}) collective-permute-start(bf16[192,2048]{1,0:T(8,128)(2,1)} %get-tuple-element.653), channel_id=1, source_target_pairs={{0,16},{1,17},{2,18},{3,19},{4,20},{5,21},{6,22},{7,23},{8,24},{9,... | collective-permute-start | bytes 2359304 | tf_op jit(solution)/shard_map/cond/branch_1_fun/ppermute | solution.py:464
  522.1 52.1 %collective-permute-start.87 = (bf16[192,2048]{1,0:T(8,128)(2,1)}, bf16[192,2048]{1,0:T(8,128)(2,1)}, u32[]{:S(2)}, u32[]{:S(2)}) collective-permute-start(bf16[192,2048]{1,0:T(8,128)(2,1)} %get-tuple-element.654), channel_id=1, source_target_pairs={{0,8},{1,9},{2,10},{3,11},{4,12},{5,13},{6,14},{7,15},{8,0},{9,1},... | collective-permute-start | bytes 2359304 | tf_op jit(solution)/shard_map/cond/branch_1_fun/ppermute | solution.py:464
  529.1 60.0 %collective-permute-start.77 = (bf16[192,2048]{1,0:T(8,128)(2,1)S(1)}, bf16[192,2048]{1,0:T(8,128)(2,1)S(1)}, u32[]{:S(2)}, u32[]{:S(2)}) collective-permute-start(bf16[192,2048]{1,0:T(8,128)(2,1)S(1)} %get-tuple-element.655), channel_id=1, source_target_pairs={{0,16},{1,17},{2,18},{3,19},{4,20},{5,21},{6,22},{7,23},{8,24},{9,... | collective-permute-start | bytes 2359304 | tf_op jit(solution)/shard_map/cond/branch_1_fun/ppermute | solution.py:464
  530.6 167.9 %collective-permute-start.79 = (bf16[192,2048]{1,0:T(8,128)(2,1)}, bf16[192,2048]{1,0:T(8,128)(2,1)}, u32[]{:S(2)}, u32[]{:S(2)}) collective-permute-start(bf16[192,2048]{1,0:T(8,128)(2,1)} %get-tuple-element.656), channel_id=1, source_target_pairs={{0,8},{1,9},{2,10},{3,11},{4,12},{5,13},{6,14},{7,15},{8,0},{9,1},... | collective-permute-start | bytes 2359304 | tf_op jit(solution)/shard_map/cond/branch_1_fun/ppermute | solution.py:464
  565.9 398.4 %reduce-scatter.29.cloned.1.call-start = ((), (), s32[]{:S(2)}) async-start(), calls=%async_computation.23 | async-start | bytes 3604480 | tf_op jit(solution)/shard_map/cond/branch_1_fun/reduce_scatter | solution.py:706
  591.7 258.5 %collective-permute-start.78 = (bf16[384,2048]{1,0:T(8,128)(2,1)}, bf16[384,2048]{1,0:T(8,128)(2,1)}, u32[]{:S(2)}, u32[]{:S(2)}) collective-permute-start(bf16[384,2048]{1,0:T(8,128)(2,1)} %pad_maximum_fusion.13), channel_id=1, source_target_pairs={{0,8},{1,9},{2,10},{3,11},{4,12},{5,13},{6,14},{7,15},{8,0},{9,1},... | collective-permute-start | bytes 4718600 | tf_op jit(solution)/shard_map/cond/branch_1_fun/ppermute | solution.py:464
  738.4 112.3 %collective-permute-start.80 = (bf16[384,2048]{1,0:T(8,128)(2,1)}, bf16[384,2048]{1,0:T(8,128)(2,1)}, u32[]{:S(2)}, u32[]{:S(2)}) collective-permute-start(bf16[384,2048]{1,0:T(8,128)(2,1)} %pad_maximum_fusion.14), channel_id=1, source_target_pairs={{0,16},{1,17},{2,18},{3,19},{4,20},{5,21},{6,22},{7,23},{8,24},{9,... | collective-permute-start | bytes 4718600 | tf_op jit(solution)/shard_map/cond/branch_1_fun/ppermute | solution.py:464
  739.4 226.3 %reduce-scatter.25.cloned.1.call-start = ((), (), s32[]{:S(2)}) async-start(), calls=%async_computation.21 | async-start | bytes 1310720 | tf_op jit(solution)/shard_map/cond/branch_1_fun/reduce_scatter | solution.py:519
  771.8 65.6 %collective-permute-start.104 = (bf16[4,256,2048]{2,1,0:T(8,128)(2,1)}, bf16[4,256,2048]{2,1,0:T(8,128)(2,1)S(1)}, u32[]{:S(2)}, u32[]{:S(2)}) collective-permute-start(bf16[4,256,2048]{2,1,0:T(8,128)(2,1)} %dynamic-slice_bitcast_fusion.18), channel_id=1, source_target_pairs={{0,4},{1,5},{2,6},{3,7},{4,0},{5,1},{6,2},{7,3},{8,12},{9,13},{10,... | collective-permute-start | bytes 12582920 | tf_op jit(solution)/shard_map/cond/branch_1_fun/ppermute | solution.py:464
  836.9 64.4 %collective-permute-start.94 = (bf16[4,256,2048]{2,1,0:T(8,128)(2,1)}, bf16[4,256,2048]{2,1,0:T(8,128)(2,1)}, u32[]{:S(2)}, u32[]{:S(2)}) collective-permute-start(bf16[4,256,2048]{2,1,0:T(8,128)(2,1)} %dynamic-slice_bitcast_fusion.19), channel_id=1, source_target_pairs={{0,4},{1,5},{2,6},{3,7},{4,0},{5,1},{6,2},{7,3},{8,12},{9,13},{10,... | collective-permute-start | bytes 12582920 | tf_op jit(solution)/shard_map/cond/branch_1_fun/ppermute | solution.py:464
  901.2 66.5 %reduce-scatter.23.cloned.1.call-start = ((), (), s32[]{:S(2)}) async-start(), calls=%async_computation.20 | async-start | bytes 655360 | tf_op jit(solution)/shard_map/cond/branch_1_fun/reduce_scatter | solution.py:519
  919.7 60.6 %reduce-scatter.21.cloned.1.call-start = ((), (), s32[]{:S(2)}) async-start(), calls=%async_computation.19 | async-start | bytes 1310720 | tf_op jit(solution)/shard_map/cond/branch_1_fun/reduce_scatter | solution.py:519
  (157 other events, 2954.6 us)
Sparse Core Ops, SparseCore 0:
  127.8 59.0 all-gather.10
  188.6 139.9 all-gather.8
  566.0 122.8 reduce-scatter.26
  739.5 79.3 reduce-scatter.28
  901.3 27.5 reduce-scatter.24
  931.6 20.2 reduce-scatter.22
  954.8 25.3 reduce-scatter.20

commit v2 on v1

v2 whole, which is shorter than its diff:
```python
import functools

import jax
import jax.numpy as jnp
from jax import lax
from jax.experimental import pallas as pl
from jax.experimental.pallas import tpu as pltpu
from jax.sharding import PartitionSpec as P

HEADS = 16
KV_HEADS = 4
HEAD_DIM = 128
GROUP = HEADS // KV_HEADS
FF = 5632


EPSILON = 1e-05
MOMENTUM = 0.5
AVERAGING = 0.5
STEP_RATE = 0.0003

MESH = pl.DeviceIdType.MESH
MESH_AXES = ("wide", "narrow")
SCORE_SCALE = HEAD_DIM ** (-0.5)
LOG2_E = 1.4426950408889634
MASKED = -1e30


def dot_nt(a, b):
    return lax.dot_general(a, b, (((1,), (1,)), ((), ())), preferred_element_type=jnp.float32)


def dot_tn(a, b):
    return lax.dot_general(a, b, (((0,), (0,)), ((), ())), preferred_element_type=jnp.float32)


UNIT_GROUP = 256
WIDTH_GROUP = 256


def unit_groups(units):
    return [(low, min(low + UNIT_GROUP, units)) for low in range(0, units, UNIT_GROUP)]


def mlp_kernel(
    cap, counts, live_ref, rows_ref, grad_ref, gateup_hbm, down_hbm,
    hidden_ref, gateup_grad_ref, back_ref, gateup_ref, down_ref, gateup_sems, down_sems,
):
    step = pl.program_id(0)
    width = rows_ref.shape[1]
    units = down_ref.shape[0]
    full, rest = units // UNIT_GROUP, units % UNIT_GROUP
    live = live_ref[step]

    def span(low, size):
        return pl.ds(low if isinstance(low, int) else pl.multiple_of(low, size), size)

    def gateup_part(k, low, size):
        both = span(2 * low, 2 * size)
        return pltpu.make_async_copy(gateup_hbm.at[:, both], gateup_ref.at[:, both], gateup_sems.at[k])

    def down_part(k, low, size):
        one = span(low, size)
        return pltpu.make_async_copy(down_hbm.at[one, :], down_ref.at[one, :], down_sems.at[k])

    @pl.when(step == 0)
    def _():
        for k, (low, high) in enumerate(unit_groups(units)):
            gateup_part(k, low, high - low).start()
            down_part(k, low, high - low).start()

    def run(count):
        def units_step(k, low, size):
            @pl.when(step == 0)
            def _():
                gateup_part(k, low, size).wait()
                down_part(k, low, size).wait()

            both, one = span(2 * low, 2 * size), span(low, size)
            gate_up = jnp.dot(rows_ref[:count, :], gateup_ref[:, both], preferred_element_type=jnp.float32)
            gate, upper = gate_up[:, :size], gate_up[:, size:]
            grad_hidden = dot_nt(grad_ref[:count, :], down_ref[one, :])
            sigmoid = 1.0 / (1.0 + jnp.exp(-gate))
            silu = gate * sigmoid
            hidden_ref[:count, one] = (silu * upper).astype(jnp.bfloat16)
            grad_gate = grad_hidden * upper * (sigmoid + silu * (1.0 - sigmoid))
            grad_upper = grad_hidden * silu
            gateup_grad_ref[:count, both] = jnp.concatenate([grad_gate, grad_upper], axis=1).astype(jnp.bfloat16)

        lax.fori_loop(0, full, lambda k, c: (units_step(k, k * UNIT_GROUP, UNIT_GROUP), c)[1], 0)
        if rest:
            units_step(full, full * UNIT_GROUP, rest)

        def back_step(k, carry):
            at = span(k * WIDTH_GROUP, WIDTH_GROUP)
            back_ref[:count, at] = dot_nt(gateup_grad_ref[:count, :], gateup_ref[at, :]).astype(jnp.bfloat16)
            return carry

        lax.fori_loop(0, width // WIDTH_GROUP, back_step, 0)
        if count < cap:
            for ref in (hidden_ref, gateup_grad_ref, back_ref):
                ref[count:, :] = jnp.zeros((cap - count, ref.shape[1]), ref.dtype)

    for low, count in zip((None,) + counts[:-1], counts):
        chosen = live > (-1 if low is None else low)
        if count < cap:
            chosen &= live <= count

        @pl.when(chosen)
        def _(count=count):
            run(count)


def mlp_block(rows, grad, live, gateup, down, cap):
    blocks = rows.shape[0] // cap
    width = rows.shape[1]
    units = down.shape[0]
    if units % 128 or cap % 128:
        return mlp_plain(rows, grad, gateup, down)
    counts = (192, 256, 320, 384) if cap == 384 else tuple(range(256, cap, 256)) + (cap,)
    groups = len(unit_groups(units))
    low = jnp.bfloat16
    by_block = lambda cols: pl.BlockSpec((cap, cols), lambda b, live: (b, 0))
    return pl.pallas_call(
        functools.partial(mlp_kernel, cap, counts),
        grid_spec=pltpu.PrefetchScalarGridSpec(
            num_scalar_prefetch=1,
            grid=(blocks,),
            in_specs=[by_block(width), by_block(width)] + [pl.BlockSpec(memory_space=pl.ANY)] * 2,
            out_specs=(by_block(units), by_block(2 * units), by_block(width)),
            scratch_shapes=[
                pltpu.VMEM(gateup.shape, low),
                pltpu.VMEM(down.shape, low),
                pltpu.SemaphoreType.DMA((groups,)),
                pltpu.SemaphoreType.DMA((groups,)),
            ],
        ),
        out_shape=(
            jax.ShapeDtypeStruct((blocks * cap, units), low),
            jax.ShapeDtypeStruct((blocks * cap, 2 * units), low),
            jax.ShapeDtypeStruct((blocks * cap, width), low),
        ),
        compiler_params=pltpu.CompilerParams(vmem_limit_bytes=56 * 1024 * 1024),
        cost_estimate=pl.CostEstimate(
            flops=10 * blocks * cap * width * units,
            bytes_accessed=2 * (gateup.size + down.size) + 12 * blocks * cap * width,
            transcendentals=blocks * cap * units,
        ),
        name="mlp_block",
    )(live, rows, grad, gateup, down)


def mlp_plain(rows, grad, gateup, down):
    groups = unit_groups(down.shape[0])
    gate_up = jnp.dot(rows, gateup, preferred_element_type=jnp.float32)
    gate = jnp.concatenate([gate_up[:, 2 * low : low + high] for low, high in groups], axis=1)
    upper = jnp.concatenate([gate_up[:, low + high : 2 * high] for low, high in groups], axis=1)
    grad_hidden = jnp.dot(grad, down.T, preferred_element_type=jnp.float32)
    sigmoid = jax.nn.sigmoid(gate)
    silu = gate * sigmoid
    hidden = (silu * upper).astype(jnp.bfloat16)
    grad_gate = grad_hidden * upper * (sigmoid + silu * (1.0 - sigmoid))
    grad_upper = grad_hidden * silu
    gateup_grad = jnp.concatenate(
        [part[:, low:high] for low, high in groups for part in (grad_gate, grad_upper)], axis=1
    ).astype(jnp.bfloat16)
    back = jnp.dot(gateup_grad, gateup.T, preferred_element_type=jnp.float32).astype(jnp.bfloat16)
    return hidden, gateup_grad, back


class Place:
    def __init__(self, n):
        self.n = n
        self.wide = lax.axis_index("wide")
        self.z = lax.axis_index("narrow")
        self.t, self.core = self.wide // 2, self.wide % 2
        self.t_x, self.t_y, self.t_d = self.t ^ 1, self.t ^ 2, self.t ^ 3
        self.by_x = self.device(self.t_x)
        self.by_y = self.device(self.t_y)
        self.by_d = self.device(self.t_d)
        self.sibling = self.device(self.t, core=1 - self.core)
        self.above = self.device(self.t, z=jnp.minimum(self.z + 1, n - 1))
        self.below = self.device(self.t, z=jnp.maximum(self.z - 1, 0))

    def device(self, t, core=None, z=None):
        return (t * 2 + (self.core if core is None else core), self.z if z is None else z)

    def greet(self, others):
        barrier = pltpu.get_barrier_semaphore()
        for other in others:
            pl.semaphore_signal(barrier, inc=1, device_id=other, device_id_type=MESH)

        @pl.when(self.z > 0)
        def _():
            pl.semaphore_signal(barrier, inc=1, device_id=self.below, device_id_type=MESH)

        @pl.when(self.z < self.n - 1)
        def _():
            pl.semaphore_signal(barrier, inc=1, device_id=self.above, device_id_type=MESH)

        inner = (self.z > 0).astype(jnp.int32) + (self.z < self.n - 1).astype(jnp.int32)
        pl.semaphore_wait(barrier, len(others) + inner)


class Copies:
    def __init__(self, send_sems, recv_sems):
        self.send_sems, self.recv_sems = send_sems, recv_sems
        self.count = 0
        self.started = []

    def make(self, src, dst, to):
        k = self.count
        self.count += 1
        return pltpu.make_async_remote_copy(
            src_ref=src, dst_ref=dst, send_sem=self.send_sems.at[k], recv_sem=self.recv_sems.at[k],
            device_id=to, device_id_type=MESH,
        )

    def same(self, ref, to):
        return self.make(ref, ref, to)

    def each(self, moves, when, act):
        def run():
            for m in moves:
                act(m)

        if when is None:
            run()
        else:
            pl.when(when)(run)

    def go(self, moves, when=None):
        self.each(moves, when, lambda m: m.start())
        self.started.append((moves, when))

    def arrive(self, moves, when=None):
        self.each(moves, when, lambda m: m.wait_recv())

    def end(self):
        for moves, when in self.started:
            self.each(moves, when, lambda m: m.wait_send())


class LineGather:
    def __init__(self, place, copies, view, own):
        self.place, self.copies, self.view, self.own = place, copies, view, own
        self.up, self.down = {}, {}

    def send(self, step):
        p, last = self.place, self.place.n - 1
        block = self.view(jnp.maximum(p.z - (step - 1), 0))
        self.up[step] = self.copies.make(self.own if step == 1 else block, block, p.above)
        self.copies.go([self.up[step]], (p.z - (step - 1) >= 0) & (p.z < last))
        block = self.view(jnp.minimum(p.z + (step - 1), last))
        self.down[step] = self.copies.make(self.own if step == 1 else block, block, p.below)
        self.copies.go([self.down[step]], (p.z + (step - 1) <= last) & (p.z > 0))

    def take(self, step):
        p = self.place
        self.copies.arrive([self.up[step]], p.z - step >= 0)
        self.copies.arrive([self.down[step]], p.z + step <= p.n - 1)

    def hand_over(self, step):
        p, last = self.place, self.place.n - 1
        moves = []
        for at, there in ((p.z - step, p.z - step >= 0), (p.z + step, p.z + step <= last)):
            block = self.view(jnp.clip(at, 0, last))
            move = self.copies.same(block, p.sibling)
            self.copies.go([move], there)
            moves.append(([move], there))
        return moves


def gather_kernel(
    n, qkv_ref, out_ref, gateup_ref, down_ref, ext_ref, qkv_all, out_all, ext_all, came, down_all,
    qkv_low, out_low, trade_low, down_low, send_sems, recv_sems, local_sems,
):
    p = Place(n)
    c = Copies(send_sems, recv_sems)
    t, core, z = p.t, p.core, p.z
    low = jnp.bfloat16
    qkv_low[...] = qkv_ref[...].astype(low)
    p.greet([p.by_x, p.by_y, p.by_d, p.sibling])

    half = qkv_ref.shape[1] // 256 * 128
    qa, qb = slice(0, half), slice(half, qkv_ref.shape[1])
    lines = [
        LineGather(p, c, lambda zz, cols=cols: qkv_all.at[t, core, zz, :, cols], qkv_low.at[:, cols])
        for cols in (qa, qb)
    ]
    lines.append(LineGather(p, c, lambda zz: ext_all.at[t, core, zz], ext_ref))
    for line in lines:
        line.send(1)
    local = []

    def place(src, dst):
        move = pltpu.make_async_copy(src, dst, local_sems.at[len(local)])
        move.start()
        local.append(move)

    place(qkv_low, qkv_all.at[t, core, z])
    place(ext_ref, ext_all.at[t, core, z])
    units = trade_low.shape[2] // 2
    for k in range(trade_low.shape[0]):
        for first, last in unit_groups(units):
            for to, start in ((2 * first, k * units), (first + last, gateup_ref.shape[1] // 2 + k * units)):
                trade_low[k, :, to : to + last - first] = gateup_ref[:, start + first : start + last].astype(low)
    place(trade_low.at[t], came.at[t])
    trade = [
        c.make(trade_low.at[k], came.at[t], to) for k, to in ((p.t_x, p.by_x), (p.t_y, p.by_y), (p.t_d, p.by_d))
    ]
    c.go(trade)
    out_low[...] = out_ref[...].astype(low)
    down_low[...] = down_ref[...].astype(low)
    place(out_low, out_all.at[t, core, z])
    place(down_low, down_all.at[core, z])
    line_out = LineGather(p, c, lambda zz: out_all.at[t, core, zz], out_low)
    line_down = LineGather(p, c, lambda zz: down_all.at[core, zz], down_low)
    down_own = c.make(down_low, down_all.at[core, z], p.sibling)
    c.go([down_own])
    handed = [([down_own], None)]
    for step in range(1, n):
        for line in lines:
            line.take(step)
            if step < n - 1:
                line.send(step + 1)
    for move in local:
        move.wait()
    a_y = c.same(qkv_all.at[t, core, :, :, qa], p.by_y)
    b_x = c.same(qkv_all.at[t, core, :, :, qb], p.by_x)
    e_x = c.same(ext_all.at[t, core], p.by_x)
    c.go([a_y, b_x, e_x])
    line_down.send(1)
    line_out.send(1)
    own = [c.same(qkv_all.at[t, core], p.sibling), c.same(ext_all.at[t, core], p.sibling)]
    c.go(own)
    c.arrive([e_x])
    e_y = [c.same(ext_all.at[k, core], p.by_y) for k in (t, p.t_x)]
    c.go(e_y)
    c.arrive([a_y])
    a_x = [c.same(qkv_all.at[k, core, :, :, qa], p.by_x) for k in (t, p.t_y)]
    c.go(a_x)
    c.arrive([b_x])
    b_y = [c.same(qkv_all.at[k, core, :, :, qb], p.by_y) for k in (t, p.t_x)]
    c.go(b_y)
    near = [
        c.same(qkv_all.at[p.t_y, core, :, :, qa], p.sibling),
        c.same(qkv_all.at[p.t_x, core, :, :, qb], p.sibling),
        c.same(ext_all.at[p.t_x, core], p.sibling),
    ]
    c.go(near)
    c.arrive(e_y)
    far = [c.same(ext_all.at[k, core], p.sibling) for k in (p.t_y, p.t_d)]
    c.go(far)
    for step in range(1, n):
        for line in (line_down, line_out):
            line.take(step)
            if step < n - 1:
                line.send(step + 1)
        handed += line_down.hand_over(step)
        if step == max(n - 2, 1):
            c.arrive(a_x)
            c.arrive(b_y)
            last = [c.same(qkv_all.at[k, core, :, :, qa], p.sibling) for k in (p.t_x, p.t_d)]
            last += [c.same(qkv_all.at[k, core, :, :, qb], p.sibling) for k in (p.t_y, p.t_d)]
            c.go(last)
    c.arrive(trade + own + near + far + last)
    for moves, when in handed:
        c.arrive(moves, when)
    c.end()


def gather_first(qkv, out, gateup, down, ext, planes, n):
    any_spec = pl.BlockSpec(memory_space=pl.ANY)
    rows = qkv.shape[0]
    part = gateup.shape[1] // planes
    low = jnp.bfloat16
    copies = 64
    return pl.pallas_call(
        functools.partial(gather_kernel, n),
        out_shape=(
            jax.ShapeDtypeStruct((planes, 2, n, rows, qkv.shape[1]), low),
            jax.ShapeDtypeStruct((planes, 2, n, rows, out.shape[1]), low),
            jax.ShapeDtypeStruct((planes, 2, n) + ext.shape, low),
            jax.ShapeDtypeStruct((planes, rows, part), low),
            jax.ShapeDtypeStruct((2, n) + down.shape, low),
        ),
        in_specs=[pl.BlockSpec(memory_space=pltpu.VMEM)] * 5,
        out_specs=(any_spec,) * 5,
        scratch_shapes=[
            pltpu.VMEM(qkv.shape, low),
            pltpu.VMEM(out.shape, low),
            pltpu.VMEM((planes, rows, part), low),
            pltpu.VMEM(down.shape, low),
            pltpu.SemaphoreType.DMA((copies,)),
            pltpu.SemaphoreType.DMA((copies,)),
            pltpu.SemaphoreType.DMA((8,)),
        ],
        compiler_params=pltpu.CompilerParams(
            collective_id=0, has_side_effects=True, vmem_limit_bytes=32 * 1024 * 1024
        ),
        name="gather_first",
    )(qkv, out, gateup, down, ext)


def fill_bias(r, key_code, query_code, query_base, bias):
    rows = bias.shape[0]
    code = key_code[r * rows : (r + 1) * rows, :]
    seen = (code <= query_code[...]) & (code >= query_base[...])
    bias[...] = jnp.where(seen, 0.0, MASKED)


class PlaneGather:
    def __init__(self, place, copies, whole):
        self.p, self.c, self.whole = place, copies, whole
        cols = whole.shape[-1]
        self.a, self.b = slice(0, cols // 2), slice(cols // 2, cols)

    def block(self, t, cols=slice(None)):
        return self.whole.at[t, self.p.core, :, :, cols]

    def begin(self):
        p, c = self.p, self.c
        self.a_y, self.b_x = c.same(self.block(p.t, self.a), p.by_y), c.same(self.block(p.t, self.b), p.by_x)
        self.over = [c.same(self.block(p.t), p.sibling)]
        c.go([self.a_y, self.b_x] + self.over)

    def middle(self):
        p, c = self.p, self.c
        c.arrive([self.a_y, self.b_x])
        self.a_x = [c.same(self.block(k, self.a), p.by_x) for k in (p.t, p.t_y)]
        self.b_y = [c.same(self.block(k, self.b), p.by_y) for k in (p.t, p.t_x)]
        near = [c.same(self.block(p.t_y, self.a), p.sibling), c.same(self.block(p.t_x, self.b), p.sibling)]
        c.go(self.a_x + self.b_y + near)
        self.over += near

    def end(self):
        p, c = self.p, self.c
        c.arrive(self.a_x + self.b_y)
        far = [c.same(self.block(k, self.a), p.sibling) for k in (p.t_x, p.t_d)]
        far += [c.same(self.block(k, self.b), p.sibling) for k in (p.t_y, p.t_d)]
        c.go(far)
        c.arrive(self.over + far)


def attend_kernel(n, with_out, *refs):
    q_ref, kv_ref, key_code, query_code, query_base = refs[:5]
    o_ref, total_ref, kv_all = refs[5 + with_out : 8 + with_out]
    out_all = refs[8 + with_out] if with_out else None
    peak_now, total_now, mixed_now, bias, send_sems, recv_sems = refs[-6:]
    p = Place(n)
    c = Copies(send_sems, recv_sems)
    z = p.z
    rows = q_ref.shape[0]
    values_at = KV_HEADS * HEAD_DIM
    slot = lambda r: kv_all.at[r * rows : (r + 1) * rows, :]
    p.greet([p.by_x, p.by_y, p.sibling] if with_out else [])
    copies = [c.make(kv_ref if r == 0 else slot(r), slot(r + 1), p.above) for r in range(n - 1)]
    if copies:
        c.go([copies[0]], z < n - 1)
    if with_out:
        out_plane = PlaneGather(p, c, out_all)
        out_plane.begin()

    kv_all[:rows, :] = kv_ref[...]
    for r in range(1, n):
        @pl.when(z < r)
        def _(r=r):
            kv_all[r * rows : (r + 1) * rows, :] = jnp.zeros((rows, kv_all.shape[1]), kv_all.dtype)

    def block(r):
        fill_bias(r, key_code, query_code, query_base, bias)
        at = slice(r * rows, (r + 1) * rows)

        def group(g, carry):
            keys = kv_all[at, pl.ds(pl.multiple_of(g * HEAD_DIM, HEAD_DIM), HEAD_DIM)]
            values = kv_all[at, pl.ds(pl.multiple_of(values_at + g * HEAD_DIM, HEAD_DIM), HEAD_DIM)]
            hidden = bias[...]
            for h in range(GROUP):
                lanes = pl.ds(pl.multiple_of((g * GROUP + h) * HEAD_DIM, HEAD_DIM), HEAD_DIM)
                scores = dot_nt(keys, q_ref[:, lanes]) * (SCORE_SCALE * LOG2_E) + hidden
                peak = jnp.max(scores, axis=0, keepdims=True)
                if r:
                    before = peak_now[g, h : h + 1, :]
                    peak = jnp.maximum(peak, before)
                weights = jnp.exp2(scores - peak)
                total = jnp.sum(weights, axis=0, keepdims=True)
                mixed = dot_tn(values, weights.astype(jnp.bfloat16))
                if r:
                    shrink = jnp.exp2(before - peak)
                    total = total + total_now[g, h : h + 1, :] * shrink
                    mixed = mixed + mixed_now[g, h] * shrink
                peak_now[g, h : h + 1, :] = peak
                total_now[g, h : h + 1, :] = total
                mixed_now[g, h] = mixed
            return carry

        lax.fori_loop(0, KV_HEADS, group, 0)

    block(0)
    for r in range(1, n):
        c.arrive([copies[r - 1]], z >= r)
        if r < n - 1:
            c.go([copies[r]], (z >= r) & (z < n - 1))
        if with_out and r == 1:
            out_plane.middle()
        if with_out and r == n - 1:
            out_plane.end()

        @pl.when(z >= r)
        def _(r=r):
            block(r)

    def finish(g, carry):
        for h in range(GROUP):
            lanes = pl.ds(pl.multiple_of((g * GROUP + h) * HEAD_DIM, HEAD_DIM), HEAD_DIM)
            total = total_now[g, h : h + 1, :]
            o_ref[:, lanes] = (mixed_now[g, h] / total).T.astype(jnp.bfloat16)
            total_ref[g, h : h + 1, :] = peak_now[g, h : h + 1, :] + jnp.log2(total)
        return carry

    lax.fori_loop(0, KV_HEADS, finish, 0)
    c.end()


def attend(query, kv, key_code, query_code, query_base, n, collective_id, out_all=None):
    rows, width = query.shape
    in_vmem = pl.BlockSpec(memory_space=pltpu.VMEM)
    any_spec = pl.BlockSpec(memory_space=pl.ANY)
    outs = [] if out_all is None else [out_all]
    copies = n + 16
    return pl.pallas_call(
        functools.partial(attend_kernel, n, len(outs)),
        in_specs=[in_vmem] * 5 + [any_spec] * len(outs),
        out_specs=(in_vmem,) * 3 + (any_spec,) * len(outs),
        input_output_aliases={5: 3} if outs else {},
        out_shape=(
            jax.ShapeDtypeStruct((rows, width), jnp.bfloat16),
            jax.ShapeDtypeStruct((KV_HEADS, GROUP, rows), jnp.float32),
            jax.ShapeDtypeStruct((n * rows, kv.shape[1]), jnp.bfloat16),
        )
        + tuple(jax.ShapeDtypeStruct(o.shape, o.dtype) for o in outs),
        scratch_shapes=[
            pltpu.VMEM((KV_HEADS, GROUP, rows), jnp.float32),
            pltpu.VMEM((KV_HEADS, GROUP, rows), jnp.float32),
            pltpu.VMEM((KV_HEADS, GROUP, HEAD_DIM, rows), jnp.float32),
            pltpu.VMEM((rows, rows), jnp.float32),
            pltpu.SemaphoreType.DMA((copies,)),
            pltpu.SemaphoreType.DMA((copies,)),
        ],
        compiler_params=pltpu.CompilerParams(
            vmem_limit_bytes=48 * 1024 * 1024, collective_id=collective_id, has_side_effects=True
        ),
        cost_estimate=pl.CostEstimate(
            flops=4 * rows * n * rows * width, bytes_accessed=8 * rows * width, transcendentals=HEADS * rows * n * rows
        ),
        name="attend",
    )(query, kv, key_code, query_code, query_base, *outs)


def attend_back_kernel(
    n, q_ref, kv_all, do_ref, total_ref, inner_ref, key_code, query_code, query_base, dq_ref, dkv_ref,
    dq_now, dkv_now, bias, leaving, came, send_sems, recv_sems,
):
    p = Place(n)
    c = Copies(send_sems, recv_sems)
    z = p.z
    rows = q_ref.shape[0]
    values_at = KV_HEADS * HEAD_DIM
    p.greet([])
    copies = {r: c.make(leaving.at[r - 1], came.at[r - 1], p.below) for r in range(1, n)}
    dq_now[...] = jnp.zeros_like(dq_now)

    def block(r):
        fill_bias(r, key_code, query_code, query_base, bias)
        at = slice(r * rows, (r + 1) * rows)

        def group(g, carry):
            key_lanes = pl.ds(pl.multiple_of(g * HEAD_DIM, HEAD_DIM), HEAD_DIM)
            value_lanes = pl.ds(pl.multiple_of(values_at + g * HEAD_DIM, HEAD_DIM), HEAD_DIM)
            keys, values, hidden = kv_all[at, key_lanes], kv_all[at, value_lanes], bias[...]
            dk = dv = None
            for h in range(GROUP):
                lanes = pl.ds(pl.multiple_of((g * GROUP + h) * HEAD_DIM, HEAD_DIM), HEAD_DIM)
                query, grad = q_ref[:, lanes], do_ref[:, lanes]
                scores = dot_nt(keys, query) * (SCORE_SCALE * LOG2_E) + hidden
                weights = jnp.exp2(scores - total_ref[g, h : h + 1, :])
                grad_weights = dot_nt(values, grad)
                grad_scores = (weights * (grad_weights - inner_ref[g, h : h + 1, :])).astype(jnp.bfloat16)
                dv_term = jnp.dot(weights.astype(jnp.bfloat16), grad, preferred_element_type=jnp.float32)
                dk_term = jnp.dot(grad_scores, query, preferred_element_type=jnp.float32)
                dv = dv_term if dv is None else dv + dv_term
                dk = dk_term if dk is None else dk + dk_term
                dq_now[g, h] += dot_tn(keys, grad_scores)
            dkv_now[:, key_lanes] = dk * SCORE_SCALE
            dkv_now[:, value_lanes] = dv
            return carry

        lax.fori_loop(0, KV_HEADS, group, 0)

    for r in range(n - 1, -1, -1):
        @pl.when(z >= r)
        def _(r=r):
            block(r)
            if r < n - 1:
                @pl.when(z < n - 1)
                def _():
                    copies[r + 1].wait_recv()
                    dkv_now[...] += came[r].astype(jnp.float32)
            if r:
                leaving[r - 1] = dkv_now[...].astype(jnp.bfloat16)
                copies[r].start()
            else:
                dkv_ref[...] = dkv_now[...]

    def finish(g, carry):
        for h in range(GROUP):
            lanes = pl.ds(pl.multiple_of((g * GROUP + h) * HEAD_DIM, HEAD_DIM), HEAD_DIM)
            dq_ref[:, lanes] = dq_now[g, h].T * SCORE_SCALE
        return carry

    lax.fori_loop(0, KV_HEADS, finish, 0)
    for r in range(1, n):
        @pl.when(z >= r)
        def _(r=r):
            copies[r].wait_send()


def attend_back(query, kv_all, grad, total, inner, key_code, query_code, query_base, n, collective_id):
    rows, width = query.shape
    kv_cols = kv_all.shape[1]
    in_vmem = pl.BlockSpec(memory_space=pltpu.VMEM)
    slots = max(n - 1, 1)
    return pl.pallas_call(
        functools.partial(attend_back_kernel, n),
        in_specs=[in_vmem] * 8,
        out_specs=(in_vmem,) * 2,
        out_shape=(
            jax.ShapeDtypeStruct((rows, width), jnp.float32),
            jax.ShapeDtypeStruct((rows, kv_cols), jnp.float32),
        ),
        scratch_shapes=[
            pltpu.VMEM((KV_HEADS, GROUP, HEAD_DIM, rows), jnp.float32),
            pltpu.VMEM((rows, kv_cols), jnp.float32),
            pltpu.VMEM((rows, rows), jnp.float32),
            pltpu.VMEM((slots, rows, kv_cols), jnp.bfloat16),
            pltpu.VMEM((slots, rows, kv_cols), jnp.bfloat16),
            pltpu.SemaphoreType.DMA((n,)),
            pltpu.SemaphoreType.DMA((n,)),
        ],
        compiler_params=pltpu.CompilerParams(
            vmem_limit_bytes=56 * 1024 * 1024, collective_id=collective_id, has_side_effects=True
        ),
        cost_estimate=pl.CostEstimate(
            flops=10 * rows * n * rows * width, bytes_accessed=16 * rows * width, transcendentals=HEADS * rows * n * rows
        ),
        name="attend_back",
    )(query, kv_all, grad, total, inner, key_code, query_code, query_base)


def rotary_tables(positions):
    half_dim = HEAD_DIM // 2
    frequency = jnp.power(10000.0, -2.0 * jnp.arange(half_dim, dtype=jnp.float32) / HEAD_DIM)
    angles = positions[:, None] * frequency[None, :]
    return (jnp.cos(angles)[:, None, :], jnp.sin(angles)[:, None, :])


def rotate_heads(values, cosine_table, sine_table):
    half_dim = HEAD_DIM // 2
    cosine, sine = cosine_table[:, 0], sine_table[:, 0]
    cosine = jnp.concatenate([cosine, cosine], axis=1)
    sine = jnp.concatenate([-sine, sine], axis=1)
    done = []
    for start in range(0, values.shape[1], HEAD_DIM):
        head = values[:, start : start + HEAD_DIM]
        done.append(head * cosine + jnp.roll(head, half_dim, axis=1) * sine)
    return jnp.concatenate(done, axis=1)


def norm_forward(values_in, gain_row):
    inverse = lax.rsqrt(jnp.mean(values_in * values_in, axis=-1, keepdims=True) + EPSILON)
    return (values_in * inverse * gain_row, inverse)


def norm_backward(values_in, inverse, gain_row, incoming):
    scaled_grad = incoming * gain_row
    return inverse * scaled_grad - values_in * inverse * inverse * inverse * jnp.mean(
        scaled_grad * values_in, axis=-1, keepdims=True
    )


def advance_state(weight, moment, average, gradient):
    moment_next = MOMENTUM * moment + gradient
    weight_next = weight - STEP_RATE * (gradient + MOMENTUM * moment_next)
    average_next = AVERAGING * average + (1.0 - AVERAGING) * weight_next
    return (weight_next, moment_next, average_next)


class Links:
    def __init__(self):
        self.wide = lax.axis_size("wide")
        self.n = lax.axis_size("narrow")
        self.planes = self.wide // 2
        self.wide_at = lax.axis_index("wide")
        self.z_at = lax.axis_index("narrow")
        self.t_at = self.wide_at // 2
        self.core_at = self.wide_at % 2
        self.bits = [1 << k for k in range(self.planes.bit_length() - 1)]
        per_chip = 2 * self.n
        self.same_chip = [[t * per_chip + j for j in range(per_chip)] for t in range(self.planes)]
        self.same_plane = [
            [t * per_chip + j for t in range(self.planes)] for j in range(per_chip)
        ]

    def swap(self, values, flip):
        pairs = [(i, i ^ (flip * self.n)) for i in range(self.wide * self.n)]
        return lax.ppermute(values, MESH_AXES, pairs)

    def column_cuts(self, cols):
        lanes = cols // 128
        count = len(self.bits)
        edges = [128 * (lanes * k // count) for k in range(count + 1)]
        orders = [self.bits[k:] + self.bits[:k] for k in range(count)]
        return list(zip(edges[:-1], edges[1:], orders))

    def scatter_core(self, term):
        mine = lax.dynamic_index_in_dim(term, self.core_at, 1, keepdims=False)
        other = lax.dynamic_index_in_dim(term, 1 - self.core_at, 1, keepdims=False)
        got = self.swap(other, 1)
        return (mine.astype(jnp.float32) + got.astype(jnp.float32)).astype(jnp.bfloat16)

    def scatter_rows(self, term):
        rows, cols = term.shape
        term = term.reshape(self.planes, 2, rows // self.wide, cols)
        term = self.scatter_core(term)
        parts = []
        for low, high, order in self.column_cuts(cols):
            part = term[:, :, low:high]
            left = sorted(self.bits, reverse=True)
            part = part.reshape((2,) * len(left) + part.shape[1:])
            for bit in order:
                axis = left.index(bit)
                my_bit = (self.t_at // bit) % 2
                mine = lax.dynamic_index_in_dim(part, my_bit, axis, keepdims=False)
                other = lax.dynamic_index_in_dim(part, 1 - my_bit, axis, keepdims=False)
                got = self.swap(other, 2 * bit)
                part = (mine.astype(jnp.float32) + got.astype(jnp.float32)).astype(jnp.bfloat16)
                left.remove(bit)
            parts.append(part)
        total = jnp.concatenate(parts, axis=1)
        return lax.psum_scatter(total, "narrow", scatter_dimension=0, tiled=True)

    def gather_tokens(self, rows):
        if self.planes != 4:
            every = lax.all_gather(
                rows, MESH_AXES, axis=0, tiled=False, axis_index_groups=self.same_plane
            )
            return [every[k] for k in range(self.planes)]
        half = rows.shape[0] // 2
        by_x = self.swap(rows, 2)
        by_y = self.swap(rows, 4)
        corner = [self.swap(by_y[:half], 2), self.swap(by_x[half:], 4)]
        return [rows, by_x, by_y, jnp.concatenate(corner)]

    def scatter_tokens(self, blocks):
        if self.planes != 4:
            every = jnp.concatenate([b.astype(jnp.bfloat16) for b in blocks])
            total = lax.psum_scatter(
                every, MESH_AXES, scatter_dimension=0, tiled=True, axis_index_groups=self.same_plane
            )
            return total.astype(jnp.float32)
        own, by_x, by_y, corner = blocks
        half = own.shape[0] // 2
        top = self.swap(corner[:half], 2).astype(jnp.float32)
        bottom = self.swap(corner[half:], 4).astype(jnp.float32)
        by_y = jnp.concatenate([by_y[:half] + top, by_y[half:]]).astype(jnp.bfloat16)
        by_x = jnp.concatenate([by_x[:half], by_x[half:] + bottom]).astype(jnp.bfloat16)
        return (
            own.astype(jnp.float32)
            + self.swap(by_x, 2).astype(jnp.float32)
            + self.swap(by_y, 4).astype(jnp.float32)
        )

    def plane_counts(self, counts, cap):
        if self.planes != 4:
            return jnp.full((self.planes,), cap, jnp.int32)
        at = [((self.t_at ^ d) * 2 + self.core_at) * self.n + self.z_at for d in range(4)]
        return counts[jnp.stack(at)]

    def trade_columns(self, pieces):
        came = jnp.zeros_like(pieces)
        for d in range(self.planes):
            piece = lax.dynamic_index_in_dim(pieces, self.t_at ^ d, 0)
            if d:
                piece = self.swap(piece, 2 * d)
            came = lax.dynamic_update_slice(came, piece, (self.t_at ^ d, 0, 0))
        return came

    def gather_first(self, qkv, out, gateup, down, gains, count):
        rows = qkv.shape[0]
        low = jnp.bfloat16
        if self.planes == 4 and self.n > 1:
            digits = jnp.stack([count // 16, count % 16]).astype(low)
            ext = jnp.concatenate([gains.reshape(1, 2 * rows), jnp.zeros((15, 2 * rows), gains.dtype)])
            ext = lax.dynamic_update_slice(ext, digits[None], (1, 0))
            qkv_all, out_all, ext_all, came, down_all = gather_first(
                qkv, out, gateup, down, ext, self.planes, self.n
            )
            ext_all = ext_all.reshape(self.wide * self.n, 16, 2 * rows)
            gain_full = ext_all[:, 0].reshape(-1, 2, rows).transpose(1, 0, 2).reshape(2, -1)
            digits = ext_all[:, 1, :2].astype(jnp.int32)
            return (
                qkv_all.reshape(self.wide * self.n * rows, -1),
                out_all,
                came,
                down_all.reshape(-1, down.shape[1]),
                gain_full,
                digits[:, 0] * 16 + digits[:, 1],
            )
        return (
            lax.all_gather(qkv.astype(low), MESH_AXES, axis=0, tiled=True),
            lax.all_gather(out.astype(low), MESH_AXES, axis=0, tiled=True),
            self.trade_columns(split_columns(gateup.astype(low), self.planes)),
            lax.all_gather(
                down.astype(low), MESH_AXES, axis=0, tiled=True, axis_index_groups=self.same_chip
            ),
            lax.all_gather(gains, MESH_AXES, axis=1, tiled=True),
            lax.all_gather(count, MESH_AXES),
        )


def dot32(a, b):
    return jnp.dot(a, b, preferred_element_type=jnp.float32)


def dot_low(a, b):
    return jnp.dot(a, b, preferred_element_type=jnp.float32).astype(jnp.bfloat16)


def together(arrays):
    return arrays[0] if len(arrays) == 1 else jnp.concatenate(arrays)


def split_columns(shard, planes):
    units = FF // planes
    found = []
    for t in range(planes):
        for low, high in unit_groups(units):
            for start in (t * units, FF + t * units):
                found.append(shard[:, start + low : start + high])
    return jnp.concatenate(found, axis=1).reshape(shard.shape[0], planes, 2 * units).transpose(1, 0, 2)


def join_columns(pieces):
    planes, _, cols = pieces.shape
    gates, uppers = [], []
    for t in range(planes):
        for low, high in unit_groups(cols // 2):
            gates.append(pieces[t, :, 2 * low : low + high])
            uppers.append(pieces[t, :, low + high : 2 * high])
    return jnp.concatenate(gates + uppers, axis=1)


def pick_live(mask, cap):
    flat = mask.reshape(-1)
    rows = flat.shape[0]
    at = jnp.arange(rows, dtype=jnp.int32)
    rank = jnp.sum(jnp.where(at[None, :] <= at[:, None], flat[None, :], 0), axis=1) - 1
    slot = jnp.arange(cap, dtype=jnp.int32)
    chosen = (rank[None, :] == slot[:, None]) & (flat[None, :] == 1)
    return chosen, slot < jnp.sum(flat)


def layer(links, cap, given):
    (
        tokens,
        active,
        cotangent,
        gain_full,
        counts,
        qkv_low,
        out_all,
        pieces,
        down_low,
    ) = given
    n, planes = links.n, links.planes
    seq_count, span_len, width = tokens.shape
    row_count = seq_count * span_len
    seq_len = n * span_len
    kv_width = KV_HEADS * HEAD_DIM
    ff_part = FF // planes
    shard_rows = pieces.shape[1]
    low = jnp.bfloat16


    def codes_of(block):
        mask = lax.dynamic_slice_in_dim(active, jnp.maximum(block, 0) * span_len, span_len, 1)
        chosen, live = pick_live(mask, cap)
        code = jnp.arange(seq_count, dtype=jnp.int32)[:, None] * seq_len + jnp.arange(span_len, dtype=jnp.int32)
        code = jnp.sum(jnp.where(chosen, code.reshape(1, -1), 0), axis=1) + block * span_len
        return chosen, live & (block >= 0), code

    chosen, live, own_code = codes_of(links.z_at)
    key_codes = []
    for r in range(n):
        _, there, code = codes_of(links.z_at - r)
        key_codes.append(jnp.where(there, code, seq_count * seq_len))
    key_code = jnp.concatenate(key_codes)[:, None]
    query_code = jnp.where(live, own_code, -1)[None]
    query_base = jnp.where(live, own_code // seq_len * seq_len, 0)[None]
    places = jnp.where(live, own_code % seq_len, 0).astype(jnp.float32)
    cosine_table, sine_table = rotary_tables(places)
    picker = chosen.astype(low)
    live_rows = live.astype(jnp.float32)[:, None]

    inputs = dot32(picker, tokens.reshape(row_count, width))
    down_grad = dot_low(picker, cotangent.reshape(row_count, width))
    upstream = down_grad.astype(jnp.float32)
    down_grad_blocks = links.gather_tokens(down_grad)

    normed, inverse_one = norm_forward(inputs, gain_full[0])
    normed_low = normed.astype(low)
    kv_part = dot32(normed_low, qkv_low[:, width:])
    kv_low = jnp.concatenate(
        [rotate_heads(kv_part[:, :kv_width], cosine_table, sine_table), kv_part[:, kv_width:]], axis=1
    ).astype(low)
    query_low = rotate_heads(dot32(normed_low, qkv_low[:, :width]), cosine_table, sine_table).astype(low)
    ids = 1 if cap < row_count else 3
    codes = (key_code, query_code, query_base)
    if out_all.ndim == 2:
        out_low = out_all
        attended_low, totals, kv_all = attend(query_low, kv_low, *codes, n, ids)
    else:
        attended_low, totals, kv_all, out_all = attend(query_low, kv_low, *codes, n, ids, out_all)
        out_low = out_all.reshape(width, width)
    pieces, attended_low = lax.optimization_barrier((pieces, attended_low))
    gateup_low = lax.all_gather(
        pieces, MESH_AXES, axis=1, tiled=True, axis_index_groups=links.same_chip
    ).reshape(width, 2 * ff_part)
    middle = inputs + live_rows * dot32(attended_low, out_low)
    normed_mid, inverse_two = norm_forward(middle, gain_full[1])
    blocks = links.gather_tokens(normed_mid.astype(low))
    lives = links.plane_counts(counts, cap)

    parts = [[k] for k in range(planes)] if planes != 4 else [[0], [1, 2], [3]]
    hidden_blocks, gateup_grad_blocks, mid_terms = [], [], [None] * planes
    row_parts, grad_parts = [], []
    for part in parts:
        rows = together([blocks[k] for k in part])
        grads = together([down_grad_blocks[k] for k in part])
        row_parts.append(rows)
        grad_parts.append(grads)
        hidden, gateup_grad, back = mlp_block(rows, grads, lives[jnp.array(part)], gateup_low, down_low, cap)
        hidden_blocks.append(hidden)
        gateup_grad_blocks.append(gateup_grad)
        for i, k in enumerate(part):
            mid_terms[k] = back[i * cap : (i + 1) * cap]
    grad_normed_mid = links.scatter_tokens(mid_terms)
    hidden_all = jnp.concatenate(hidden_blocks)

    term_down = dot_low(hidden_all.T, jnp.concatenate(grad_parts))
    term_gateup = dot_low(jnp.concatenate(row_parts).T, jnp.concatenate(gateup_grad_blocks))
    down_half = links.scatter_core(term_down.reshape(1, 2, ff_part // 2, width))[0]
    gateup_half = links.scatter_core(term_gateup.reshape(planes, 2, n * shard_rows, 2 * ff_part))
    grad_down = lax.psum_scatter(down_half, "narrow", scatter_dimension=0, tiled=True)
    grad_pieces = lax.psum_scatter(gateup_half, "narrow", scatter_dimension=1, tiled=True)
    down_terms = dot_low(hidden_all, down_low)
    order = [k for part in parts for k in part]
    down_terms = {k: down_terms[i * cap : (i + 1) * cap] for i, k in enumerate(order)}
    down_proj = links.scatter_tokens([down_terms[k] for k in range(planes)])
    layer_out = (middle + down_proj).astype(low)

    grad_middle = upstream + norm_backward(middle, inverse_two, gain_full[1], grad_normed_mid)
    branch_grad_low = grad_middle.astype(low)
    branch_grad_low, down_half, gateup_half = lax.optimization_barrier(
        (branch_grad_low, down_half, gateup_half)
    )
    grad_attended_low = dot_low(branch_grad_low, out_low.T)
    grad_out = links.scatter_rows(dot_low(attended_low.T, branch_grad_low))
    inner = jnp.sum(
        (grad_attended_low.astype(jnp.float32) * attended_low.astype(jnp.float32)).reshape(
            cap, HEADS, HEAD_DIM
        ),
        axis=-1,
    )
    inner = inner.T.reshape(KV_HEADS, GROUP, cap)
    grad_query, grad_kv = attend_back(
        query_low, kv_all, grad_attended_low, totals, inner, *codes, n, ids + 1
    )
    grad_query_low = rotate_heads(grad_query, cosine_table, -sine_table).astype(low)
    grad_q_rows = links.scatter_rows(dot_low(normed_low.T, grad_query_low))
    grad_kv_low = jnp.concatenate(
        [rotate_heads(grad_kv[:, :kv_width], cosine_table, -sine_table), grad_kv[:, kv_width:]], axis=1
    ).astype(low)
    grad_kv_rows = links.scatter_rows(dot_low(normed_low.T, grad_kv_low))
    grad_normed = dot32(grad_query_low, qkv_low[:, :width].T) + dot32(grad_kv_low, qkv_low[:, width:].T)
    grad_tokens = (
        grad_middle + norm_backward(inputs, inverse_one, gain_full[0], grad_normed)
    ).astype(low)

    def spread(packed, skipped):
        back = lax.dot_general(
            picker, packed, (((0,), (0,)), ((), ())), preferred_element_type=jnp.float32
        ).astype(low)
        mask = lax.dynamic_slice_in_dim(active, links.z_at * span_len, span_len, 1)
        return jnp.where(mask[:, :, None] == 1, back.reshape(skipped.shape), skipped)

    layer_out, grad_tokens = spread(layer_out, tokens), spread(grad_tokens, cotangent)
    grad_gateup = join_columns(links.trade_columns(grad_pieces))
    grad_qkv = jnp.concatenate([grad_q_rows, grad_kv_rows], axis=1)
    return layer_out, grad_tokens, grad_qkv, grad_out, grad_gateup, grad_down


def on_device(
    tokens,
    active,
    cotangent,
    gain_rows,
    w_qkv,
    w_out,
    w_gateup,
    w_down,
    moment_gains,
    moment_qkv,
    moment_out,
    moment_gateup,
    moment_down,
    average_gains,
    average_qkv,
    average_out,
    average_gateup,
    average_down,
):
    links = Links()
    seq_count, span_len, _ = tokens.shape
    row_count = seq_count * span_len
    low = jnp.bfloat16

    gains_low = gain_rows.astype(low)
    own_mask = lax.dynamic_slice_in_dim(active, links.z_at * span_len, span_len, 1)
    qkv_low, out_all, pieces, down_low, gain_full, counts = links.gather_first(
        w_qkv, w_out, w_gateup, w_down, gains_low, jnp.sum(own_mask)
    )
    gain_full = gain_full.astype(jnp.float32)
    given = (tokens, active, cotangent, gain_full, counts, qkv_low, out_all, pieces, down_low)
    few = -(-3 * row_count // 4 // 128) * 128
    if few < row_count:
        found = lax.cond(
            jnp.max(counts) <= few,
            lambda *g: layer(links, few, g),
            lambda *g: layer(links, row_count, g),
            *given,
        )
    else:
        found = layer(links, row_count, given)
    layer_out, grad_tokens, grad_qkv, grad_out, grad_gateup, grad_down = found
    grad_qkv, grad_out, grad_gateup, grad_down = (
        g.astype(jnp.float32) for g in (grad_qkv, grad_out, grad_gateup, grad_down)
    )

    def gain_grad(shard, gradient, row):
        return jnp.sum(shard.astype(low).astype(jnp.float32) * gradient, axis=1) / gains_low[row].astype(jnp.float32)

    grad_gains = jnp.stack([gain_grad(w_qkv, grad_qkv, 0), gain_grad(w_gateup, grad_gateup, 1)])
    state_gains = advance_state(gain_rows, moment_gains, average_gains, grad_gains)
    state_qkv = advance_state(w_qkv, moment_qkv, average_qkv, grad_qkv)
    state_out = advance_state(w_out, moment_out, average_out, grad_out)
    state_gateup = advance_state(w_gateup, moment_gateup, average_gateup, grad_gateup)
    state_down = advance_state(w_down, moment_down, average_down, grad_down)
    return (
        layer_out,
        grad_tokens,
        grad_gains,
        grad_qkv,
        grad_out,
        grad_gateup,
        grad_down,
        state_gains[0],
        state_qkv[0],
        state_out[0],
        state_gateup[0],
        state_down[0],
        state_gains[1],
        state_qkv[1],
        state_out[1],
        state_gateup[1],
        state_down[1],
        state_gains[2],
        state_qkv[2],
        state_out[2],
        state_gateup[2],
        state_down[2],
    )


def solution(mesh):
    in_specs = (
        P("wide", "narrow", None),
        P("wide", None),
        P("wide", "narrow", None),
        P(None, ("wide", "narrow")),
        P(("wide", "narrow"), None),
        P(("wide", "narrow"), None),
        P(("wide", "narrow"), None),
        P(("wide", "narrow"), None),
        P(None, ("wide", "narrow")),
        P(("wide", "narrow"), None),
        P(("wide", "narrow"), None),
        P(("wide", "narrow"), None),
        P(("wide", "narrow"), None),
        P(None, ("wide", "narrow")),
        P(("wide", "narrow"), None),
        P(("wide", "narrow"), None),
        P(("wide", "narrow"), None),
        P(("wide", "narrow"), None),
    )
    out_specs = (
        P("wide", "narrow", None),
        P("wide", "narrow", None),
        P(None, ("wide", "narrow")),
        P(("wide", "narrow"), None),
        P(("wide", "narrow"), None),
        P(("wide", "narrow"), None),
        P(("wide", "narrow"), None),
        P(None, ("wide", "narrow")),
        P(("wide", "narrow"), None),
        P(("wide", "narrow"), None),
        P(("wide", "narrow"), None),
        P(("wide", "narrow"), None),
        P(None, ("wide", "narrow")),
        P(("wide", "narrow"), None),
        P(("wide", "narrow"), None),
        P(("wide", "narrow"), None),
        P(("wide", "narrow"), None),
        P(None, ("wide", "narrow")),
        P(("wide", "narrow"), None),
        P(("wide", "narrow"), None),
        P(("wide", "narrow"), None),
        P(("wide", "narrow"), None),
    )
    return jax.shard_map(
        on_device, mesh=mesh, in_specs=in_specs, out_specs=out_specs, check_vma=False
    )
```

time: 1040 us -> 964 us (0.927)
  Pallas kernels: 163 us -> 307 us
  matrix products: 230 us -> 112 us
  waiting for transfers between devices: 304 us -> 230 us
  starting transfers between devices: 72.7 us -> 36.6 us
    ppermute x6 -> x0, waiting for transfers between devices: 164 us -> none  [shift(): return lax.ppermute(values, MESH_AXES, pairs)]
    pallas_call x2 -> x5, Pallas kernels: 71.2 us -> 209 us  [the longest x1 99.6 us: attend_back(): pl.pallas_call(functools.partial(attend_back_kernel, n), in_specs=[in_vme...]
    dot_general x25 -> x6, matrix products: 143 us -> 32.1 us  [dot32(): return jnp.dot(a, b, preferred_element_type=jnp.float32)]
    another operation x3 -> x202, local copies, waits for them, and re-layouts: 2.33 us -> 73.3 us
    ppermute x50 -> x36, waiting for transfers between devices: 126 us -> 190 us  [swap(): return lax.ppermute(values, MESH_AXES, pairs)]
    ppermute x6 -> x0, starting transfers between devices: 30.7 us -> none  [shift(): return lax.ppermute(values, MESH_AXES, pairs)]
    unnamed x250 -> x52, local copies, waits for them, and re-layouts: 35.2 us -> 9.3 us
    dynamic_update_slice x16 -> x0, local copies, waits for them, and re-layouts: 19.3 us -> none  [gather_planes(): lax.dynamic_update_slice(whole, piece[None], (self.wide_at ^ flip, 0, low))]
  transfers between devices with their start and end apart: 63 -> 42, of which waited for: 22 -> 19; matrix products, arithmetic and copies ran while one was open for 30% -> 21% of each run, Pallas kernels for 7% -> 10%
where the time goes in v2:
time: 964 us; the launch traced here: 949 us
  Pallas kernels  307 us (32%)
  waiting for transfers between devices  230 us (24%)
  local copies, waits for them, and re-layouts  123 us (13%)
  other arithmetic  112 us (12%)
  matrix products  112 us (12%)
  starting transfers between devices  36.6 us (4%)
  between operations  18.1 us (2%)
  loops' own time  10.8 us (1%)
    ppermute x36, waiting for transfers between devices, swap(): return lax.ppermute(values, MESH_AXES, pairs)  190 us
    pallas_call x1, Pallas kernels, attend_back(): pl.pallas_call(functools.partial(attend_back_kernel, n), in_specs=[in_vme...  99.6 us
    pallas_call x1, Pallas kernels, gather_first(): pl.pallas_call(functools.partial(gather_kernel, n), out_shape=(jax.ShapeD...  98.1 us
    another operation x202, local copies, waits for them, and re-layouts  73.3 us
    dot_general x8, matrix products, dot_low(): jnp.dot(a, b, preferred_element_type=jnp.float32).astype(jnp.bfloat16)  69.4 us
    pallas_call x3, Pallas kernels, mlp_block(): pl.pallas_call(functools.partial(mlp_kernel, cap, counts), grid_spec=pltp...  64.9 us
    pallas_call x1, Pallas kernels, attend(): pl.pallas_call(functools.partial(attend_kernel, n, len(outs)), in_specs=[...  44.1 us
    ppermute x36, starting transfers between devices, swap(): return lax.ppermute(values, MESH_AXES, pairs)  36.1 us
  transfers between devices with their start and end apart: 42, of which 19 were waited for; matrix products, arithmetic and copies ran while one was open for 21% of the time, Pallas kernels for 10%

profile of v2, /device:TPU:0, one launch (start us, length us, event | category | flops | bytes accessed | tf_op | source)
XLA Modules:
  0.0 949.0 jit_solution(17436737529904385458)
XLA Ops:
  17.9 98.1 %gather_first.1 = (bf16[4,2,4,64,3072]{4,3,2,1,0:T(8,128)(2,1)}, bf16[4,2,4,64,2048]{4,3,2,1,0:T(8,128)(2,1)}, bf16[4,2,4,16,128]{4,3,2,1,0:T(8,128)(2,1)S(1)}, ...) custom-call(f32[64,3072]{1,0:T(8,128)S(1)} %copy-done.4, f32[64,2048]{1,0:T(8,128)S(1)} %copy-done.6, ...), custom_call_target="tpu_custom_call" | custom-call | tf_op jit(solution)/shard_map/gather_first/pallas_call | solution.py:379
  117.6 806.9 %conditional.3 = (bf16[2,256,2048]{2,1,0:T(8,128)(2,1)}, bf16[2,256,2048]{2,1,0:T(8,128)(2,1)}, f32[64,3072]{1,0:T(8,128)S(1)}, f32[64,11264]{1,0:T(8,128)S(1)},...) conditional(s32[]{:T(128)} %convert_element_type.761, (s32[]{:T(128)}, s32[2,1024]{1,0:T(2,128)S(1)}, ...), branch_computations={%region_2.25_spmd, %region_25.48_spmd} | conditional | flops 173134053376 | bytes 1785272576
  153.2 44.1 %attend.3 = (bf16[384,2048]{1,0:T(8,128)(2,1)S(1)}, f32[4,4,384]{2,1,0:T(4,128)S(1)}, bf16[1536,1024]{1,0:T(8,128)(2,1)}, bf16[4,2,4,64,2048]{4,3,2,1,0:T(8,128)(2,1)S(1)}) custom-call(bf16[384,2048]{1,0:T(8,128)(2,1)S(1)} %get-tuple-element.784.refs_0_.q_ref, bf16[384,1024]{1,0:T(8,128)(2,1)S(1)} %fusion.205.refs_1_, ...), custom_call_target="tpu_custom_call", output_to_operand_aliasing={{3}: (5, {})} | custom-call | flops 4831838208 | bytes 6291456 | tf_op jit(solution)/shard_map/cond/branch_1_fun/attend/pallas_call | solution.py:532
  202.0 7.9 multiply_reduce_fusion.6
  221.9 28.1 %collective-permute-done.37 = bf16[384,2048]{1,0:T(8,128)(2,1)} collective-permute-done((bf16[384,2048]{1,0:T(8,128)(2,1)}, bf16[384,2048]{1,0:T(8,128)(2,1)}, u32[]{:S(2)}, u32[]{:S(2)}) %collective-permute-start.37) | collective-permute-done | bytes 1572896 | tf_op jit(solution)/shard_map/cond/branch_1_fun/ppermute | solution.py:717
  254.6 29.0 %collective-permute-done.39 = bf16[384,2048]{1,0:T(8,128)(2,1)S(1)} collective-permute-done((bf16[384,2048]{1,0:T(8,128)(2,1)}, bf16[384,2048]{1,0:T(8,128)(2,1)S(1)}, u32[]{:S(2)}, u32[]{:S(2)}) %collective-permute-start.39) | collective-permute-done | bytes 1572896 | tf_op jit(solution)/shard_map/cond/branch_1_fun/ppermute | solution.py:717
  305.2 13.6 %collective-permute-done.42 = bf16[192,2048]{1,0:T(8,128)(2,1)S(1)} collective-permute-done((bf16[192,2048]{1,0:T(8,128)(2,1)S(1)}, bf16[192,2048]{1,0:T(8,128)(2,1)S(1)}, u32[]{:S(2)}, u32[]{:S(2)}) %collective-permute-start.42) | collective-permute-done | bytes 786464 | tf_op jit(solution)/shard_map/cond/branch_1_fun/ppermute | solution.py:717
  320.9 12.5 %all-gather.5.cloned.1.call-done = bf16[4,512,2816]{2,1,0:T(8,128)(2,1)} async-done(((bf16[4,64,2816]{2,1,0:T(8,128)(2,1)}), bf16[4,512,2816]{2,1,0:T(8,128)(2,1)}) %all-gather.5.cloned.1.call-update) | async-done | bytes 11534352 | tf_op jit(solution)/shard_map/cond/branch_1_fun/all_gather | solution.py:937
  333.4 19.1 %mlp_block.9 = (bf16[384,1408]{1,0:T(8,128)(2,1)}, bf16[384,2816]{1,0:T(8,128)(2,1)}, bf16[384,2048]{1,0:T(8,128)(2,1)}) custom-call(s32[1]{0:T(128)} %get-tuple-element.807.live_ref, bf16[384,2048]{1,0:T(8,128)(2,1)} %get-tuple-element.505.rows_ref, bf16[384,2048]{1,0:T(8,128)(2,1)} %get-tuple-element.813.grad_ref, bf16[2048,2816]{1,0:T(8,128)(2,1)} %bitcast.828, ...), custom_call_target="tpu_custom_call" | custom-call | flops 11072962560 | bytes 26738688 | tf_op jit(solution)/shard_map/cond/branch_1_fun/mlp_block/pallas_call | solution.py:124
  352.5 17.6 %mlp_block.11 = (bf16[384,1408]{1,0:T(8,128)(2,1)}, bf16[384,2816]{1,0:T(8,128)(2,1)}, bf16[384,2048]{1,0:T(8,128)(2,1)}) custom-call(s32[1]{0:T(128)} %get-tuple-element.806.live_ref, bf16[384,2048]{1,0:T(8,128)(2,1)} %pad_maximum_fusion.16.rows_ref, bf16[384,2048]{1,0:T(8,128)(2,1)} %pad_maximum_fusion.17.grad_ref, bf16[2048,2816]{1,0:T(8,128)(2,1)} %bitcast.829, ...), custom_call_target="tpu_custom_call" | custom-call | flops 11072962560 | bytes 26738688 | tf_op jit(solution)/shard_map/cond/branch_1_fun/mlp_block/pallas_call | solution.py:124
  370.1 28.1 %mlp_block.10 = (bf16[768,1408]{1,0:T(8,128)(2,1)}, bf16[768,2816]{1,0:T(8,128)(2,1)}, bf16[768,2048]{1,0:T(8,128)(2,1)}) custom-call(s32[2]{0:T(128)} %gather_fusion.3, bf16[768,2048]{1,0:T(8,128)(2,1)} %pad_maximum_fusion.14.rows_ref, bf16[768,2048]{1,0:T(8,128)(2,1)} %pad_maximum_fusion.15.grad_ref, bf16[2048,2816]{1,0:T(8,128)(2,1)} %bitcast.830, ...), custom_call_target="tpu_custom_call" | custom-call | flops 22145925120 | bytes 36175872 | tf_op jit(solution)/shard_map/cond/branch_1_fun/mlp_block/pallas_call | solution.py:124
  398.3 24.7 %convolution_convert_fusion.9 = bf16[2048,2816]{1,0:T(8,128)(2,1)S(1)} fusion(bf16[1536,2048]{1,0:T(8,128)(2,1)} %constant_dynamic-update-slice_fusion.132, bf16[384,2816]{1,0:T(8,128)(2,1)} %get-tuple-element.149, bf16[768,2816]{1,0:T(8,128)(2,1)} %get-tuple-element.148, bf16[384,2816]{1,0:T(8,128)(2,1)} %get-tuple-element.147), kind=kOutput, calls=%fused_computation.511 | convolution fusion | flops 17748459520 | bytes 26476544 | tf_op jit(solution)/shard_map/cond/branch_1_fun/dot_general | solution.py:837
  439.1 8.1 fusion.160
  453.5 11.8 %convolution_convert_fusion.12 = bf16[1408,2048]{1,0:T(8,128)(2,1)S(1)} fusion(bf16[1536,1408]{1,0:T(8,128)(2,1)S(1)} %constant_dynamic-update-slice_fusion.124, bf16[1536,2048]{1,0:T(8,128)(2,1)} %constant_dynamic-update-slice_fusion.127), kind=kOutput, calls=%fused_computation.523 | convolution fusion | flops 8861253632 | bytes 16384000 | tf_op jit(solution)/shard_map/cond/branch_1_fun/dot_general | solution.py:837
  465.3 10.5 %convolution_convert_fusion.13 = bf16[1536,2048]{1,0:T(8,128)(2,1)S(1)} fusion(bf16[1536,1408]{1,0:T(8,128)(2,1)S(1)} %constant_dynamic-update-slice_fusion.124, bf16[1408,2048]{1,0:T(8,128)(2,1)S(1)} %bitcast.850), kind=kOutput, calls=%fused_computation.524 | convolution fusion | flops 8861515776 | bytes 16384000 | tf_op jit(solution)/shard_map/cond/branch_1_fun/dot_general | solution.py:837
  488.9 11.6 %collective-permute-done.46 = bf16[192,2048]{1,0:T(8,128)(2,1)} collective-permute-done((bf16[192,2048]{1,0:T(8,128)(2,1)}, bf16[192,2048]{1,0:T(8,128)(2,1)}, u32[]{:S(2)}, u32[]{:S(2)}) %collective-permute-start.46) | collective-permute-done | bytes 786464 | tf_op jit(solution)/shard_map/cond/branch_1_fun/ppermute | solution.py:717
  506.7 28.1 %collective-permute-done.51 = bf16[384,2048]{1,0:T(8,128)(2,1)S(1)} collective-permute-done((bf16[384,2048]{1,0:T(8,128)(2,1)}, bf16[384,2048]{1,0:T(8,128)(2,1)S(1)}, u32[]{:S(2)}, u32[]{:S(2)}) %collective-permute-start.51) | collective-permute-done | bytes 1572896 | tf_op jit(solution)/shard_map/cond/branch_1_fun/ppermute | solution.py:717
  563.0 99.6 %attend_back.3 = (f32[384,2048]{1,0:T(8,128)}, f32[384,1024]{1,0:T(8,128)}) custom-call(bf16[384,2048]{1,0:T(8,128)(2,1)} %copy-done.14, bf16[1536,1024]{1,0:T(8,128)(2,1)} %get-tuple-element.146.kv_all, bf16[384,2048]{1,0:T(8,128)(2,1)} %copy-done.111, f32[4,4,384]{2,1,0:T(4,128)} %copy-done.19, f32[4,4,384]{2,1,0:T(4,128)} %reshape.1072.inner_ref, ...), custom_call_target="tpu_custom_call" | custom-call | flops 12079595520 | bytes 12582912 | tf_op jit(solution)/shard_map/cond/branch_1_fun/attend_back/pallas_call | solution.py:634
  701.3 23.0 %collective-permute-done.60 = bf16[2,256,512]{2,1,0:T(8,128)(2,1)S(1)} collective-permute-done((bf16[2,256,512]{2,1,0:T(8,128)(2,1)}, bf16[2,256,512]{2,1,0:T(8,128)(2,1)S(1)}, u32[]{:S(2)}, u32[]{:S(2)}) %collective-permute-start.60) | collective-permute-done | bytes 524320 | tf_op jit(solution)/shard_map/cond/branch_1_fun/ppermute | solution.py:717
  726.8 10.4 %collective-permute-done.62 = bf16[2,256,512]{2,1,0:T(8,128)(2,1)} collective-permute-done((bf16[2,256,512]{2,1,0:T(8,128)(2,1)}, bf16[2,256,512]{2,1,0:T(8,128)(2,1)}, u32[]{:S(2)}, u32[]{:S(2)}) %collective-permute-start.62) | collective-permute-done | bytes 524320 | tf_op jit(solution)/shard_map/cond/branch_1_fun/ppermute | solution.py:717
  762.3 18.4 %collective-permute-done.55 = bf16[2,256,1024]{2,1,0:T(8,128)(2,1)} collective-permute-done((bf16[2,256,1024]{2,1,0:T(8,128)(2,1)S(1)}, bf16[2,256,1024]{2,1,0:T(8,128)(2,1)}, u32[]{:S(2)}, u32[]{:S(2)}) %collective-permute-start.55) | collective-permute-done | bytes 1048608 | tf_op jit(solution)/shard_map/cond/branch_1_fun/ppermute | solution.py:717
  785.4 8.5 fusion.168
  796.8 13.6 %collective-permute-done.58 = bf16[256,1024]{1,0:T(8,128)(2,1)S(1)} collective-permute-done((bf16[256,1024]{1,0:T(8,128)(2,1)S(1)}, bf16[256,1024]{1,0:T(8,128)(2,1)S(1)}, u32[]{:S(2)}, u32[]{:S(2)}) %collective-permute-start.58) | collective-permute-done | bytes 524320 | tf_op jit(solution)/shard_map/cond/branch_1_fun/ppermute | solution.py:717
  846.7 27.6 %reduce-scatter.25.cloned.1.call-done = bf16[64,2048]{1,0:T(8,128)(2,1)} async-done(((bf16[256,2048]{1,0:T(8,128)(2,1)}), bf16[64,2048]{1,0:T(8,128)(2,1)}) %reduce-scatter.25.cloned.1.call-update) | async-done | bytes 262160 | tf_op jit(solution)/shard_map/cond/branch_1_fun/reduce_scatter | solution.py:751
  (524 shorter events, 326.3 us)
Async XLA Ops:
  126.4 207.0 %all-gather.5.cloned.1.call-start = ((), (), s32[]{:S(2)}) async-start(), calls=%async_computation.16 | async-start | bytes 12976128 | tf_op jit(solution)/shard_map/cond/branch_1_fun/all_gather | solution.py:937
  201.2 632.8 %reduce-scatter.27.cloned.1.call-start = ((), (), s32[]{:S(2)}) async-start(), calls=%async_computation.20 | async-start | bytes 7208960 | tf_op jit(solution)/shard_map/cond/branch_1_fun/reduce_scatter | solution.py:966
  212.7 37.3 %collective-permute-start.37 = (bf16[384,2048]{1,0:T(8,128)(2,1)}, bf16[384,2048]{1,0:T(8,128)(2,1)}, u32[]{:S(2)}, u32[]{:S(2)}) collective-permute-start(bf16[384,2048]{1,0:T(8,128)(2,1)} %get-tuple-element.505.rows_ref), channel_id=1, source_target_pairs={{0,16},{1,17},{2,18},{3,19},{4,20},{5,21},{6,22},{7,23},{8,24},{9,... | collective-permute-start | bytes 4718600 | tf_op jit(solution)/shard_map/cond/branch_1_fun/ppermute | solution.py:717
  213.9 38.6 %collective-permute-start.36 = (bf16[384,2048]{1,0:T(8,128)(2,1)}, bf16[384,2048]{1,0:T(8,128)(2,1)}, u32[]{:S(2)}, u32[]{:S(2)}) collective-permute-start(bf16[384,2048]{1,0:T(8,128)(2,1)} %get-tuple-element.505.rows_ref), channel_id=1, source_target_pairs={{0,8},{1,9},{2,10},{3,11},{4,12},{5,13},{6,14},{7,15},{8,0},{9,1},... | collective-permute-start | bytes 4718600 | tf_op jit(solution)/shard_map/cond/branch_1_fun/ppermute | solution.py:717
  217.4 66.1 %collective-permute-start.39 = (bf16[384,2048]{1,0:T(8,128)(2,1)}, bf16[384,2048]{1,0:T(8,128)(2,1)S(1)}, u32[]{:S(2)}, u32[]{:S(2)}) collective-permute-start(bf16[384,2048]{1,0:T(8,128)(2,1)} %get-tuple-element.813.grad_ref), channel_id=1, source_target_pairs={{0,16},{1,17},{2,18},{3,19},{4,20},{5,21},{6,22},{7,23},{8,24},{9,... | collective-permute-start | bytes 4718600 | tf_op jit(solution)/shard_map/cond/branch_1_fun/ppermute | solution.py:717
  218.6 66.5 %collective-permute-start.38 = (bf16[384,2048]{1,0:T(8,128)(2,1)}, bf16[384,2048]{1,0:T(8,128)(2,1)}, u32[]{:S(2)}, u32[]{:S(2)}) collective-permute-start(bf16[384,2048]{1,0:T(8,128)(2,1)} %get-tuple-element.813.grad_ref), channel_id=1, source_target_pairs={{0,8},{1,9},{2,10},{3,11},{4,12},{5,13},{6,14},{7,15},{8,0},{9,1},... | collective-permute-start | bytes 4718600 | tf_op jit(solution)/shard_map/cond/branch_1_fun/ppermute | solution.py:717
  251.2 50.7 %collective-permute-start.40 = (bf16[192,2048]{1,0:T(8,128)(2,1)S(1)}, bf16[192,2048]{1,0:T(8,128)(2,1)S(1)}, u32[]{:S(2)}, u32[]{:S(2)}) collective-permute-start(bf16[192,2048]{1,0:T(8,128)(2,1)S(1)} %slice.1664), channel_id=1, source_target_pairs={{0,8},{1,9},{2,10},{3,11},{4,12},{5,13},{6,14},{7,15},{8,0},{9,1},... | collective-permute-start | bytes 2359304 | tf_op jit(solution)/shard_map/cond/branch_1_fun/ppermute | solution.py:717
  253.7 49.3 %collective-permute-start.41 = (bf16[192,2048]{1,0:T(8,128)(2,1)S(1)}, bf16[192,2048]{1,0:T(8,128)(2,1)S(1)}, u32[]{:S(2)}, u32[]{:S(2)}) collective-permute-start(bf16[192,2048]{1,0:T(8,128)(2,1)S(1)} %slice.1665), channel_id=1, source_target_pairs={{0,16},{1,17},{2,18},{3,19},{4,20},{5,21},{6,22},{7,23},{8,24},{9,... | collective-permute-start | bytes 2359304 | tf_op jit(solution)/shard_map/cond/branch_1_fun/ppermute | solution.py:717
  283.7 35.1 %collective-permute-start.42 = (bf16[192,2048]{1,0:T(8,128)(2,1)S(1)}, bf16[192,2048]{1,0:T(8,128)(2,1)S(1)}, u32[]{:S(2)}, u32[]{:S(2)}) collective-permute-start(bf16[192,2048]{1,0:T(8,128)(2,1)S(1)} %slice.1666), channel_id=1, source_target_pairs={{0,8},{1,9},{2,10},{3,11},{4,12},{5,13},{6,14},{7,15},{8,0},{9,1},... | collective-permute-start | bytes 2359304 | tf_op jit(solution)/shard_map/cond/branch_1_fun/ppermute | solution.py:717
  286.4 32.4 %collective-permute-start.43 = (bf16[192,2048]{1,0:T(8,128)(2,1)S(1)}, bf16[192,2048]{1,0:T(8,128)(2,1)S(1)}, u32[]{:S(2)}, u32[]{:S(2)}) collective-permute-start(bf16[192,2048]{1,0:T(8,128)(2,1)S(1)} %slice.1667), channel_id=1, source_target_pairs={{0,16},{1,17},{2,18},{3,19},{4,20},{5,21},{6,22},{7,23},{8,24},{9,... | collective-permute-start | bytes 2359304 | tf_op jit(solution)/shard_map/cond/branch_1_fun/ppermute | solution.py:717
  447.2 395.7 %reduce-scatter.29.cloned.1.call-start = ((), (), s32[]{:S(2)}) async-start(), calls=%async_computation.21 | async-start | bytes 3604480 | tf_op jit(solution)/shard_map/cond/branch_1_fun/reduce_scatter | solution.py:965
  483.3 51.5 %collective-permute-start.51 = (bf16[384,2048]{1,0:T(8,128)(2,1)}, bf16[384,2048]{1,0:T(8,128)(2,1)S(1)}, u32[]{:S(2)}, u32[]{:S(2)}) collective-permute-start(bf16[384,2048]{1,0:T(8,128)(2,1)} %pad_maximum_fusion.21), channel_id=1, source_target_pairs={{0,16},{1,17},{2,18},{3,19},{4,20},{5,21},{6,22},{7,23},{8,24},{9,... | collective-permute-start | bytes 4718600 | tf_op jit(solution)/shard_map/cond/branch_1_fun/ppermute | solution.py:717
  485.7 49.1 %collective-permute-start.49 = (bf16[384,2048]{1,0:T(8,128)(2,1)}, bf16[384,2048]{1,0:T(8,128)(2,1)}, u32[]{:S(2)}, u32[]{:S(2)}) collective-permute-start(bf16[384,2048]{1,0:T(8,128)(2,1)} %pad_maximum_fusion.20), channel_id=1, source_target_pairs={{0,8},{1,9},{2,10},{3,11},{4,12},{5,13},{6,14},{7,15},{8,0},{9,1},... | collective-permute-start | bytes 4718600 | tf_op jit(solution)/shard_map/cond/branch_1_fun/ppermute | solution.py:717
  488.9 54.7 %collective-permute-start.52 = (bf16[1,704,2048]{2,1,0:T(8,128)(2,1)}, bf16[1,704,2048]{2,1,0:T(8,128)(2,1)}, u32[]{:S(2)}, u32[]{:S(2)}) collective-permute-start(bf16[1,704,2048]{2,1,0:T(8,128)(2,1)} %dynamic-slice_bitcast_fusion.20), channel_id=1, source_target_pairs={{0,4},{1,5},{2,6},{3,7},{4,0},{5,1},{6,2},{7,3},{8,12},{9,13},{10,... | collective-permute-start | bytes 8650760 | tf_op jit(solution)/shard_map/cond/branch_1_fun/ppermute | solution.py:717
  506.0 234.0 %collective-permute-start.47 = (bf16[384,2048]{1,0:T(8,128)(2,1)}, bf16[384,2048]{1,0:T(8,128)(2,1)}, u32[]{:S(2)}, u32[]{:S(2)}) collective-permute-start(bf16[384,2048]{1,0:T(8,128)(2,1)} %pad_maximum_fusion.19), channel_id=1, source_target_pairs={{0,16},{1,17},{2,18},{3,19},{4,20},{5,21},{6,22},{7,23},{8,24},{9,... | collective-permute-start | bytes 4718600 | tf_op jit(solution)/shard_map/cond/branch_1_fun/ppermute | solution.py:717
  548.5 296.6 %reduce-scatter.23.cloned.1.call-start = ((), (), s32[]{:S(2)}) async-start(), calls=%async_computation.18 | async-start | bytes 655360 | tf_op jit(solution)/shard_map/cond/branch_1_fun/reduce_scatter | solution.py:751
  676.9 64.9 %collective-permute-start.45 = (bf16[384,2048]{1,0:T(8,128)(2,1)}, bf16[384,2048]{1,0:T(8,128)(2,1)}, u32[]{:S(2)}, u32[]{:S(2)}) collective-permute-start(bf16[384,2048]{1,0:T(8,128)(2,1)} %pad_maximum_fusion.18), channel_id=1, source_target_pairs={{0,8},{1,9},{2,10},{3,11},{4,12},{5,13},{6,14},{7,15},{8,0},{9,1},... | collective-permute-start | bytes 4718600 | tf_op jit(solution)/shard_map/cond/branch_1_fun/ppermute | solution.py:717
  687.5 60.6 %collective-permute-start.54 = (bf16[4,256,2048]{2,1,0:T(8,128)(2,1)}, bf16[4,256,2048]{2,1,0:T(8,128)(2,1)}, u32[]{:S(2)}, u32[]{:S(2)}) collective-permute-start(bf16[4,256,2048]{2,1,0:T(8,128)(2,1)} %dynamic-slice_bitcast_fusion.19), channel_id=1, source_target_pairs={{0,4},{1,5},{2,6},{3,7},{4,0},{5,1},{6,2},{7,3},{8,12},{9,13},{10,... | collective-permute-start | bytes 12582920 | tf_op jit(solution)/shard_map/cond/branch_1_fun/ppermute | solution.py:717
  697.0 59.0 %collective-permute-start.64 = (bf16[4,256,2048]{2,1,0:T(8,128)(2,1)}, bf16[4,256,2048]{2,1,0:T(8,128)(2,1)}, u32[]{:S(2)}, u32[]{:S(2)}) collective-permute-start(bf16[4,256,2048]{2,1,0:T(8,128)(2,1)} %dynamic-slice_bitcast_fusion.18), channel_id=1, source_target_pairs={{0,4},{1,5},{2,6},{3,7},{4,0},{5,1},{6,2},{7,3},{8,12},{9,13},{10,... | collective-permute-start | bytes 12582920 | tf_op jit(solution)/shard_map/cond/branch_1_fun/ppermute | solution.py:717
  748.0 97.6 %reduce-scatter.21.cloned.1.call-start = ((), (), s32[]{:S(2)}) async-start(), calls=%async_computation.17 | async-start | bytes 1310720 | tf_op jit(solution)/shard_map/cond/branch_1_fun/reduce_scatter | solution.py:751
  761.3 50.8 %collective-permute-start.65 = (bf16[2,256,1024]{2,1,0:T(8,128)(2,1)}, bf16[2,256,1024]{2,1,0:T(8,128)(2,1)}, u32[]{:S(2)}, u32[]{:S(2)}) collective-permute-start(bf16[2,256,1024]{2,1,0:T(8,128)(2,1)} %dynamic-slice_bitcast_fusion.23), channel_id=1, source_target_pairs={{0,8},{1,9},{2,10},{3,11},{4,12},{5,13},{6,14},{7,15},{8,0},{9,1},... | collective-permute-start | bytes 3145736 | tf_op jit(solution)/shard_map/cond/branch_1_fun/ppermute | solution.py:717
  811.8 62.5 %reduce-scatter.25.cloned.1.call-start = ((), (), s32[]{:S(2)}) async-start(), calls=%async_computation.19 | async-start | bytes 1310720 | tf_op jit(solution)/shard_map/cond/branch_1_fun/reduce_scatter | solution.py:751
  838.0 40.4 %collective-permute-start.69 = (bf16[1,64,2816]{2,1,0:T(8,128)(2,1)}, bf16[1,64,2816]{2,1,0:T(8,128)(2,1)}, u32[]{:S(2)}, u32[]{:S(2)}) collective-permute-start(bf16[1,64,2816]{2,1,0:T(8,128)(2,1)} %get-tuple-element.775), channel_id=1, source_target_pairs={{0,8},{1,9},{2,10},{3,11},{4,12},{5,13},{6,14},{7,15},{8,0},{9,1},... | collective-permute-start | bytes 1081352 | tf_op jit(solution)/shard_map/cond/branch_1_fun/ppermute | solution.py:717
  844.2 36.0 %collective-permute-start.70 = (bf16[1,64,2816]{2,1,0:T(8,128)(2,1)S(1)}, bf16[1,64,2816]{2,1,0:T(8,128)(2,1)}, u32[]{:S(2)}, u32[]{:S(2)}) collective-permute-start(bf16[1,64,2816]{2,1,0:T(8,128)(2,1)S(1)} %get-tuple-element.774), channel_id=1, source_target_pairs={{0,16},{1,17},{2,18},{3,19},{4,20},{5,21},{6,22},{7,23},{8,24},{9,... | collective-permute-start | bytes 1081352 | tf_op jit(solution)/shard_map/cond/branch_1_fun/ppermute | solution.py:717
  (113 other events, 2055.0 us)
Sparse Core Ops, SparseCore 0:
  201.3 132.0 all-gather.4
  447.3 111.8 reduce-scatter.26
  562.1 88.0 reduce-scatter.28
  748.2 28.7 reduce-scatter.22
  811.9 33.6 reduce-scatter.20
  848.4 25.8 reduce-scatter.24

commit v3 on v2

--- a/solution.py
+++ b/solution.py
@@ -43,7 +43,7 @@
 
 
 def mlp_kernel(
-    cap, counts, live_ref, rows_ref, grad_ref, gateup_hbm, down_hbm,
+    cap, counts, live_ref, rows_ref, grad_ref, gateup_first, gateup_last, down_hbm,
     hidden_ref, gateup_grad_ref, back_ref, gateup_ref, down_ref, gateup_sems, down_sems,
 ):
     step = pl.program_id(0)
@@ -55,9 +55,12 @@
     def span(low, size):
         return pl.ds(low if isinstance(low, int) else pl.multiple_of(low, size), size)
 
-    def gateup_part(k, low, size):
+    def gateup_part(k, low, size, to=None):
         both = span(2 * low, 2 * size)
-        return pltpu.make_async_copy(gateup_hbm.at[:, both], gateup_ref.at[:, both], gateup_sems.at[k])
+        into = both if to is None else span(2 * to, 2 * size)
+        first = gateup_first.shape[1]
+        held = gateup_first.at[:, both] if 2 * low < first else gateup_last.at[:, span(2 * low - first, 2 * size)]
+        return pltpu.make_async_copy(held, gateup_ref.at[:, into], gateup_sems.at[k])
 
     def down_part(k, low, size):
         one = span(low, size)
@@ -73,7 +76,7 @@
         def units_step(k, low, size):
             @pl.when(step == 0)
             def _():
-                gateup_part(k, low, size).wait()
+                gateup_part(k, 0 if size == UNIT_GROUP else low, size, low).wait()
                 down_part(k, low, size).wait()
 
             both, one = span(2 * low, 2 * size), span(low, size)
@@ -111,12 +114,13 @@
             run(count)
 
 
-def mlp_block(rows, grad, live, gateup, down, cap):
+def mlp_block(rows, grad, live, gateup_first, gateup_last, down, cap):
     blocks = rows.shape[0] // cap
     width = rows.shape[1]
     units = down.shape[0]
     if units % 128 or cap % 128:
-        return mlp_plain(rows, grad, gateup, down)
+        return mlp_plain(rows, grad, jnp.concatenate([gateup_first, gateup_last], axis=1), down)
+    gateup_cols = gateup_first.shape[1] + gateup_last.shape[1]
     counts = (192, 256, 320, 384) if cap == 384 else tuple(range(256, cap, 256)) + (cap,)
     groups = len(unit_groups(units))
     low = jnp.bfloat16
@@ -126,10 +130,10 @@
         grid_spec=pltpu.PrefetchScalarGridSpec(
             num_scalar_prefetch=1,
             grid=(blocks,),
-            in_specs=[by_block(width), by_block(width)] + [pl.BlockSpec(memory_space=pl.ANY)] * 2,
+            in_specs=[by_block(width), by_block(width)] + [pl.BlockSpec(memory_space=pl.ANY)] * 3,
             out_specs=(by_block(units), by_block(2 * units), by_block(width)),
             scratch_shapes=[
-                pltpu.VMEM(gateup.shape, low),
+                pltpu.VMEM((width, gateup_cols), low),
                 pltpu.VMEM(down.shape, low),
                 pltpu.SemaphoreType.DMA((groups,)),
                 pltpu.SemaphoreType.DMA((groups,)),
@@ -143,11 +147,11 @@
         compiler_params=pltpu.CompilerParams(vmem_limit_bytes=56 * 1024 * 1024),
         cost_estimate=pl.CostEstimate(
             flops=10 * blocks * cap * width * units,
-            bytes_accessed=2 * (gateup.size + down.size) + 12 * blocks * cap * width,
+            bytes_accessed=2 * (width * gateup_cols + down.size) + 12 * blocks * cap * width,
             transcendentals=blocks * cap * units,
         ),
         name="mlp_block",
-    )(live, rows, grad, gateup, down)
+    )(live, rows, grad, gateup_first, gateup_last, down)
 
 
 def mlp_plain(rows, grad, gateup, down):
@@ -403,6 +407,265 @@
     )(qkv, out, gateup, down, ext)
 
 
+class PlaneScatter:
+    def __init__(self, place, copies, left, right, parts, turned, leaving, came, total, first, second):
+        self.p, self.c, self.left, self.right, self.parts = place, copies, left, right, parts
+        self.turned, self.leaving, self.came, self.total = turned, leaving, came, total
+        self.first, self.second = first, second
+        self.moves = {}
+
+    def turn(self):
+        rows = self.turned.shape[1]
+
+        def one(k, carry):
+            self.turned[k] = self.left[:, pl.ds(pl.multiple_of(k * rows, rows), rows)].T
+            return carry
+
+        lax.fori_loop(0, self.turned.shape[0], one, 0)
+
+    def at(self, part):
+        low, high, _ = self.parts[part]
+        return slice(low, high)
+
+    def begin(self, part):
+        p, cols = self.p, self.at(part)
+        right = self.right[:, cols]
+
+        def terms(into, core):
+            def one(t, carry):
+                term = jnp.dot(self.turned[t * 2 + core], right, preferred_element_type=jnp.float32)
+                into[t, :, cols] = term.astype(jnp.bfloat16)
+                return carry
+
+            lax.fori_loop(0, into.shape[0], one, 0)
+
+        terms(self.leaving, 1 - p.core)
+        self.moves[part, 0] = [self.c.make(self.leaving.at[:, :, cols], self.came.at[:, :, cols], p.sibling)]
+        self.c.go(self.moves[part, 0])
+        terms(self.total, p.core)
+
+    def add(self, t, cols, came):
+        both = self.total[t, :, cols].astype(jnp.float32) + came.astype(jnp.float32)
+        self.total[t, :, cols] = both.astype(jnp.bfloat16)
+
+    def across_first(self, part):
+        p, c, cols = self.p, self.c, self.at(part)
+        c.arrive(self.moves[part, 0])
+
+        def one(t, carry):
+            self.add(t, cols, self.came[t, :, cols])
+            return carry
+
+        lax.fori_loop(0, self.total.shape[0], one, 0)
+        near, to = (p.t_x, p.by_x) if self.parts[part][2] else (p.t_y, p.by_y)
+        self.moves[part, 1] = [
+            c.make(self.total.at[t, :, cols], self.first.at[k, :, cols], to) for k, t in enumerate((near, p.t_d))
+        ]
+        c.go(self.moves[part, 1])
+
+    def across_second(self, part):
+        p, c, cols = self.p, self.c, self.at(part)
+        c.arrive(self.moves[part, 1])
+        near, to = (p.t_y, p.by_y) if self.parts[part][2] else (p.t_x, p.by_x)
+        self.add(near, cols, self.first[1, :, cols])
+        self.moves[part, 2] = [c.make(self.total.at[near, :, cols], self.second.at[:, cols], to)]
+        c.go(self.moves[part, 2])
+        self.add(p.t, cols, self.first[0, :, cols])
+
+    def end(self, part):
+        cols = self.at(part)
+        self.c.arrive(self.moves[part, 2])
+        self.add(self.p.t, cols, self.second[:, cols])
+
+
+class LineScatter:
+    def __init__(self, place, copies, read, cols, up_leaving, up_came, down_leaving, down_came):
+        self.p, self.c, self.read, self.cols = place, copies, read, cols
+        self.ways = ((up_leaving, up_came, place.above), (down_leaving, down_came, place.below))
+        self.rows = up_came.shape[1]
+        self.moves = []
+
+    def block(self, d):
+        at = pl.ds(pl.multiple_of(jnp.clip(d, 0, self.p.n - 1) * self.rows, self.rows), self.rows)
+        return self.read(at, self.cols).astype(jnp.float32)
+
+    def step(self, s):
+        p, c, n, cols = self.p, self.c, self.p.n, self.cols
+        self.take()
+        self.moves = []
+        for way, (leaving, came, to) in enumerate(self.ways):
+            behind = p.z if way == 0 else n - 1 - p.z
+            block = n - s + p.z if way == 0 else p.z - (n - s)
+            sends = (behind <= s - 1) & (behind < n - 1)
+
+            @pl.when(sends & (behind == 0) if s > 1 else sends)
+            def _():
+                leaving[s - 1, :, cols] = self.block(block).astype(jnp.bfloat16)
+
+            if s > 1:
+                @pl.when(sends & (behind > 0))
+                def _():
+                    both = self.block(block) + came[s - 2, :, cols].astype(jnp.float32)
+                    leaving[s - 1, :, cols] = both.astype(jnp.bfloat16)
+
+            move = c.make(leaving.at[s - 1, :, cols], came.at[s - 1, :, cols], to)
+            c.go([move], sends)
+            self.moves.append((move, (behind >= 1) & (behind <= s)))
+
+    def take(self):
+        for move, when in self.moves:
+            self.c.arrive([move], when)
+
+    def end(self, out_ref):
+        p, n, cols = self.p, self.p.n, self.cols
+        self.take()
+        up_came, down_came = self.ways[0][1], self.ways[1][1]
+        own = self.block(p.z)
+
+        @pl.when(p.z == 0)
+        def _():
+            out_ref[:, cols] = own + down_came[n - 2, :, cols].astype(jnp.float32)
+
+        @pl.when(p.z == n - 1)
+        def _():
+            out_ref[:, cols] = own + up_came[n - 2, :, cols].astype(jnp.float32)
+
+        @pl.when((p.z > 0) & (p.z < n - 1))
+        def _():
+            out_ref[:, cols] = own + (
+                up_came[n - 2, :, cols].astype(jnp.float32) + down_came[n - 2, :, cols].astype(jnp.float32)
+            )
+
+
+def plane_parts(cols, count):
+    edges = [cols // 128 * k // count * 128 for k in range(count + 1)]
+    return [(low, high, k % 2 == 0) for k, (low, high) in enumerate(zip(edges[:-1], edges[1:]))]
+
+
+def plane_scratch(rows, width, cols, planes):
+    low = jnp.bfloat16
+    line = width // planes // 2
+    return [
+        pltpu.VMEM((planes * 2, line, rows), low),
+        pltpu.VMEM((planes, line, cols), low),
+        pltpu.VMEM((planes, line, cols), low),
+        pltpu.VMEM((planes, line, cols), low),
+        pltpu.VMEM((2, line, cols), low),
+        pltpu.VMEM((line, cols), low),
+    ]
+
+
+def qkv_back_kernel(
+    n, parts, normed_ref, grad_ref, weights_hbm, pieces_ref, out_sum, sum_ref, back_ref, gateup_ref, out_ref, weights,
+    traded, turned, leaving, came, total, first, second, up_leaving, up_came, down_leaving, down_came, out_up_leaving,
+    out_up_came, out_down_leaving, out_down_came, send_sems, recv_sems, load_sem,
+):
+    p = Place(n)
+    c = Copies(send_sems, recv_sems)
+    held = weights.shape[0]
+
+    def load(k):
+        return pltpu.make_async_copy(weights_hbm.at[k * held : (k + 1) * held], weights, load_sem)
+
+    load(0).start()
+    p.greet([p.by_x, p.by_y, p.by_d, p.sibling])
+    trade = [
+        c.make(pieces_ref.at[k], traded.at[p.t], to) for k, to in ((p.t_x, p.by_x), (p.t_y, p.by_y), (p.t_d, p.by_d))
+    ]
+    c.go(trade)
+    traded[p.t] = pieces_ref[p.t]
+    out_line = LineScatter(
+        p, c, lambda at, cols: out_sum[at, cols], slice(None), out_up_leaving, out_up_came, out_down_leaving, out_down_came
+    )
+    out_line.step(1)
+    scatter = PlaneScatter(p, c, normed_ref, grad_ref, parts, turned, leaving, came, total, first, second)
+    every = range(len(parts))
+    scatter.turn()
+    for k in every:
+        scatter.begin(k)
+    chunk = 2 * HEAD_DIM
+
+    def back(half):
+        load(half).wait()
+
+        def one(k, carry):
+            at = pl.ds(pl.multiple_of(k * chunk, chunk), chunk)
+            to = pl.ds(pl.multiple_of(half * held + k * chunk, chunk), chunk)
+            back_ref[:, to] = dot_nt(grad_ref[...], weights[at, :])
+            return carry
+
+        lax.fori_loop(0, held // chunk, one, 0)
+
+    for k in every:
+        scatter.across_first(k)
+    if n > 2:
+        out_line.step(2)
+    back(0)
+    load(1).start()
+    c.arrive(trade)
+    units = traded.shape[2] // 2
+    for k in range(traded.shape[0]):
+        for low, high in unit_groups(units):
+            for at, start in ((2 * low, k * units), (low + high, gateup_ref.shape[1] // 2 + k * units)):
+                columns = traded[k, :, at : at + high - low]
+                gateup_ref[:, start + low : start + high] = columns.astype(jnp.float32)
+    for s in range(3, n):
+        out_line.step(s)
+    for k in every:
+        scatter.across_second(k)
+    back(1)
+    lines = [
+        LineScatter(
+            p, c, lambda at, cols: total[p.t, at, cols], scatter.at(k), up_leaving, up_came, down_leaving, down_came
+        )
+        for k in every
+    ]
+    for k in every:
+        scatter.end(k)
+        lines[k].step(1)
+    for s in range(2, n):
+        for line in lines:
+            line.step(s)
+    out_line.end(out_ref)
+    for line in lines:
+        line.end(sum_ref)
+    c.end()
+
+
+def qkv_back(normed, grad, weights, pieces, out_sum, planes, n, collective_id):
+    rows, width = normed.shape
+    cols = grad.shape[1]
+    parts = plane_parts(cols, 4)
+    in_vmem = pl.BlockSpec(memory_space=pltpu.VMEM)
+    low = jnp.bfloat16
+    line = pltpu.VMEM((n - 1, width // planes // 2 // n, cols), low)
+    out_line = pltpu.VMEM((n - 1, out_sum.shape[0] // n, out_sum.shape[1]), low)
+    copies = len(parts) * (4 + 2 * n) + 2 * n + 4
+    return pl.pallas_call(
+        functools.partial(qkv_back_kernel, n, parts),
+        in_specs=[in_vmem, in_vmem, pl.BlockSpec(memory_space=pl.ANY), in_vmem, in_vmem],
+        out_specs=(in_vmem,) * 4,
+        out_shape=(
+            jax.ShapeDtypeStruct((width // planes // 2 // n, cols), jnp.float32),
+            jax.ShapeDtypeStruct((rows, width), jnp.float32),
+            jax.ShapeDtypeStruct((pieces.shape[1], planes * pieces.shape[2]), jnp.float32),
+            jax.ShapeDtypeStruct((out_sum.shape[0] // n, out_sum.shape[1]), jnp.float32),
+        ),
+        scratch_shapes=[pltpu.VMEM((weights.shape[0] // 2, cols), low), pltpu.VMEM(pieces.shape, low)]
+        + plane_scratch(rows, width, cols, planes)
+        + [line] * 4
+        + [out_line] * 4
+        + [pltpu.SemaphoreType.DMA((copies,)), pltpu.SemaphoreType.DMA((copies,)), pltpu.SemaphoreType.DMA],
+        compiler_params=pltpu.CompilerParams(
+            vmem_limit_bytes=60 * 1024 * 1024, collective_id=collective_id, has_side_effects=True
+        ),
+        cost_estimate=pl.CostEstimate(
+            flops=48 * rows * width * cols, bytes_accessed=2 * weights.size + 8 * rows * width, transcendentals=0
+        ),
+        name="qkv_back",
+    )(normed, grad, weights, pieces, out_sum)
+
+
 def fill_bias(r, key_code, query_code, query_base, bias):
     rows = bias.shape[0]
     code = key_code[r * rows : (r + 1) * rows, :]
@@ -444,29 +707,69 @@
 
 
 def attend_kernel(n, with_out, *refs):
-    q_ref, kv_ref, key_code, query_code, query_base = refs[:5]
-    o_ref, total_ref, kv_all = refs[5 + with_out : 8 + with_out]
-    out_all = refs[8 + with_out] if with_out else None
-    peak_now, total_now, mixed_now, bias, send_sems, recv_sems = refs[-6:]
+    inputs_ref, gain_ref, cosine, sine, weights_hbm, key_code, query_code, query_base = refs[:8]
+    refs = refs[8:]
+    if with_out:
+        (own_grad, _), refs = refs[:2], refs[2:]
+    (normed_ref, inverse_ref, q_ref, o_ref, total_ref, kv_all), refs = refs[:6], refs[6:]
+    if with_out:
+        (out_all, grad_x, grad_y, grad_d), refs = refs[:4], refs[4:]
+    weights, peak_now, total_now, mixed_now, bias, send_sems, recv_sems, load_sems = refs
     p = Place(n)
     c = Copies(send_sems, recv_sems)
     z = p.z
-    rows = q_ref.shape[0]
+    rows, width = q_ref.shape
     values_at = KV_HEADS * HEAD_DIM
+    pair = 2 * HEAD_DIM
     slot = lambda r: kv_all.at[r * rows : (r + 1) * rows, :]
+    loads = [
+        pltpu.make_async_copy(weights_hbm.at[:, cols], weights.at[:, cols], load_sems.at[k])
+        for k, cols in enumerate((slice(width, weights.shape[1]), slice(0, width)))
+    ]
+    for load in loads:
+        load.start()
     p.greet([p.by_x, p.by_y, p.sibling] if with_out else [])
-    copies = [c.make(kv_ref if r == 0 else slot(r), slot(r + 1), p.above) for r in range(n - 1)]
+    if with_out:
+        half = rows // 2
+        near = [c.make(own_grad, grad_x, p.by_x), c.make(own_grad, grad_y, p.by_y)]
+        out_plane = PlaneGather(p, c, out_all)
+        out_plane.begin()
+        c.go(near)
+    inputs = inputs_ref[...]
+    inverse = lax.rsqrt(jnp.mean(inputs * inputs, axis=1, keepdims=True) + EPSILON)
+    inverse_ref[...] = inverse
+    normed_ref[...] = (inputs * inverse * gain_ref[...]).astype(jnp.bfloat16)
+
+    def project(low, into, to, turned):
+        at = pl.ds(pl.multiple_of(low, pair), pair)
+        both = jnp.dot(normed_ref[...], weights[:, at], preferred_element_type=jnp.float32)
+        for k in range(2):
+            head = both[:, k * HEAD_DIM : (k + 1) * HEAD_DIM]
+            if turned:
+                head = head * cosine[...] + pltpu.roll(head, HEAD_DIM // 2, 1) * sine[...]
+            lanes = pl.ds(pl.multiple_of(to + k * HEAD_DIM, HEAD_DIM), HEAD_DIM)
+            into[:rows, lanes] = head.astype(jnp.bfloat16)
+
+    def project_all(start, count, into, to, turned):
+        def one(k, carry):
+            project(start + k * pair, into, to + k * pair, turned)
+            return carry
+
+        lax.fori_loop(0, count // pair, one, 0)
+
+    loads[0].wait()
+    project_all(width, values_at, kv_all, 0, True)
+    project_all(width + values_at, values_at, kv_all, values_at, False)
+    copies = [c.make(slot(r), slot(r + 1), p.above) for r in range(n - 1)]
     if copies:
         c.go([copies[0]], z < n - 1)
-    if with_out:
-        out_plane = PlaneGather(p, c, out_all)
-        out_plane.begin()
-
-    kv_all[:rows, :] = kv_ref[...]
     for r in range(1, n):
         @pl.when(z < r)
         def _(r=r):
             kv_all[r * rows : (r + 1) * rows, :] = jnp.zeros((rows, kv_all.shape[1]), kv_all.dtype)
+
+    loads[1].wait()
+    project_all(0, width, q_ref, 0, True)
 
     def block(r):
         fill_bias(r, key_code, query_code, query_base, bias)
@@ -504,6 +807,13 @@
             c.go([copies[r]], (z >= r) & (z < n - 1))
         if with_out and r == 1:
             out_plane.middle()
+        if with_out and r == max(n - 2, 1):
+            c.arrive(near)
+            corners = [
+                c.make(grad_y.at[:half], grad_d.at[:half], p.by_x),
+                c.make(grad_x.at[half:], grad_d.at[half:], p.by_y),
+            ]
+            c.go(corners)
         if with_out and r == n - 1:
             out_plane.end()
 
@@ -520,56 +830,83 @@
         return carry
 
     lax.fori_loop(0, KV_HEADS, finish, 0)
+    if with_out:
+        c.arrive(corners)
     c.end()
 
 
-def attend(query, kv, key_code, query_code, query_base, n, collective_id, out_all=None):
-    rows, width = query.shape
+def attend(
+    inputs, gain, cosine, sine, weights, key_code, query_code, query_base, n, collective_id, down_grad=None, out_all=None
+):
+    rows, width = inputs.shape
+    kv_cols = weights.shape[1] - width
+    low = jnp.bfloat16
     in_vmem = pl.BlockSpec(memory_space=pltpu.VMEM)
     any_spec = pl.BlockSpec(memory_space=pl.ANY)
-    outs = [] if out_all is None else [out_all]
-    copies = n + 16
+    given = [] if out_all is None else [down_grad, out_all]
+    more = [] if out_all is None else [out_all] + [down_grad] * 3
+    copies = n + 24
     return pl.pallas_call(
-        functools.partial(attend_kernel, n, len(outs)),
-        in_specs=[in_vmem] * 5 + [any_spec] * len(outs),
-        out_specs=(in_vmem,) * 3 + (any_spec,) * len(outs),
-        input_output_aliases={5: 3} if outs else {},
+        functools.partial(attend_kernel, n, out_all is not None),
+        in_specs=[in_vmem] * 4 + [any_spec] + [in_vmem] * 3 + [any_spec] * len(given),
+        out_specs=(in_vmem,) * 6 + (any_spec,) * len(more),
+        input_output_aliases={9: 6} if given else {},
         out_shape=(
-            jax.ShapeDtypeStruct((rows, width), jnp.bfloat16),
+            jax.ShapeDtypeStruct((rows, width), low),
+            jax.ShapeDtypeStruct((rows, 1), jnp.float32),
+            jax.ShapeDtypeStruct((rows, width), low),
+            jax.ShapeDtypeStruct((rows, width), low),
             jax.ShapeDtypeStruct((KV_HEADS, GROUP, rows), jnp.float32),
-            jax.ShapeDtypeStruct((n * rows, kv.shape[1]), jnp.bfloat16),
+            jax.ShapeDtypeStruct((n * rows, kv_cols), low),
         )
-        + tuple(jax.ShapeDtypeStruct(o.shape, o.dtype) for o in outs),
+        + tuple(jax.ShapeDtypeStruct(o.shape, o.dtype) for o in more),
         scratch_shapes=[
+            pltpu.VMEM(weights.shape, low),
             pltpu.VMEM((KV_HEADS, GROUP, rows), jnp.float32),
             pltpu.VMEM((KV_HEADS, GROUP, rows), jnp.float32),
             pltpu.VMEM((KV_HEADS, GROUP, HEAD_DIM, rows), jnp.float32),
             pltpu.VMEM((rows, rows), jnp.float32),
             pltpu.SemaphoreType.DMA((copies,)),
             pltpu.SemaphoreType.DMA((copies,)),
+            pltpu.SemaphoreType.DMA((2,)),
         ],
         compiler_params=pltpu.CompilerParams(
-            vmem_limit_bytes=48 * 1024 * 1024, collective_id=collective_id, has_side_effects=True
+            vmem_limit_bytes=52 * 1024 * 1024, collective_id=collective_id, has_side_effects=True
         ),
         cost_estimate=pl.CostEstimate(
-            flops=4 * rows * n * rows * width, bytes_accessed=8 * rows * width, transcendentals=HEADS * rows * n * rows
+            flops=64 * rows * n * rows * width, bytes_accessed=8 * rows * width, transcendentals=HEADS * rows * n * rows
         ),
         name="attend",
-    )(query, kv, key_code, query_code, query_base, *outs)
-
-
-def attend_back_kernel(
-    n, q_ref, kv_all, do_ref, total_ref, inner_ref, key_code, query_code, query_base, dq_ref, dkv_ref,
-    dq_now, dkv_now, bias, leaving, came, send_sems, recv_sems,
-):
+    )(inputs, gain, cosine, sine, weights, key_code, query_code, query_base, *given)
+
+
+def attend_back_kernel(n, parts, *refs):
+    q_ref, kv_all, do_ref, total_ref, mixed_ref, key_code, query_code, query_base, cosine, sine = refs[:10]
+    refs = refs[10:]
+    if parts:
+        branch_ref, refs = refs[0], refs[1:]
+    grad_ref, refs = refs[0], refs[1:]
+    if parts:
+        out_sum, refs = refs[0], refs[1:]
+    dq_now, dkv_now, bias, inner_now, leaving, came, send_sems, recv_sems = refs[:8]
     p = Place(n)
     c = Copies(send_sems, recv_sems)
     z = p.z
     rows = q_ref.shape[0]
     values_at = KV_HEADS * HEAD_DIM
-    p.greet([])
+    p.greet([p.by_x, p.by_y, p.sibling] if parts else [])
+    every = range(len(parts))
+    if parts:
+        scatter = PlaneScatter(p, c, mixed_ref, branch_ref, parts, *refs[8:])
     copies = {r: c.make(leaving.at[r - 1], came.at[r - 1], p.below) for r in range(1, n)}
     dq_now[...] = jnp.zeros_like(dq_now)
+    q_cols = HEADS * HEAD_DIM
+
+    def turned_back(head):
+        return head * cosine[...] - pltpu.roll(head, HEAD_DIM // 2, 1) * sine[...]
+
+    def put(low, head):
+        grad_ref[:, low : low + HEAD_DIM] = head.astype(jnp.bfloat16)
 
     def block(r):
         fill_bias(r, key_code, query_code, query_base, bias)
@@ -586,7 +923,7 @@
                 scores = dot_nt(keys, query) * (SCORE_SCALE * LOG2_E) + hidden
                 weights = jnp.exp2(scores - total_ref[g, h : h + 1, :])
                 grad_weights = dot_nt(values, grad)
-                grad_scores = (weights * (grad_weights - inner_ref[g, h : h + 1, :])).astype(jnp.bfloat16)
+                grad_scores = (weights * (grad_weights - inner_now[g, h : h + 1, :])).astype(jnp.bfloat16)
                 dv_term = jnp.dot(weights.astype(jnp.bfloat16), grad, preferred_element_type=jnp.float32)
                 dk_term = jnp.dot(grad_scores, query, preferred_element_type=jnp.float32)
                 dv = dv_term if dv is None else dv + dv_term
@@ -598,6 +935,14 @@
 
         lax.fori_loop(0, KV_HEADS, group, 0)
 
+    def inner_of(g, carry):
+        for h in range(GROUP):
+            lanes = pl.ds(pl.multiple_of((g * GROUP + h) * HEAD_DIM, HEAD_DIM), HEAD_DIM)
+            both = do_ref[:, lanes].astype(jnp.float32) * mixed_ref[:, lanes].astype(jnp.float32)
+            inner_now[g, h : h + 1, :] = jnp.sum(both.T, axis=0, keepdims=True)
+        return carry
+
+    lax.fori_loop(0, KV_HEADS, inner_of, 0)
     for r in range(n - 1, -1, -1):
         @pl.when(z >= r)
         def _(r=r):
@@ -611,12 +956,29 @@
                 leaving[r - 1] = dkv_now[...].astype(jnp.bfloat16)
                 copies[r].start()
             else:
-                dkv_ref[...] = dkv_now[...]
+                for g in range(KV_HEADS):
+                    put(q_cols + g * HEAD_DIM, turned_back(dkv_now[:, g * HEAD_DIM : (g + 1) * HEAD_DIM]))
+                grad_ref[:, q_cols + values_at :] = dkv_now[:, values_at:].astype(jnp.bfloat16)
+
+        if parts and r == n - 1:
+            scatter.turn()
+            for k in every:
+                scatter.begin(k)
+        if parts and r == max(n - 2, 0):
+            for k in every:
+                scatter.across_first(k)
+        if parts and r == max(n - 3, 0):
+            for k in every:
+                scatter.across_second(k)
+    if parts:
+        for k in every:
+            scatter.end(k)
+        out_sum[...] = scatter.total[p.t]
 
     def finish(g, carry):
         for h in range(GROUP):
             lanes = pl.ds(pl.multiple_of((g * GROUP + h) * HEAD_DIM, HEAD_DIM), HEAD_DIM)
-            dq_ref[:, lanes] = dq_now[g, h].T * SCORE_SCALE
+            grad_ref[:, lanes] = turned_back(dq_now[g, h].T * SCORE_SCALE).astype(jnp.bfloat16)
         return carry
 
     lax.fori_loop(0, KV_HEADS, finish, 0)
@@ -624,57 +986,54 @@
         @pl.when(z >= r)
         def _(r=r):
             copies[r].wait_send()
-
-
-def attend_back(query, kv_all, grad, total, inner, key_code, query_code, query_base, n, collective_id):
+    c.end()
+
+
+def attend_back(
+    query, kv_all, grad, total, mixed, key_code, query_code, query_base, cosine, sine, n, collective_id, branch_grad=None,
+    planes=0,
+):
     rows, width = query.shape
     kv_cols = kv_all.shape[1]
     in_vmem = pl.BlockSpec(memory_space=pltpu.VMEM)
     slots = max(n - 1, 1)
+    more, parts, shapes, scratch = (), [], (), []
+    if branch_grad is not None:
+        more, parts = (branch_grad,), plane_parts(width, 2)
+        shapes = (jax.ShapeDtypeStruct((width // planes // 2, width), jnp.bfloat16),)
+        scratch = plane_scratch(rows, width, width, planes)
+    copies = n + 4 * len(parts)
     return pl.pallas_call(
-        functools.partial(attend_back_kernel, n),
-        in_specs=[in_vmem] * 8,
-        out_specs=(in_vmem,) * 2,
-        out_shape=(
-            jax.ShapeDtypeStruct((rows, width), jnp.float32),
-            jax.ShapeDtypeStruct((rows, kv_cols), jnp.float32),
-        ),
+        functools.partial(attend_back_kernel, n, parts),
+        in_specs=[in_vmem] * (10 + len(more)),
+        out_specs=(in_vmem,) * (1 + len(shapes)),
+        out_shape=(jax.ShapeDtypeStruct((rows, width + kv_cols), jnp.bfloat16),) + shapes,
         scratch_shapes=[
             pltpu.VMEM((KV_HEADS, GROUP, HEAD_DIM, rows), jnp.float32),
             pltpu.VMEM((rows, kv_cols), jnp.float32),
             pltpu.VMEM((rows, rows), jnp.float32),
+            pltpu.VMEM((KV_HEADS, GROUP, rows), jnp.float32),
             pltpu.VMEM((slots, rows, kv_cols), jnp.bfloat16),
             pltpu.VMEM((slots, rows, kv_cols), jnp.bfloat16),
-            pltpu.SemaphoreType.DMA((n,)),
-            pltpu.SemaphoreType.DMA((n,)),
-        ],
+            pltpu.SemaphoreType.DMA((copies,)),
+            pltpu.SemaphoreType.DMA((copies,)),
+        ]
+        + scratch,
         compiler_params=pltpu.CompilerParams(
-            vmem_limit_bytes=56 * 1024 * 1024, collective_id=collective_id, has_side_effects=True
+            vmem_limit_bytes=60 * 1024 * 1024, collective_id=collective_id, has_side_effects=True
         ),
         cost_estimate=pl.CostEstimate(
-            flops=10 * rows * n * rows * width, bytes_accessed=16 * rows * width, transcendentals=HEADS * rows * n * rows
+            flops=72 * rows * n * rows * width, bytes_accessed=16 * rows * width, transcendentals=HEADS * rows * n * rows
         ),
         name="attend_back",
-    )(query, kv_all, grad, total, inner, key_code, query_code, query_base)
+    )(query, kv_all, grad, total, mixed, key_code, query_code, query_base, cosine, sine, *more)
 
 
 def rotary_tables(positions):
     half_dim = HEAD_DIM // 2
     frequency = jnp.power(10000.0, -2.0 * jnp.arange(half_dim, dtype=jnp.float32) / HEAD_DIM)
     angles = positions[:, None] * frequency[None, :]
-    return (jnp.cos(angles)[:, None, :], jnp.sin(angles)[:, None, :])
-
-
-def rotate_heads(values, cosine_table, sine_table):
-    half_dim = HEAD_DIM // 2
-    cosine, sine = cosine_table[:, 0], sine_table[:, 0]
-    cosine = jnp.concatenate([cosine, cosine], axis=1)
-    sine = jnp.concatenate([-sine, sine], axis=1)
-    done = []
-    for start in range(0, values.shape[1], HEAD_DIM):
-        head = values[:, start : start + HEAD_DIM]
-        done.append(head * cosine + jnp.roll(head, half_dim, axis=1) * sine)
-    return jnp.concatenate(done, axis=1)
+    return (jnp.cos(angles), jnp.sin(angles))
 
 
 def norm_forward(values_in, gain_row):
@@ -762,24 +1121,33 @@
         corner = [self.swap(by_y[:half], 2), self.swap(by_x[half:], 4)]
         return [rows, by_x, by_y, jnp.concatenate(corner)]
 
-    def scatter_tokens(self, blocks):
+    def scatter_far(self, blocks):
         if self.planes != 4:
-            every = jnp.concatenate([b.astype(jnp.bfloat16) for b in blocks])
-            total = lax.psum_scatter(
-                every, MESH_AXES, scatter_dimension=0, tiled=True, axis_index_groups=self.same_plane
-            )
-            return total.astype(jnp.float32)
+            return jnp.concatenate([b.astype(jnp.bfloat16) for b in blocks]), None, None
         own, by_x, by_y, corner = blocks
         half = own.shape[0] // 2
         top = self.swap(corner[:half], 2).astype(jnp.float32)
         bottom = self.swap(corner[half:], 4).astype(jnp.float32)
         by_y = jnp.concatenate([by_y[:half] + top, by_y[half:]]).astype(jnp.bfloat16)
         by_x = jnp.concatenate([by_x[:half], by_x[half:] + bottom]).astype(jnp.bfloat16)
-        return (
-            own.astype(jnp.float32)
-            + self.swap(by_x, 2).astype(jnp.float32)
-            + self.swap(by_y, 4).astype(jnp.float32)
-        )
+        return own, by_x, by_y
+
+    def scatter_near(self, own, by_x, by_y):
+        if self.planes != 4:
+            total = lax.psum_scatter(
+                own, MESH_AXES, scatter_dimension=0, tiled=True, axis_index_groups=self.same_plane
+            )
+            return total, None, None
+        return own, self.swap(by_x, 2), self.swap(by_y, 4)
+
+    def scatter_sum(self, own, came_x, came_y):
+        if came_x is None:
+            return own.astype(jnp.float32)
+        return own.astype(jnp.float32) + came_x.astype(jnp.float32) + came_y.astype(jnp.float32)
+
+    def gather_chip(self, pieces):
+        every = lax.all_gather(pieces, MESH_AXES, axis=1, tiled=True, axis_index_groups=self.same_chip)
+        return every.reshape(-1, every.shape[-1])
 
     def plane_counts(self, counts, cap):
         if self.planes != 4:
@@ -893,6 +1261,9 @@
     low = jnp.bfloat16
 
 
+    first_cols = 2 * UNIT_GROUP * max(ff_part // UNIT_GROUP * 2 // 5, 1)
+    gateup_first = links.gather_chip(pieces[:, :, :first_cols])
+
     def codes_of(block):
         mask = lax.dynamic_slice_in_dim(active, jnp.maximum(block, 0) * span_len, span_len, 1)
         chosen, live = pick_live(mask, cap)
@@ -916,27 +1287,24 @@
     inputs = dot32(picker, tokens.reshape(row_count, width))
     down_grad = dot_low(picker, cotangent.reshape(row_count, width))
     upstream = down_grad.astype(jnp.float32)
-    down_grad_blocks = links.gather_tokens(down_grad)
-
-    normed, inverse_one = norm_forward(inputs, gain_full[0])
-    normed_low = normed.astype(low)
-    kv_part = dot32(normed_low, qkv_low[:, width:])
-    kv_low = jnp.concatenate(
-        [rotate_heads(kv_part[:, :kv_width], cosine_table, sine_table), kv_part[:, kv_width:]], axis=1
-    ).astype(low)
-    query_low = rotate_heads(dot32(normed_low, qkv_low[:, :width]), cosine_table, sine_table).astype(low)
+
+    cosine = jnp.concatenate([cosine_table, cosine_table], axis=1)
+    sine = jnp.concatenate([-sine_table, sine_table], axis=1)
     ids = 1 if cap < row_count else 3
     codes = (key_code, query_code, query_base)
+    first = (inputs, gain_full[:1], cosine, sine, qkv_low, *codes, n, ids)
     if out_all.ndim == 2:
         out_low = out_all
-        attended_low, totals, kv_all = attend(query_low, kv_low, *codes, n, ids)
+        normed_low, inverse_one, query_low, attended_low, totals, kv_all = attend(*first)
+        down_grad_blocks = links.gather_tokens(down_grad)
     else:
-        attended_low, totals, kv_all, out_all = attend(query_low, kv_low, *codes, n, ids, out_all)
+        normed_low, inverse_one, query_low, attended_low, totals, kv_all, out_all, *others = attend(
+            *first, down_grad, out_all
+        )
+        down_grad_blocks = [down_grad, *others]
         out_low = out_all.reshape(width, width)
-    pieces, attended_low = lax.optimization_barrier((pieces, attended_low))
-    gateup_low = lax.all_gather(
-        pieces, MESH_AXES, axis=1, tiled=True, axis_index_groups=links.same_chip
-    ).reshape(width, 2 * ff_part)
+    pieces_last, attended_low = lax.optimization_barrier((pieces[:, :, first_cols:], attended_low))
+    gateup_last = links.gather_chip(pieces_last)
     middle = inputs + live_rows * dot32(attended_low, out_low)
     normed_mid, inverse_two = norm_forward(middle, gain_full[1])
     blocks = links.gather_tokens(normed_mid.astype(low))
@@ -950,53 +1318,56 @@
         grads = together([down_grad_blocks[k] for k in part])
         row_parts.append(rows)
         grad_parts.append(grads)
-        hidden, gateup_grad, back = mlp_block(rows, grads, lives[jnp.array(part)], gateup_low, down_low, cap)
+        hidden, gateup_grad, back = mlp_block(
+            rows, grads, lives[jnp.array(part)], gateup_first, gateup_last, down_low, cap
+        )
         hidden_blocks.append(hidden)
         gateup_grad_blocks.append(gateup_grad)
         for i, k in enumerate(part):
             mid_terms[k] = back[i * cap : (i + 1) * cap]
-    grad_normed_mid = links.scatter_tokens(mid_terms)
-    hidden_all = jnp.concatenate(hidden_blocks)
-
-    term_down = dot_low(hidden_all.T, jnp.concatenate(grad_parts))
-    term_gateup = dot_low(jnp.concatenate(row_parts).T, jnp.concatenate(gateup_grad_blocks))
+    mid_far = links.scatter_far(mid_terms)
+    hidden_all, rows_all = jnp.concatenate(hidden_blocks), jnp.concatenate(row_parts)
+    grads_all, gateup_grad_all = jnp.concatenate(grad_parts), jnp.concatenate(gateup_grad_blocks)
+    mid_far, hidden_all, gateup_grad_all = lax.optimization_barrier((mid_far, hidden_all, gateup_grad_all))
+    mid_near = links.scatter_near(*mid_far)
+    term_down = dot_low(hidden_all.T, grads_all)
     down_half = links.scatter_core(term_down.reshape(1, 2, ff_part // 2, width))[0]
+    grad_down = lax.psum_scatter(down_half, "narrow", scatter_dimension=0, tiled=True)
+    term_gateup = dot_low(rows_all.T, gateup_grad_all)
     gateup_half = links.scatter_core(term_gateup.reshape(planes, 2, n * shard_rows, 2 * ff_part))
-    grad_down = lax.psum_scatter(down_half, "narrow", scatter_dimension=0, tiled=True)
+    gateup_half, grad_down = lax.optimization_barrier((gateup_half, grad_down))
     grad_pieces = lax.psum_scatter(gateup_half, "narrow", scatter_dimension=1, tiled=True)
     down_terms = dot_low(hidden_all, down_low)
+    down_terms, mid_near = lax.optimization_barrier((down_terms, mid_near))
+    grad_normed_mid = links.scatter_sum(*mid_near)
     order = [k for part in parts for k in part]
     down_terms = {k: down_terms[i * cap : (i + 1) * cap] for i, k in enumerate(order)}
-    down_proj = links.scatter_tokens([down_terms[k] for k in range(planes)])
-    layer_out = (middle + down_proj).astype(low)
+    down_far = links.scatter_far([down_terms[k] for k in range(planes)])
 
     grad_middle = upstream + norm_backward(middle, inverse_two, gain_full[1], grad_normed_mid)
     branch_grad_low = grad_middle.astype(low)
-    branch_grad_low, down_half, gateup_half = lax.optimization_barrier(
-        (branch_grad_low, down_half, gateup_half)
-    )
+    branch_grad_low, gateup_half = lax.optimization_barrier((branch_grad_low, gateup_half))
     grad_attended_low = dot_low(branch_grad_low, out_low.T)
-    grad_out = links.scatter_rows(dot_low(attended_low.T, branch_grad_low))
-    inner = jnp.sum(
-        (grad_attended_low.astype(jnp.float32) * attended_low.astype(jnp.float32)).reshape(
-            cap, HEADS, HEAD_DIM
-        ),
-        axis=-1,
-    )
-    inner = inner.T.reshape(KV_HEADS, GROUP, cap)
-    grad_query, grad_kv = attend_back(
-        query_low, kv_all, grad_attended_low, totals, inner, *codes, n, ids + 1
-    )
-    grad_query_low = rotate_heads(grad_query, cosine_table, -sine_table).astype(low)
-    grad_q_rows = links.scatter_rows(dot_low(normed_low.T, grad_query_low))
-    grad_kv_low = jnp.concatenate(
-        [rotate_heads(grad_kv[:, :kv_width], cosine_table, -sine_table), grad_kv[:, kv_width:]], axis=1
-    ).astype(low)
-    grad_kv_rows = links.scatter_rows(dot_low(normed_low.T, grad_kv_low))
-    grad_normed = dot32(grad_query_low, qkv_low[:, :width].T) + dot32(grad_kv_low, qkv_low[:, width:].T)
+    grad_attended_low, down_far = lax.optimization_barrier((grad_attended_low, down_far))
+    down_near = links.scatter_near(*down_far)
+    back = (query_low, kv_all, grad_attended_low, totals, attended_low, *codes, cosine, sine, n, ids + 1)
+    if planes == 4 and n > 1:
+        grad_projected_low, out_sum = attend_back(*back, branch_grad_low, planes)
+        down_near, grad_projected_low = lax.optimization_barrier((down_near, grad_projected_low))
+        grad_qkv, grad_normed, grad_gateup, grad_out = qkv_back(
+            normed_low, grad_projected_low, qkv_low, grad_pieces, out_sum, planes, n, ids + 4
+        )
+    else:
+        grad_projected_low = attend_back(*back)[0]
+        grad_out = links.scatter_rows(dot_low(attended_low.T, branch_grad_low))
+        grad_qkv = links.scatter_rows(dot_low(normed_low.T, grad_projected_low)).astype(jnp.float32)
+        grad_normed = dot32(grad_projected_low, qkv_low.T)
+        grad_gateup = join_columns(links.trade_columns(grad_pieces)).astype(jnp.float32)
     grad_tokens = (
         grad_middle + norm_backward(inputs, inverse_one, gain_full[0], grad_normed)
     ).astype(low)
+
+    layer_out = (middle + links.scatter_sum(*down_near)).astype(low)
 
     def spread(packed, skipped):
         back = lax.dot_general(
@@ -1006,8 +1377,6 @@
         return jnp.where(mask[:, :, None] == 1, back.reshape(skipped.shape), skipped)
 
     layer_out, grad_tokens = spread(layer_out, tokens), spread(grad_tokens, cotangent)
-    grad_gateup = join_columns(links.trade_columns(grad_pieces))
-    grad_qkv = jnp.concatenate([grad_q_rows, grad_kv_rows], axis=1)
     return layer_out, grad_tokens, grad_qkv, grad_out, grad_gateup, grad_down
 
 

time: 964 us -> 834 us (0.87)
  Pallas kernels: 307 us -> 469 us
  waiting for transfers between devices: 230 us -> 77 us
  local copies, waits for them, and re-layouts: 123 us -> 53.1 us
  matrix products: 112 us -> 77.5 us
  other arithmetic: 112 us -> 96.5 us
  starting transfers between devices: 36.6 us -> 21.6 us
    pallas_call x2 -> x3, Pallas kernels: 144 us -> 305 us  [the longest x1 110 us: attend_back(): pl.pallas_call(functools.partial(attend_back_kernel, n, parts), in_specs=...]
    ppermute x36 -> x14, waiting for transfers between devices: 190 us -> 66.9 us  [swap(): return lax.ppermute(values, MESH_AXES, pairs)]
    another operation x202 -> x0, local copies, waits for them, and re-layouts: 73.3 us -> none
    reduce_scatter x3 -> x0, waiting for transfers between devices: 28.2 us -> none  [scatter_rows(): return lax.psum_scatter(total, 'narrow', scatter_dimension=0, tiled=True)]
    dot_general x6 -> x2, matrix products: 32.1 us -> 11 us  [dot32(): return jnp.dot(a, b, preferred_element_type=jnp.float32)]
    cond x0 -> x100, local copies, waits for them, and re-layouts: none -> 16.2 us
    concatenate x7 -> x8, other arithmetic: 8.09 us -> 24 us  [the longest x1 13.6 us: layer(): jnp.concatenate(gateup_grad_blocks)]
    ppermute x36 -> x14, starting transfers between devices: 36.1 us -> 21.5 us  [swap(): return lax.ppermute(values, MESH_AXES, pairs)]
  transfers between devices with their start and end apart: 42 -> 18, of which waited for: 19 -> 9; matrix products, arithmetic and copies ran while one was open for 21% -> 19% of each run, Pallas kernels for 10% -> 31%
where the time goes in v3:
time: 834 us; the launch traced here: 822 us
  Pallas kernels  469 us (56%)
  other arithmetic  96.5 us (12%)
  matrix products  77.5 us (9%)
  waiting for transfers between devices  77 us (9%)
  local copies, waits for them, and re-layouts  53.1 us (6%)
  starting transfers between devices  21.6 us (3%)
  between operations  17.7 us (2%)
  loops' own time  9.44 us (1%)
    pallas_call x1, Pallas kernels, attend_back(): pl.pallas_call(functools.partial(attend_back_kernel, n, parts), in_specs=...  110 us
    pallas_call x1, Pallas kernels, qkv_back(): pl.pallas_call(functools.partial(qkv_back_kernel, n, parts), in_specs=[in...  102 us
    pallas_call x1, Pallas kernels, gather_first(): pl.pallas_call(functools.partial(gather_kernel, n), out_shape=(jax.ShapeD...  98.1 us
    pallas_call x1, Pallas kernels, attend(): pl.pallas_call(functools.partial(attend_kernel, n, out_all is not None),...  93.4 us
    ppermute x14, waiting for transfers between devices, swap(): return lax.ppermute(values, MESH_AXES, pairs)  66.9 us
    pallas_call x3, Pallas kernels, mlp_block(): pl.pallas_call(functools.partial(mlp_kernel, cap, counts), grid_spec=pltp...  65.8 us
    dot_general x5, matrix products, dot_low(): jnp.dot(a, b, preferred_element_type=jnp.float32).astype(jnp.bfloat16)  59.6 us
    ppermute x14, starting transfers between devices, swap(): return lax.ppermute(values, MESH_AXES, pairs)  21.5 us
  transfers between devices with their start and end apart: 18, of which 9 were waited for; matrix products, arithmetic and copies ran while one was open for 19% of the time, Pallas kernels for 31%

profile of v3, /device:TPU:0, one launch (start us, length us, event | category | flops | bytes accessed | tf_op | source)
XLA Modules:
  0.0 822.1 jit_solution(10000800616490601335)
XLA Ops:
  17.9 98.1 %gather_first.1 = (bf16[4,2,4,64,3072]{4,3,2,1,0:T(8,128)(2,1)}, bf16[4,2,4,64,2048]{4,3,2,1,0:T(8,128)(2,1)}, bf16[4,2,4,16,128]{4,3,2,1,0:T(8,128)(2,1)S(1)}, ...) custom-call(f32[64,3072]{1,0:T(8,128)S(1)} %copy-done.4, f32[64,2048]{1,0:T(8,128)S(1)} %copy-done.6, ...), custom_call_target="tpu_custom_call" | custom-call | tf_op jit(solution)/shard_map/gather_first/pallas_call | solution.py:383
  118.3 672.8 %conditional.1 = (bf16[2,256,2048]{2,1,0:T(8,128)(2,1)}, bf16[2,256,2048]{2,1,0:T(8,128)(2,1)}, f32[64,3072]{1,0:T(8,128)S(1)}, f32[64,2048]{1,0:T(8,128)S(1)}, ...) conditional(s32[]{:T(128)} %convert_element_type.324, (s32[]{:T(128)}, s32[2,1024]{1,0:T(2,128)}, ...), branch_computations={%region_2.20_spmd, %region_20.38_spmd} | conditional | flops 566091055104 | bytes 1006516928 | solution.py:1417
  145.2 93.4 %attend.3 = (bf16[384,2048]{1,0:T(8,128)(2,1)}, f32[384,1]{1,0:T(8,128)S(1)}, bf16[384,2048]{1,0:T(8,128)(2,1)}, bf16[384,2048]{1,0:T(8,128)(2,1)}, f32[4,4,384]...) custom-call(f32[384,2048]{1,0:T(8,128)} %fusion.72.refs_0_, ...), custom_call_target="tpu_custom_call", output_to_operand_aliasing={{6}: (9, {})} | custom-call | flops 77309411328 | bytes 6291456 | tf_op jit(solution)/shard_map/cond/branch_1_fun/attend/pallas_call | solution.py:849
  240.0 8.3 %multiply_reduce_fusion.5 = (f32[384]{0:T(512)S(1)}, f32[384,2048]{1,0:T(8,128)S(1)}) fusion(f32[384,2048]{1,0:T(8,128)} %fusion.72.refs_0_, bf16[384,2048]{1,0:T(8,128)(2,1)} %get-tuple-element.131.refs_4_, bf16[2048,2048]{1,0:T(8,128)(2,1)} %bitcast.193, f32[384]{0:T(512)S(1)} %fusion.105), kind=kOutput, calls=%fused_computation.177 | convolution fusion | flops 3224370688 | bytes 16256000 | tf_op jit(solution)/shard_map/cond/branch_1_fun/dot_general | solution.py:1201
  259.5 27.6 %collective-permute-done.15 = bf16[384,2048]{1,0:T(8,128)(2,1)S(1)} collective-permute-done((bf16[384,2048]{1,0:T(8,128)(2,1)}, bf16[384,2048]{1,0:T(8,128)(2,1)S(1)}, u32[]{:S(2)}, u32[]{:S(2)}) %collective-permute-start.15) | collective-permute-done | bytes 1572896 | tf_op jit(solution)/shard_map/cond/branch_1_fun/ppermute | solution.py:1076
  298.1 7.2 collective-permute-done.16
  309.1 5.7 all-gather.11.cloned.1.call-done
  314.8 17.4 %mlp_block.11 = (bf16[384,1408]{1,0:T(8,128)(2,1)}, bf16[384,2816]{1,0:T(8,128)(2,1)}, bf16[384,2048]{1,0:T(8,128)(2,1)}) custom-call(s32[1]{0:T(128)} %get-tuple-element.385.live_ref, bf16[384,2048]{1,0:T(8,128)(2,1)} %pad_maximum_fusion.15.rows_ref, bf16[384,2048]{1,0:T(8,128)(2,1)} %get-tuple-element.145.grad_ref, bf16[2048,1024]{1,0:T(8,128)(2,1)} %bitcast.206, ...), custom_call_target="tpu_custom_call" | custom-call | flops 11072962560 | bytes 26738688 | tf_op jit(solution)/shard_map/cond/branch_1_fun/mlp_block/pallas_call | solution.py:128
  338.1 17.9 %mlp_block.9 = (bf16[384,1408]{1,0:T(8,128)(2,1)}, bf16[384,2816]{1,0:T(8,128)(2,1)}, bf16[384,2048]{1,0:T(8,128)(2,1)}) custom-call(s32[1]{0:T(128)} %get-tuple-element.386.live_ref, bf16[384,2048]{1,0:T(8,128)(2,1)} %get-tuple-element.295.rows_ref, bf16[384,2048]{1,0:T(8,128)(2,1)} %convolution_convert_fusion.12.refs_8_.grad_ref, ...), custom_call_target="tpu_custom_call" | custom-call | flops 11072962560 | bytes 26738688 | tf_op jit(solution)/shard_map/cond/branch_1_fun/mlp_block/pallas_call | solution.py:128
  356.0 30.5 %mlp_block.10 = (bf16[768,1408]{1,0:T(8,128)(2,1)}, bf16[768,2816]{1,0:T(8,128)(2,1)}, bf16[768,2048]{1,0:T(8,128)(2,1)}) custom-call(s32[2]{0:T(128)} %gather_fusion.3, bf16[768,2048]{1,0:T(8,128)(2,1)} %pad_maximum_fusion.13.rows_ref, bf16[768,2048]{1,0:T(8,128)(2,1)} %pad_maximum_fusion.14.grad_ref, bf16[2048,1024]{1,0:T(8,128)(2,1)} %bitcast.208, ...), custom_call_target="tpu_custom_call" | custom-call | flops 22145925120 | bytes 36175872 | tf_op jit(solution)/shard_map/cond/branch_1_fun/mlp_block/pallas_call | solution.py:128
  386.5 13.6 %pad_maximum_fusion.11 = bf16[1536,2816]{1,0:T(8,128)(2,1)} fusion(bf16[384,2816]{1,0:T(8,128)(2,1)S(1)} %copy-done.63, bf16[768,2816]{1,0:T(8,128)(2,1)} %get-tuple-element.151, bf16[384,2816]{1,0:T(8,128)(2,1)S(1)} %copy-done.64), kind=kLoop, calls=%fused_computation.154 | loop fusion | flops 25952256 | bytes 17301504 | tf_op jit(solution)/shard_map/cond/branch_1_fun/concatenate | solution.py:1330
  401.8 6.3 pad_maximum_fusion.12
  414.1 10.8 %convolution_convert_fusion.7 = bf16[1408,2048]{1,0:T(8,128)(2,1)S(1)} fusion(bf16[1536,1408]{1,0:T(8,128)(2,1)S(1)} %pad_maximum_fusion.12, bf16[384,2048]{1,0:T(8,128)(2,1)} %get-tuple-element.145.grad_ref, bf16[384,2048]{1,0:T(8,128)(2,1)S(1)} %copy-done.74, bf16[384,2048]{1,0:T(8,128)(2,1)S(1)} %copy-done.73, bf16[384,2048]{1,0:T(8,128)(2,1)S(1)} %copy-done.71), kind=kOutput, calls=%fused_computation.155 | convolution fusion | flops 8886419456 | bytes 16384000 | tf_op jit(solution)/shard_map/cond/branch_1_fun/dot_general | solution.py:1205
  433.1 22.8 %convolution_convert_fusion.6 = bf16[2048,2816]{1,0:T(8,128)(2,1)S(1)} fusion(bf16[1536,2048]{1,0:T(8,128)(2,1)} %constant_dynamic-update-slice_fusion.5, bf16[1536,2816]{1,0:T(8,128)(2,1)} %pad_maximum_fusion.11), kind=kOutput, calls=%fused_computation.153 | convolution fusion | flops 17722507264 | bytes 26476544 | tf_op jit(solution)/shard_map/cond/branch_1_fun/dot_general | solution.py:1205
  461.9 5.7 fusion.64
  474.4 13.7 %convolution_convert_fusion.8 = bf16[1536,2048]{1,0:T(8,128)(2,1)S(1)} fusion(bf16[1536,1408]{1,0:T(8,128)(2,1)} %copy-done.53, bf16[1408,2048]{1,0:T(8,128)(2,1)} %get-tuple-element.138.down_hbm), kind=kOutput, calls=%fused_computation.156 | convolution fusion | flops 8861515776 | bytes 16384000 | tf_op jit(solution)/shard_map/cond/branch_1_fun/dot_general | solution.py:1205
  488.1 19.8 %collective-permute-done.20 = bf16[384,2048]{1,0:T(8,128)(2,1)S(1)} collective-permute-done((bf16[384,2048]{1,0:T(8,128)(2,1)}, bf16[384,2048]{1,0:T(8,128)(2,1)S(1)}, u32[]{:S(2)}, u32[]{:S(2)}) %collective-permute-start.20) | collective-permute-done | bytes 1572896 | tf_op jit(solution)/shard_map/cond/branch_1_fun/ppermute | solution.py:1076
  512.1 8.2 fusion.55
  530.4 7.1 fusion.108
  537.5 9.3 %collective-permute-done.25 = bf16[192,2048]{1,0:T(8,128)(2,1)S(1)} collective-permute-done((bf16[192,2048]{1,0:T(8,128)(2,1)}, bf16[192,2048]{1,0:T(8,128)(2,1)S(1)}, u32[]{:S(2)}, u32[]{:S(2)}) %collective-permute-start.25) | collective-permute-done | bytes 786464 | tf_op jit(solution)/shard_map/cond/branch_1_fun/ppermute | solution.py:1076
  552.5 10.1 %convolution_convert_fusion.11.refs_2_ = bf16[384,2048]{1,0:T(8,128)(2,1)} fusion(bf16[384,2048]{1,0:T(8,128)(2,1)S(1)} %get-tuple-element.162.refs_10_, bf16[2048,2048]{1,0:T(8,128)(2,1)} %bitcast.194), kind=kOutput, calls=%fused_computation.183 | convolution fusion | flops 3222011904 | bytes 11534336 | tf_op jit(solution)/shard_map/cond/branch_1_fun/dot_general | solution.py:1205
  564.6 110.3 %attend_back.3 = (bf16[384,3072]{1,0:T(8,128)(2,1)}, bf16[256,2048]{1,0:T(8,128)(2,1)}) custom-call(bf16[384,2048]{1,0:T(8,128)(2,1)} %get-tuple-element.167.refs_0_, bf16[1536,1024]{1,0:T(8,128)(2,1)} %get-tuple-element.168.refs_1_, bf16[384,2048]{1,0:T(8,128)(2,1)} %convolution_convert_fusion.11.refs_2_, f32[4,4,384]{2,1,0:T(4,128)} %copy-done.20, ...), custom_call_target="tpu_custom_call" | custom-call | flops 86973087744 | bytes 12582912 | tf_op jit(solution)/shard_map/cond/branch_1_fun/attend_back/pallas_call | solution.py:1006
  680.1 101.6 %qkv_back.3 = (f32[64,3072]{1,0:T(8,128)}, f32[384,2048]{1,0:T(8,128)}, f32[64,11264]{1,0:T(8,128)}, f32[64,2048]{1,0:T(8,128)}) custom-call(bf16[384,2048]{1,0:T(8,128)(2,1)} %get-tuple-element.176.normed_ref, bf16[384,3072]{1,0:T(8,128)(2,1)} %get-tuple-element.177.grad_ref, bf16[2048,3072]{1,0:T(8,128)(2,1)} %get-tuple-element.127.refs_4_.weights_hbm, ...), custom_call_target="tpu_custom_call" | custom-call | flops 115964116992 | bytes 18874368 | tf_op jit(solution)/shard_map/cond/branch_1_fun/qkv_back/pallas_call | solution.py:644
  802.7 6.4 add_multiply_fusion.2
  (265 shorter events, 143.1 us)
Async XLA Ops:
  7.2 111.1 %copy-start.104 = (s32[2]{0:T(128)S(1)}, s32[2]{0:T(128)}, u32[]{:S(2)}) copy-start(s32[2]{0:T(128)} %constant.268.clone) | copy-start | bytes 28
  118.3 672.9 %copy-start.7 = (f32[64,2048]{1,0:T(8,128)S(1)}, f32[64,2048]{1,0:T(8,128)}, u32[]{:S(2)}) copy-start(f32[64,2048]{1,0:T(8,128)} %out_ref.1) | copy-start | bytes 1572868
  126.7 182.4 %all-gather.9.cloned.1.call-start = ((), (), s32[]{:S(2)}) async-start(), calls=%async_computation.8 | async-start | bytes 4718592 | tf_op jit(solution)/shard_map/cond/branch_1_fun/all_gather | solution.py:1149
  128.8 186.1 %all-gather.11.cloned.1.call-start = ((), (), s32[]{:S(2)}) async-start(), calls=%async_computation.9 | async-start | bytes 8257536 | tf_op jit(solution)/shard_map/cond/branch_1_fun/all_gather | solution.py:1149
  239.2 285.3 %reduce-scatter.9.cloned.1.call-start = ((), (), s32[]{:S(2)}) async-start(), calls=%async_computation.10 | async-start | bytes 3604480 | tf_op jit(solution)/shard_map/cond/branch_1_fun/reduce_scatter | solution.py:1335
  251.2 35.9 %collective-permute-start.15 = (bf16[384,2048]{1,0:T(8,128)(2,1)}, bf16[384,2048]{1,0:T(8,128)(2,1)S(1)}, u32[]{:S(2)}, u32[]{:S(2)}) collective-permute-start(bf16[384,2048]{1,0:T(8,128)(2,1)} %get-tuple-element.295.rows_ref), channel_id=1, source_target_pairs={{0,16},{1,17},{2,18},{3,19},{4,20},{5,21},{6,22},{7,23},{8,24},{9,... | collective-permute-start | bytes 4718600 | tf_op jit(solution)/shard_map/cond/branch_1_fun/ppermute | solution.py:1076
  251.4 36.2 %collective-permute-start.14 = (bf16[384,2048]{1,0:T(8,128)(2,1)}, bf16[384,2048]{1,0:T(8,128)(2,1)}, u32[]{:S(2)}, u32[]{:S(2)}) collective-permute-start(bf16[384,2048]{1,0:T(8,128)(2,1)} %get-tuple-element.295.rows_ref), channel_id=1, source_target_pairs={{0,8},{1,9},{2,10},{3,11},{4,12},{5,13},{6,14},{7,15},{8,0},{9,1},... | collective-permute-start | bytes 4718600 | tf_op jit(solution)/shard_map/cond/branch_1_fun/ppermute | solution.py:1076
  287.2 18.1 %collective-permute-start.16 = (bf16[192,2048]{1,0:T(8,128)(2,1)S(1)}, bf16[192,2048]{1,0:T(8,128)(2,1)S(1)}, u32[]{:S(2)}, u32[]{:S(2)}) collective-permute-start(bf16[192,2048]{1,0:T(8,128)(2,1)S(1)} %slice.202), channel_id=1, source_target_pairs={{0,8},{1,9},{2,10},{3,11},{4,12},{5,13},{6,14},{7,15},{8,0},{9,1},... | collective-permute-start | bytes 2359304 | tf_op jit(solution)/shard_map/cond/branch_1_fun/ppermute | solution.py:1076
  288.8 18.0 %collective-permute-start.17 = (bf16[192,2048]{1,0:T(8,128)(2,1)S(1)}, bf16[192,2048]{1,0:T(8,128)(2,1)S(1)}, u32[]{:S(2)}, u32[]{:S(2)}) collective-permute-start(bf16[192,2048]{1,0:T(8,128)(2,1)S(1)} %slice.203), channel_id=1, source_target_pairs={{0,16},{1,17},{2,18},{3,19},{4,20},{5,21},{6,22},{7,23},{8,24},{9,... | collective-permute-start | bytes 2359304 | tf_op jit(solution)/shard_map/cond/branch_1_fun/ppermute | solution.py:1076
  334.9 73.1 %collective-permute-start.19 = (bf16[192,2048]{1,0:T(8,128)(2,1)}, bf16[192,2048]{1,0:T(8,128)(2,1)}, u32[]{:S(2)}, u32[]{:S(2)}) collective-permute-start(bf16[192,2048]{1,0:T(8,128)(2,1)} %get-tuple-element.366), channel_id=1, source_target_pairs={{0,8},{1,9},{2,10},{3,11},{4,12},{5,13},{6,14},{7,15},{8,0},{9,1},... | collective-permute-start | bytes 2359304 | tf_op jit(solution)/shard_map/cond/branch_1_fun/ppermute | solution.py:1076
  338.1 70.0 %collective-permute-start.18 = (bf16[192,2048]{1,0:T(8,128)(2,1)}, bf16[192,2048]{1,0:T(8,128)(2,1)}, u32[]{:S(2)}, u32[]{:S(2)}) collective-permute-start(bf16[192,2048]{1,0:T(8,128)(2,1)} %get-tuple-element.367), channel_id=1, source_target_pairs={{0,16},{1,17},{2,18},{3,19},{4,20},{5,21},{6,22},{7,23},{8,24},{9,... | collective-permute-start | bytes 2359304 | tf_op jit(solution)/shard_map/cond/branch_1_fun/ppermute | solution.py:1076
  428.4 33.5 %collective-permute-start.23 = (bf16[1,704,2048]{2,1,0:T(8,128)(2,1)}, bf16[1,704,2048]{2,1,0:T(8,128)(2,1)}, u32[]{:S(2)}, u32[]{:S(2)}) collective-permute-start(bf16[1,704,2048]{2,1,0:T(8,128)(2,1)} %dynamic-slice_bitcast_fusion.3), channel_id=1, source_target_pairs={{0,4},{1,5},{2,6},{3,7},{4,0},{5,1},{6,2},{7,3},{8,12},{9,13},{10,... | collective-permute-start | bytes 8650760 | tf_op jit(solution)/shard_map/cond/branch_1_fun/ppermute | solution.py:1076
  461.9 50.2 %collective-permute-start.22 = (bf16[4,256,2816]{2,1,0:T(8,128)(2,1)}, bf16[4,256,2816]{2,1,0:T(8,128)(2,1)}, u32[]{:S(2)}, u32[]{:S(2)}) collective-permute-start(bf16[4,256,2816]{2,1,0:T(8,128)(2,1)} %dynamic-slice_bitcast_fusion.2), channel_id=1, source_target_pairs={{0,4},{1,5},{2,6},{3,7},{4,0},{5,1},{6,2},{7,3},{8,12},{9,13},{10,... | collective-permute-start | bytes 17301512 | tf_op jit(solution)/shard_map/cond/branch_1_fun/ppermute | solution.py:1076
  467.6 212.5 %reduce-scatter.11.cloned.1.call-start = ((), (), s32[]{:S(2)}) async-start(), calls=%async_computation.11 | async-start | bytes 7208960 | tf_op jit(solution)/shard_map/cond/branch_1_fun/reduce_scatter | solution.py:1339
  469.6 38.3 %collective-permute-start.20 = (bf16[384,2048]{1,0:T(8,128)(2,1)}, bf16[384,2048]{1,0:T(8,128)(2,1)S(1)}, u32[]{:S(2)}, u32[]{:S(2)}) collective-permute-start(bf16[384,2048]{1,0:T(8,128)(2,1)} %pad_maximum_fusion.16), channel_id=1, source_target_pairs={{0,8},{1,9},{2,10},{3,11},{4,12},{5,13},{6,14},{7,15},{8,0},{9,1},... | collective-permute-start | bytes 4718600 | tf_op jit(solution)/shard_map/cond/branch_1_fun/ppermute | solution.py:1076
  472.7 36.5 %collective-permute-start.21 = (bf16[384,2048]{1,0:T(8,128)(2,1)S(1)}, bf16[384,2048]{1,0:T(8,128)(2,1)S(1)}, u32[]{:S(2)}, u32[]{:S(2)}) collective-permute-start(bf16[384,2048]{1,0:T(8,128)(2,1)S(1)} %pad_maximum_fusion.17), channel_id=1, source_target_pairs={{0,16},{1,17},{2,18},{3,19},{4,20},{5,21},{6,22},{7,23},{8,24},{9,... | collective-permute-start | bytes 4718600 | tf_op jit(solution)/shard_map/cond/branch_1_fun/ppermute | solution.py:1076
  527.5 19.3 %collective-permute-start.25 = (bf16[192,2048]{1,0:T(8,128)(2,1)}, bf16[192,2048]{1,0:T(8,128)(2,1)S(1)}, u32[]{:S(2)}, u32[]{:S(2)}) collective-permute-start(bf16[192,2048]{1,0:T(8,128)(2,1)} %get-tuple-element.358), channel_id=1, source_target_pairs={{0,8},{1,9},{2,10},{3,11},{4,12},{5,13},{6,14},{7,15},{8,0},{9,1},... | collective-permute-start | bytes 2359304 | tf_op jit(solution)/shard_map/cond/branch_1_fun/ppermute | solution.py:1076
  528.9 19.0 %collective-permute-start.24 = (bf16[192,2048]{1,0:T(8,128)(2,1)}, bf16[192,2048]{1,0:T(8,128)(2,1)S(1)}, u32[]{:S(2)}, u32[]{:S(2)}) collective-permute-start(bf16[192,2048]{1,0:T(8,128)(2,1)} %get-tuple-element.360), channel_id=1, source_target_pairs={{0,16},{1,17},{2,18},{3,19},{4,20},{5,21},{6,22},{7,23},{8,24},{9,... | collective-permute-start | bytes 2359304 | tf_op jit(solution)/shard_map/cond/branch_1_fun/ppermute | solution.py:1076
  562.5 112.3 %collective-permute-start.26 = (bf16[384,2048]{1,0:T(8,128)(2,1)}, bf16[384,2048]{1,0:T(8,128)(2,1)}, u32[]{:S(2)}, u32[]{:S(2)}) collective-permute-start(bf16[384,2048]{1,0:T(8,128)(2,1)} %pad_maximum_fusion.18), channel_id=1, source_target_pairs={{0,8},{1,9},{2,10},{3,11},{4,12},{5,13},{6,14},{7,15},{8,0},{9,1},... | collective-permute-start | bytes 4718600 | tf_op jit(solution)/shard_map/cond/branch_1_fun/ppermute | solution.py:1076
  563.1 111.7 %collective-permute-start.27 = (bf16[384,2048]{1,0:T(8,128)(2,1)}, bf16[384,2048]{1,0:T(8,128)(2,1)}, u32[]{:S(2)}, u32[]{:S(2)}) collective-permute-start(bf16[384,2048]{1,0:T(8,128)(2,1)} %pad_maximum_fusion.19), channel_id=1, source_target_pairs={{0,16},{1,17},{2,18},{3,19},{4,20},{5,21},{6,22},{7,23},{8,24},{9,... | collective-permute-start | bytes 4718600 | tf_op jit(solution)/shard_map/cond/branch_1_fun/ppermute | solution.py:1076
  564.6 110.3 %copy-start.85 = (s32[512]{0:T(512)S(1)}, s32[512]{0:T(512)}, u32[]{:S(2)}) copy-start(s32[512]{0:T(512)} %copy-done.84) | copy-start | bytes 6148 | tf_op jit(solution)/shard_map/cond
  564.6 110.3 %copy-start.89 = (pred[512]{0:T(512)(128)(4,1)S(1)}, pred[512]{0:T(512)(128)(4,1)}, u32[]{:S(2)}) copy-start(pred[512]{0:T(512)(128)(4,1)} %copy-done.88) | copy-start | bytes 1540 | tf_op jit(solution)/shard_map/cond
  680.1 101.6 %copy-start.15 = (f32[1,2048]{1,0:T(1,128)S(1)}, f32[1,2048]{1,0:T(1,128)}, u32[]{:S(2)}) copy-start(f32[1,2048]{1,0:T(1,128)} %copy-done.14) | copy-start | bytes 24580 | tf_op jit(solution)/shard_map/cond
  680.1 101.6 %copy-start.30 = (f32[384,2048]{1,0:T(8,128)S(1)}, f32[384,2048]{1,0:T(8,128)}, u32[]{:S(2)}) copy-start(f32[384,2048]{1,0:T(8,128)} %fusion.72.refs_0_) | copy-start | bytes 9437188 | tf_op jit(solution)/shard_map/cond
  (60 other events, 707.9 us)
Sparse Core Ops, SparseCore 0:
  129.7 58.4 all-gather.8
  239.4 75.4 all-gather.10
  467.7 56.8 reduce-scatter.8
  526.7 143.9 reduce-scatter.10

commit v4 on v3

--- a/solution.py
+++ b/solution.py
@@ -36,6 +36,7 @@
 
 UNIT_GROUP = 256
 WIDTH_GROUP = 256
+LANES = 128
 
 
 def unit_groups(units):
@@ -44,7 +45,7 @@
 
 def mlp_kernel(
     cap, counts, live_ref, rows_ref, grad_ref, gateup_first, gateup_last, down_hbm,
-    hidden_ref, gateup_grad_ref, back_ref, gateup_ref, down_ref, gateup_sems, down_sems,
+    hidden_ref, gateup_grad_ref, back_ref, out_ref, gateup_ref, down_ref, gateup_sems, down_sems,
 ):
     step = pl.program_id(0)
     width = rows_ref.shape[1]
@@ -97,11 +98,13 @@
         def back_step(k, carry):
             at = span(k * WIDTH_GROUP, WIDTH_GROUP)
             back_ref[:count, at] = dot_nt(gateup_grad_ref[:count, :], gateup_ref[at, :]).astype(jnp.bfloat16)
+            out = jnp.dot(hidden_ref[:count, :], down_ref[:, at], preferred_element_type=jnp.float32)
+            out_ref[:count, at] = out.astype(jnp.bfloat16)
             return carry
 
         lax.fori_loop(0, width // WIDTH_GROUP, back_step, 0)
         if count < cap:
-            for ref in (hidden_ref, gateup_grad_ref, back_ref):
+            for ref in (hidden_ref, gateup_grad_ref, back_ref, out_ref):
                 ref[count:, :] = jnp.zeros((cap - count, ref.shape[1]), ref.dtype)
 
     for low, count in zip((None,) + counts[:-1], counts):
@@ -131,7 +134,7 @@
             num_scalar_prefetch=1,
             grid=(blocks,),
             in_specs=[by_block(width), by_block(width)] + [pl.BlockSpec(memory_space=pl.ANY)] * 3,
-            out_specs=(by_block(units), by_block(2 * units), by_block(width)),
+            out_specs=(by_block(units), by_block(2 * units), by_block(width), by_block(width)),
             scratch_shapes=[
                 pltpu.VMEM((width, gateup_cols), low),
                 pltpu.VMEM(down.shape, low),
@@ -143,10 +146,11 @@
             jax.ShapeDtypeStruct((blocks * cap, units), low),
             jax.ShapeDtypeStruct((blocks * cap, 2 * units), low),
             jax.ShapeDtypeStruct((blocks * cap, width), low),
+            jax.ShapeDtypeStruct((blocks * cap, width), low),
         ),
         compiler_params=pltpu.CompilerParams(vmem_limit_bytes=56 * 1024 * 1024),
         cost_estimate=pl.CostEstimate(
-            flops=10 * blocks * cap * width * units,
+            flops=12 * blocks * cap * width * units,
             bytes_accessed=2 * (width * gateup_cols + down.size) + 12 * blocks * cap * width,
             transcendentals=blocks * cap * units,
         ),
@@ -169,7 +173,8 @@
         [part[:, low:high] for low, high in groups for part in (grad_gate, grad_upper)], axis=1
     ).astype(jnp.bfloat16)
     back = jnp.dot(gateup_grad, gateup.T, preferred_element_type=jnp.float32).astype(jnp.bfloat16)
-    return hidden, gateup_grad, back
+    out = jnp.dot(hidden, down, preferred_element_type=jnp.float32).astype(jnp.bfloat16)
+    return hidden, gateup_grad, back, out
 
 
 class Place:
@@ -666,6 +671,191 @@
     )(normed, grad, weights, pieces, out_sum)
 
 
+class TokenScatter:
+    def __init__(self, place, copies, blocks, near, corner_x, corner_y, came_x, came_y, load_sem):
+        self.p, self.c, self.blocks, self.near = place, copies, blocks, near
+        self.corner_x, self.corner_y, self.came_x, self.came_y = corner_x, corner_y, came_x, came_y
+        self.cap = near.shape[0] // 2
+        self.keep = pltpu.make_async_copy(blocks[1], near, load_sem)
+
+    def begin(self):
+        p, c, half = self.p, self.c, self.cap // 2
+        self.keep.start()
+        self.far = [
+            c.make(self.blocks[2].at[:half], self.corner_x, p.by_x), c.make(self.blocks[2].at[half:], self.corner_y, p.by_y)
+        ]
+        c.go(self.far)
+
+    def middle(self):
+        p, c, near, cap = self.p, self.c, self.near, self.cap
+        self.keep.wait()
+        c.arrive(self.far)
+        for at, came in ((slice(cap // 2, cap), self.corner_y), (slice(cap, cap + cap // 2), self.corner_x)):
+            near[at, :] = (near[at, :].astype(jnp.float32) + came[...].astype(jnp.float32)).astype(jnp.bfloat16)
+        self.close = [c.make(near.at[:cap], self.came_x, p.by_x), c.make(near.at[cap:], self.came_y, p.by_y)]
+        c.go(self.close)
+
+    def end(self):
+        self.c.arrive(self.close)
+
+
+def mid_back_kernel(
+    n, cap, units, *refs,
+):
+    back, rows_in, gateup_in, hidden_in, grads_in = (refs[k : k + 3] for k in range(0, 15, 3))
+    sum_ref, down_ref, gateup_ref = refs[15:18]
+    (
+        wide_now, both_now, turned, own, near, corner_x, corner_y, came_x, came_y, down_leaving, down_came,
+        gateup_leaving, gateup_came, send_sems, recv_sems, load_sems,
+    ) = refs[18:]
+    p = Place(n)
+    c = Copies(send_sems, recv_sems)
+    low = jnp.bfloat16
+    loaded = [0]
+
+    def load(parts, into, cols=None):
+        moves = []
+        for at, part in zip((slice(0, cap), slice(cap, 3 * cap), slice(3 * cap, 4 * cap)), parts):
+            to = into.at[at] if cols is None else into.at[at, cols]
+            moves.append(pltpu.make_async_copy(part, to, load_sems.at[loaded[0]]))
+            loaded[0] += 1
+            moves[-1].start()
+        return moves
+
+    def wait(moves):
+        for m in moves:
+            m.wait()
+
+    first = load(grads_in, wide_now) + load(hidden_in, both_now, slice(0, units))
+    keep = pltpu.make_async_copy(back[0], own, load_sems.at[14])
+    keep.start()
+    tokens = TokenScatter(p, c, back, near, corner_x, corner_y, came_x, came_y, load_sems.at[15])
+    p.greet([p.by_x, p.by_y, p.sibling])
+    tokens.begin()
+
+    wait(first)
+
+    def turn(k, carry):
+        at = pl.ds(pl.multiple_of(k * LANES, LANES), LANES)
+        turned[at, :] = both_now[:, at].T
+        return carry
+
+    lax.fori_loop(0, units // LANES, turn, 0)
+    part = units // 2
+    width = wide_now.shape[1]
+
+    def down_half(core, put):
+        def one(k, carry):
+            at = pl.ds(pl.multiple_of(k * WIDTH_GROUP, WIDTH_GROUP), WIDTH_GROUP)
+            left = turned[pl.ds(pl.multiple_of(core * part, 16), part), :]
+            put(at, jnp.dot(left, wide_now[:, at], preferred_element_type=jnp.float32))
+            return carry
+
+        lax.fori_loop(0, width // WIDTH_GROUP, one, 0)
+
+    def put_leaving(at, term):
+        down_leaving[:, at] = term.astype(low)
+
+    def put_down(at, term):
+        down_ref[:, at] = (term + down_came[:, at].astype(jnp.float32)).astype(low)
+
+    down_half(1 - p.core, put_leaving)
+    down_move = [c.make(down_leaving, down_came, p.sibling)]
+    c.go(down_move)
+    tokens.middle()
+    c.arrive(down_move)
+    down_half(p.core, put_down)
+
+    second = load(rows_in, wide_now) + load(gateup_in, both_now)
+    wait(second)
+    line = gateup_ref.shape[1]
+    cols = 2 * units
+
+    def gateup_part(k, put):
+        left = wide_now[:, pl.ds(pl.multiple_of(k * line, line), line)].T
+
+        def one(j, carry):
+            at = pl.ds(pl.multiple_of(j * WIDTH_GROUP, WIDTH_GROUP), WIDTH_GROUP)
+            put(at, jnp.dot(left, both_now[:, at], preferred_element_type=jnp.float32))
+            return carry
+
+        lax.fori_loop(0, cols // WIDTH_GROUP, one, 0)
+
+    moves = []
+    planes = gateup_ref.shape[0]
+    for t in range(planes):
+        slot = t % 2
+        if t >= 2:
+            moves[t - 2].wait_send()
+
+        def put_slot(at, term, slot=slot):
+            gateup_leaving[slot, :, at] = term.astype(low)
+
+        gateup_part(t * 2 + 1 - p.core, put_slot)
+        moves.append(c.make(gateup_leaving.at[slot], gateup_came.at[t], p.sibling))
+        moves[-1].start()
+    for t in range(planes):
+        moves[t].wait_recv()
+
+        def put_sum(at, term, t=t):
+            gateup_ref[t, :, at] = (term + gateup_came[t, :, at].astype(jnp.float32)).astype(low)
+
+        gateup_part(t * 2 + p.core, put_sum)
+    for t in range(max(planes - 2, 0), planes):
+        moves[t].wait_send()
+    tokens.end()
+    keep.wait()
+    sum_ref[...] = own[...].astype(jnp.float32) + (
+        came_x[...].astype(jnp.float32) + came_y[...].astype(jnp.float32)
+    )
+    c.end()
+
+
+def mid_back(back, rows, gateup_grads, hidden, grads, cap, planes, n, collective_id):
+    width = rows[0].shape[1]
+    units = hidden[0].shape[1]
+    line = width // planes // 2
+    low = jnp.bfloat16
+    any_spec = pl.BlockSpec(memory_space=pl.ANY)
+    in_vmem = pl.BlockSpec(memory_space=pltpu.VMEM)
+    vmem = lambda *shape: pltpu.VMEM(shape, low)
+    return pl.pallas_call(
+        functools.partial(mid_back_kernel, n, cap, units),
+        in_specs=[any_spec] * 15,
+        out_specs=(in_vmem,) * 3,
+        out_shape=(
+            jax.ShapeDtypeStruct((cap, width), jnp.float32),
+            jax.ShapeDtypeStruct((units // 2, width), low),
+            jax.ShapeDtypeStruct((planes, line, 2 * units), low),
+        ),
+        scratch_shapes=[
+            vmem(4 * cap, width),
+            vmem(4 * cap, 2 * units),
+            vmem(units, 4 * cap),
+            vmem(cap, width),
+            vmem(2 * cap, width),
+            vmem(cap // 2, width),
+            vmem(cap // 2, width),
+            vmem(cap, width),
+            vmem(cap, width),
+            vmem(units // 2, width),
+            vmem(units // 2, width),
+            vmem(2, line, 2 * units),
+            vmem(planes, line, 2 * units),
+            pltpu.SemaphoreType.DMA((12,)),
+            pltpu.SemaphoreType.DMA((12,)),
+            pltpu.SemaphoreType.DMA((16,)),
+        ],
+        compiler_params=pltpu.CompilerParams(
+            vmem_limit_bytes=61 * 1024 * 1024, collective_id=collective_id, has_side_effects=True
+        ),
+        cost_estimate=pl.CostEstimate(
+            flops=48 * cap * width * units, bytes_accessed=32 * cap * (width + units), transcendentals=0
+        ),
+        name="mid_back",
+    )(*back, *rows, *gateup_grads, *hidden, *grads)
+
+
 def fill_bias(r, key_code, query_code, query_base, bias):
     rows = bias.shape[0]
     code = key_code[r * rows : (r + 1) * rows, :]
@@ -884,10 +1074,10 @@
     q_ref, kv_all, do_ref, total_ref, mixed_ref, key_code, query_code, query_base, cosine, sine = refs[:10]
     refs = refs[10:]
     if parts:
-        branch_ref, refs = refs[0], refs[1:]
+        branch_ref, down_terms, refs = refs[0], refs[1:4], refs[4:]
     grad_ref, refs = refs[0], refs[1:]
     if parts:
-        out_sum, refs = refs[0], refs[1:]
+        (out_sum, came_x, came_y), refs = refs[:3], refs[3:]
     dq_now, dkv_now, bias, inner_now, leaving, came, send_sems, recv_sems = refs[:8]
     p = Place(n)
     c = Copies(send_sems, recv_sems)
@@ -897,7 +1087,9 @@
     p.greet([p.by_x, p.by_y, p.sibling] if parts else [])
     every = range(len(parts))
     if parts:
-        scatter = PlaneScatter(p, c, mixed_ref, branch_ref, parts, *refs[8:])
+        scatter = PlaneScatter(p, c, mixed_ref, branch_ref, parts, *refs[8:14])
+        tokens = TokenScatter(p, c, down_terms, *refs[14:17], came_x, came_y, refs[17])
+        tokens.begin()
     copies = {r: c.make(leaving.at[r - 1], came.at[r - 1], p.below) for r in range(1, n)}
     dq_now[...] = jnp.zeros_like(dq_now)
     q_cols = HEADS * HEAD_DIM
@@ -965,6 +1157,7 @@
             for k in every:
                 scatter.begin(k)
         if parts and r == max(n - 2, 0):
+            tokens.middle()
             for k in every:
                 scatter.across_first(k)
         if parts and r == max(n - 3, 0):
@@ -974,6 +1167,7 @@
         for k in every:
             scatter.end(k)
         out_sum[...] = scatter.total[p.t]
+        tokens.end()
 
     def finish(g, carry):
         for h in range(GROUP):
@@ -991,7 +1185,7 @@
 
 def attend_back(
     query, kv_all, grad, total, mixed, key_code, query_code, query_base, cosine, sine, n, collective_id, branch_grad=None,
-    planes=0,
+    down_terms=(), planes=0,
 ):
     rows, width = query.shape
     kv_cols = kv_all.shape[1]
@@ -999,14 +1193,18 @@
     slots = max(n - 1, 1)
     more, parts, shapes, scratch = (), [], (), []
     if branch_grad is not None:
-        more, parts = (branch_grad,), plane_parts(width, 2)
-        shapes = (jax.ShapeDtypeStruct((width // planes // 2, width), jnp.bfloat16),)
+        more, parts = (branch_grad, *down_terms), plane_parts(width, 2)
+        came = jax.ShapeDtypeStruct((rows, width), jnp.bfloat16)
+        shapes = (jax.ShapeDtypeStruct((width // planes // 2, width), jnp.bfloat16), came, came)
         scratch = plane_scratch(rows, width, width, planes)
-    copies = n + 4 * len(parts)
+        scratch += [pltpu.VMEM((count, width), jnp.bfloat16) for count in (2 * rows, rows // 2, rows // 2)]
+        scratch.append(pltpu.SemaphoreType.DMA)
+    copies = n + 4 * len(parts) + 4
+    any_spec = pl.BlockSpec(memory_space=pl.ANY)
     return pl.pallas_call(
         functools.partial(attend_back_kernel, n, parts),
-        in_specs=[in_vmem] * (10 + len(more)),
-        out_specs=(in_vmem,) * (1 + len(shapes)),
+        in_specs=[in_vmem] * (10 + len(more[:1])) + [any_spec] * len(more[1:]),
+        out_specs=(in_vmem,) * (1 + len(shapes[:1])) + (any_spec,) * len(shapes[1:]),
         out_shape=(jax.ShapeDtypeStruct((rows, width + kv_cols), jnp.bfloat16),) + shapes,
         scratch_shapes=[
             pltpu.VMEM((KV_HEADS, GROUP, HEAD_DIM, rows), jnp.float32),
@@ -1121,29 +1319,17 @@
         corner = [self.swap(by_y[:half], 2), self.swap(by_x[half:], 4)]
         return [rows, by_x, by_y, jnp.concatenate(corner)]
 
-    def scatter_far(self, blocks):
-        if self.planes != 4:
-            return jnp.concatenate([b.astype(jnp.bfloat16) for b in blocks]), None, None
-        own, by_x, by_y, corner = blocks
-        half = own.shape[0] // 2
-        top = self.swap(corner[:half], 2).astype(jnp.float32)
-        bottom = self.swap(corner[half:], 4).astype(jnp.float32)
-        by_y = jnp.concatenate([by_y[:half] + top, by_y[half:]]).astype(jnp.bfloat16)
-        by_x = jnp.concatenate([by_x[:half], by_x[half:] + bottom]).astype(jnp.bfloat16)
-        return own, by_x, by_y
-
-    def scatter_near(self, own, by_x, by_y):
+    def scatter_tokens(self, parts, cap):
+        every = jnp.concatenate(parts)
         if self.planes != 4:
             total = lax.psum_scatter(
-                own, MESH_AXES, scatter_dimension=0, tiled=True, axis_index_groups=self.same_plane
+                every, MESH_AXES, scatter_dimension=0, tiled=True, axis_index_groups=self.same_plane
             )
-            return total, None, None
-        return own, self.swap(by_x, 2), self.swap(by_y, 4)
-
-    def scatter_sum(self, own, came_x, came_y):
-        if came_x is None:
-            return own.astype(jnp.float32)
-        return own.astype(jnp.float32) + came_x.astype(jnp.float32) + came_y.astype(jnp.float32)
+            return total.astype(jnp.float32)
+        total = every[:cap].astype(jnp.float32)
+        for k in range(1, 4):
+            total += self.swap(every[k * cap : (k + 1) * cap], 2 * k).astype(jnp.float32)
+        return total
 
     def gather_chip(self, pieces):
         every = lax.all_gather(pieces, MESH_AXES, axis=1, tiled=True, axis_index_groups=self.same_chip)
@@ -1311,54 +1497,48 @@
     lives = links.plane_counts(counts, cap)
 
     parts = [[k] for k in range(planes)] if planes != 4 else [[0], [1, 2], [3]]
-    hidden_blocks, gateup_grad_blocks, mid_terms = [], [], [None] * planes
+    hidden_blocks, gateup_grad_blocks, back_parts, down_parts = [], [], [], []
     row_parts, grad_parts = [], []
     for part in parts:
         rows = together([blocks[k] for k in part])
         grads = together([down_grad_blocks[k] for k in part])
         row_parts.append(rows)
         grad_parts.append(grads)
-        hidden, gateup_grad, back = mlp_block(
+        hidden, gateup_grad, back, down_part = mlp_block(
             rows, grads, lives[jnp.array(part)], gateup_first, gateup_last, down_low, cap
         )
         hidden_blocks.append(hidden)
         gateup_grad_blocks.append(gateup_grad)
-        for i, k in enumerate(part):
-            mid_terms[k] = back[i * cap : (i + 1) * cap]
-    mid_far = links.scatter_far(mid_terms)
-    hidden_all, rows_all = jnp.concatenate(hidden_blocks), jnp.concatenate(row_parts)
-    grads_all, gateup_grad_all = jnp.concatenate(grad_parts), jnp.concatenate(gateup_grad_blocks)
-    mid_far, hidden_all, gateup_grad_all = lax.optimization_barrier((mid_far, hidden_all, gateup_grad_all))
-    mid_near = links.scatter_near(*mid_far)
-    term_down = dot_low(hidden_all.T, grads_all)
-    down_half = links.scatter_core(term_down.reshape(1, 2, ff_part // 2, width))[0]
-    grad_down = lax.psum_scatter(down_half, "narrow", scatter_dimension=0, tiled=True)
-    term_gateup = dot_low(rows_all.T, gateup_grad_all)
-    gateup_half = links.scatter_core(term_gateup.reshape(planes, 2, n * shard_rows, 2 * ff_part))
-    gateup_half, grad_down = lax.optimization_barrier((gateup_half, grad_down))
+        back_parts.append(back)
+        down_parts.append(down_part)
+    if planes == 4 and n > 1 and cap <= 384:
+        grad_normed_mid, down_half, gateup_half = mid_back(
+            back_parts, row_parts, gateup_grad_blocks, hidden_blocks, grad_parts, cap, planes, n, ids + 8
+        )
+    else:
+        grad_normed_mid = links.scatter_tokens(back_parts, cap)
+        term_down = dot_low(jnp.concatenate(hidden_blocks).T, jnp.concatenate(grad_parts))
+        down_half = links.scatter_core(term_down.reshape(1, 2, ff_part // 2, width))[0]
+        term_gateup = dot_low(jnp.concatenate(row_parts).T, jnp.concatenate(gateup_grad_blocks))
+        gateup_half = links.scatter_core(term_gateup.reshape(planes, 2, n * shard_rows, 2 * ff_part))
     grad_pieces = lax.psum_scatter(gateup_half, "narrow", scatter_dimension=1, tiled=True)
-    down_terms = dot_low(hidden_all, down_low)
-    down_terms, mid_near = lax.optimization_barrier((down_terms, mid_near))
-    grad_normed_mid = links.scatter_sum(*mid_near)
-    order = [k for part in parts for k in part]
-    down_terms = {k: down_terms[i * cap : (i + 1) * cap] for i, k in enumerate(order)}
-    down_far = links.scatter_far([down_terms[k] for k in range(planes)])
 
     grad_middle = upstream + norm_backward(middle, inverse_two, gain_full[1], grad_normed_mid)
     branch_grad_low = grad_middle.astype(low)
-    branch_grad_low, gateup_half = lax.optimization_barrier((branch_grad_low, gateup_half))
     grad_attended_low = dot_low(branch_grad_low, out_low.T)
-    grad_attended_low, down_far = lax.optimization_barrier((grad_attended_low, down_far))
-    down_near = links.scatter_near(*down_far)
     back = (query_low, kv_all, grad_attended_low, totals, attended_low, *codes, cosine, sine, n, ids + 1)
     if planes == 4 and n > 1:
-        grad_projected_low, out_sum = attend_back(*back, branch_grad_low, planes)
-        down_near, grad_projected_low = lax.optimization_barrier((down_near, grad_projected_low))
+        grad_projected_low, out_sum, *came = attend_back(*back, branch_grad_low, down_parts, planes)
+        down_proj = sum((part.astype(jnp.float32) for part in came), down_parts[0].astype(jnp.float32))
+        down_half, grad_pieces, grad_projected_low = lax.optimization_barrier(
+            (down_half, grad_pieces, grad_projected_low)
+        )
         grad_qkv, grad_normed, grad_gateup, grad_out = qkv_back(
             normed_low, grad_projected_low, qkv_low, grad_pieces, out_sum, planes, n, ids + 4
         )
     else:
         grad_projected_low = attend_back(*back)[0]
+        down_proj = links.scatter_tokens(down_parts, cap)
         grad_out = links.scatter_rows(dot_low(attended_low.T, branch_grad_low))
         grad_qkv = links.scatter_rows(dot_low(normed_low.T, grad_projected_low)).astype(jnp.float32)
         grad_normed = dot32(grad_projected_low, qkv_low.T)
@@ -1367,7 +1547,8 @@
         grad_middle + norm_backward(inputs, inverse_one, gain_full[0], grad_normed)
     ).astype(low)
 
-    layer_out = (middle + links.scatter_sum(*down_near)).astype(low)
+    grad_down = lax.psum_scatter(down_half, "narrow", scatter_dimension=0, tiled=True)
+    layer_out = (middle + down_proj).astype(low)
 
     def spread(packed, skipped):
         back = lax.dot_general(

time: 834 us -> 761 us (0.912)
  Pallas kernels: 469 us -> 551 us
  other arithmetic: 96.5 us -> 41.4 us
  matrix products: 77.5 us -> 35 us
  waiting for transfers between devices: 77 us -> 57 us
  local copies, waits for them, and re-layouts: 53.1 us -> 35.7 us
  starting transfers between devices: 21.6 us -> 4.22 us
    pallas_call x0 -> x1, Pallas kernels: none -> 71.9 us  [mid_back(): pl.pallas_call(functools.partial(mid_back_kernel, n, cap, units), in_spec...]
    dot_general x5 -> x2, matrix products: 59.6 us -> 12.8 us  [dot_low(): jnp.dot(a, b, preferred_element_type=jnp.float32).astype(jnp.bfloat16)]
    concatenate x9 -> x0, other arithmetic: 32.8 us -> none  [the longest x1 13.6 us: layer(): jnp.concatenate(gateup_grad_blocks)]
    ppermute x14 -> x4, waiting for transfers between devices: 66.9 us -> 42.8 us  [swap(): return lax.ppermute(values, MESH_AXES, pairs)]
    ppermute x14 -> x4, starting transfers between devices: 21.5 us -> 4.05 us  [swap(): return lax.ppermute(values, MESH_AXES, pairs)]
    cond x100 -> x0, local copies, waits for them, and re-layouts: 16.2 us -> none
    another operation x0 -> x88, local copies, waits for them, and re-layouts: none -> 12.1 us
    unnamed x0 -> x1, loops' own time: none -> 9.48 us
  transfers between devices with their start and end apart: 18 -> 8, of which waited for: 9 -> 5; matrix products, arithmetic and copies ran while one was open for 19% -> 10% of each run, Pallas kernels for 31% -> 41%
where the time goes in v4:
time: 761 us; the launch traced here: 751 us
  Pallas kernels  551 us (72%)
  waiting for transfers between devices  57 us (7%)
  other arithmetic  41.4 us (5%)
  local copies, waits for them, and re-layouts  35.7 us (5%)
  matrix products  35 us (5%)
  between operations  17.4 us (2%)
  loops' own time  9.48 us (1%)
    pallas_call x1, Pallas kernels, attend_back(): pl.pallas_call(functools.partial(attend_back_kernel, n, parts), in_specs=...  115 us
    pallas_call x1, Pallas kernels, qkv_back(): pl.pallas_call(functools.partial(qkv_back_kernel, n, parts), in_specs=[in...  98.4 us
    pallas_call x1, Pallas kernels, gather_first(): pl.pallas_call(functools.partial(gather_kernel, n), out_shape=(jax.ShapeD...  98.1 us
    pallas_call x1, Pallas kernels, attend(): pl.pallas_call(functools.partial(attend_kernel, n, out_all is not None),...  93.4 us
    pallas_call x3, Pallas kernels, mlp_block(): pl.pallas_call(functools.partial(mlp_kernel, cap, counts), grid_spec=pltp...  73.7 us
    pallas_call x1, Pallas kernels, mid_back(): pl.pallas_call(functools.partial(mid_back_kernel, n, cap, units), in_spec...  71.9 us
    ppermute x4, waiting for transfers between devices, swap(): return lax.ppermute(values, MESH_AXES, pairs)  42.8 us
  transfers between devices with their start and end apart: 8, of which 5 were waited for; matrix products, arithmetic and copies ran while one was open for 10% of the time, Pallas kernels for 41%

profile of v4, /device:TPU:0, one launch (start us, length us, event | category | flops | bytes accessed | tf_op | source)
XLA Modules:
  0.0 751.2 jit_solution(7196791898844710369)
XLA Ops:
  17.5 98.1 %gather_first.1 = (bf16[4,2,4,64,3072]{4,3,2,1,0:T(8,128)(2,1)}, bf16[4,2,4,64,2048]{4,3,2,1,0:T(8,128)(2,1)}, bf16[4,2,4,16,128]{4,3,2,1,0:T(8,128)(2,1)S(1)}, ...) custom-call(f32[64,3072]{1,0:T(8,128)S(1)} %copy-done.4, f32[64,2048]{1,0:T(8,128)S(1)} %copy-done.6, ...), custom_call_target="tpu_custom_call" | custom-call | tf_op jit(solution)/shard_map/gather_first/pallas_call | solution.py:388
  117.2 607.7 %conditional.3 = (bf16[2,256,2048]{2,1,0:T(8,128)(2,1)}, bf16[2,256,2048]{2,1,0:T(8,128)(2,1)}, f32[64,3072]{1,0:T(8,128)}, f32[64,2048]{1,0:T(8,128)S(1)}, f32[64,11264]{1,0:T(8,128)}, /*index=5*/f32[176,2048]{1,0:T(8,128)}) conditional(s32[]{:T(128)} %convert_element_type.216, (s32[]{:T(128)}, s32[2,1024]{1,0:T(2,128)S(1)}, ...), branch_computations={%region_2.20_spmd, %region_20.38_spmd} | conditional | flops 566066282496 | bytes 815422144
  139.2 2.7 fusion.77.refs_0_
  142.7 93.4 %attend.3 = (bf16[384,2048]{1,0:T(8,128)(2,1)}, f32[384,1]{1,0:T(8,128)S(1)}, bf16[384,2048]{1,0:T(8,128)(2,1)}, bf16[384,2048]{1,0:T(8,128)(2,1)}, f32[4,4,384]...) custom-call(f32[384,2048]{1,0:T(8,128)} %fusion.77.refs_0_, ...), custom_call_target="tpu_custom_call", output_to_operand_aliasing={{6}: (9, {})} | custom-call | flops 77309411328 | bytes 6291456 | tf_op jit(solution)/shard_map/cond/branch_1_fun/attend/pallas_call | solution.py:1039
  237.0 8.3 %multiply_reduce_fusion.5 = (f32[384]{0:T(512)S(1)}, f32[384,2048]{1,0:T(8,128)S(1)}) fusion(f32[384,2048]{1,0:T(8,128)} %fusion.77.refs_0_, bf16[384,2048]{1,0:T(8,128)(2,1)} %get-tuple-element.135.refs_4_, bf16[2048,2048]{1,0:T(8,128)(2,1)} %bitcast.152, f32[384]{0:T(512)S(1)} %fusion.100), kind=kOutput, calls=%fused_computation.158 | convolution fusion | flops 3224370688 | bytes 16256000 | tf_op jit(solution)/shard_map/cond/branch_1_fun/dot_general | solution.py:1387
  252.5 32.0 %collective-permute-done.10 = bf16[384,2048]{1,0:T(8,128)(2,1)S(1)} collective-permute-done((bf16[384,2048]{1,0:T(8,128)(2,1)}, bf16[384,2048]{1,0:T(8,128)(2,1)S(1)}, u32[]{:S(2)}, u32[]{:S(2)}) %collective-permute-start.10) | collective-permute-done | bytes 1572896 | tf_op jit(solution)/shard_map/cond/branch_1_fun/ppermute | solution.py:1274
  295.3 8.6 %collective-permute-done.11 = bf16[192,2048]{1,0:T(8,128)(2,1)} collective-permute-done((bf16[192,2048]{1,0:T(8,128)(2,1)}, bf16[192,2048]{1,0:T(8,128)(2,1)}, u32[]{:S(2)}, u32[]{:S(2)}) %collective-permute-start.11) | collective-permute-done | bytes 786464 | tf_op jit(solution)/shard_map/cond/branch_1_fun/ppermute | solution.py:1274
  308.6 5.0 all-gather.11.cloned.1.call-done
  313.7 19.7 %mlp_block.9 = (bf16[384,1408]{1,0:T(8,128)(2,1)}, bf16[384,2816]{1,0:T(8,128)(2,1)}, bf16[384,2048]{1,0:T(8,128)(2,1)}, bf16[384,2048]{1,0:T(8,128)(2,1)}) custom-call(s32[1]{0:T(128)} %get-tuple-element.535.live_ref, bf16[384,2048]{1,0:T(8,128)(2,1)} %multiply_convert_fusion.1.rows_ref.refs_3_, ...), custom_call_target="tpu_custom_call" | custom-call | flops 13287555072 | bytes 26738688 | tf_op jit(solution)/shard_map/cond/branch_1_fun/mlp_block/pallas_call | solution.py:131
  333.4 22.3 %mlp_block.11 = (bf16[384,1408]{1,0:T(8,128)(2,1)}, bf16[384,2816]{1,0:T(8,128)(2,1)}, bf16[384,2048]{1,0:T(8,128)(2,1)}, bf16[384,2048]{1,0:T(8,128)(2,1)}) custom-call(s32[1]{0:T(128)} %get-tuple-element.534.live_ref, bf16[384,2048]{1,0:T(8,128)(2,1)} %copy-done.60, bf16[384,2048]{1,0:T(8,128)(2,1)} %get-tuple-element.152.grad_ref.refs_14_, ...), custom_call_target="tpu_custom_call" | custom-call | flops 13287555072 | bytes 26738688 | tf_op jit(solution)/shard_map/cond/branch_1_fun/mlp_block/pallas_call | solution.py:131
  355.7 31.8 %mlp_block.10 = (bf16[768,1408]{1,0:T(8,128)(2,1)}, bf16[768,2816]{1,0:T(8,128)(2,1)}, bf16[768,2048]{1,0:T(8,128)(2,1)}, bf16[768,2048]{1,0:T(8,128)(2,1)}) custom-call(s32[2]{0:T(128)} %gather_fusion.3, bf16[768,2048]{1,0:T(8,128)(2,1)} %copy-done.57, bf16[768,2048]{1,0:T(8,128)(2,1)} %copy-done.56, bf16[2048,1024]{1,0:T(8,128)(2,1)} %bitcast.171, ...), custom_call_target="tpu_custom_call" | custom-call | flops 26575110144 | bytes 36175872 | tf_op jit(solution)/shard_map/cond/branch_1_fun/mlp_block/pallas_call | solution.py:131
  387.4 71.9 %mid_back.1 = (f32[384,2048]{1,0:T(8,128)}, bf16[704,2048]{1,0:T(8,128)(2,1)}, bf16[4,256,2816]{2,1,0:T(8,128)(2,1)}) custom-call(bf16[384,2048]{1,0:T(8,128)(2,1)} %get-tuple-element.146.refs_0_, bf16[768,2048]{1,0:T(8,128)(2,1)} %get-tuple-element.150.refs_1_, bf16[384,2048]{1,0:T(8,128)(2,1)} %get-tuple-element.153.refs_2_, ...), custom_call_target="tpu_custom_call" | custom-call | flops 53150220288 | bytes 42467328 | tf_op jit(solution)/shard_map/cond/branch_1_fun/mid_back/pallas_call | solution.py:822
  462.7 3.4 multiply_reduce_fusion.4
  468.5 2.7 fusion.101.refs_10_
  471.2 10.7 %convolution_convert_fusion.6.refs_2_ = bf16[384,2048]{1,0:T(8,128)(2,1)} fusion(bf16[384,2048]{1,0:T(8,128)(2,1)S(1)} %fusion.101.refs_10_, bf16[2048,2048]{1,0:T(8,128)(2,1)} %bitcast.153), kind=kOutput, calls=%fused_computation.162 | convolution fusion | flops 3222011904 | bytes 11534336 | tf_op jit(solution)/shard_map/cond/branch_1_fun/dot_general | solution.py:1391
  481.8 115.4 %attend_back.3 = (bf16[384,3072]{1,0:T(8,128)(2,1)}, bf16[256,2048]{1,0:T(8,128)(2,1)}, bf16[384,2048]{1,0:T(8,128)(2,1)}, bf16[384,2048]{1,0:T(8,128)(2,1)}) custom-call(bf16[384,2048]{1,0:T(8,128)(2,1)} %get-tuple-element.144.refs_0_, bf16[1536,1024]{1,0:T(8,128)(2,1)} %get-tuple-element.145.refs_1_, bf16[384,2048]{1,0:T(8,128)(2,1)} %convolution_convert_fusion.6.refs_2_, ...), custom_call_target="tpu_custom_call" | custom-call | flops 86973087744 | bytes 12582912 | tf_op jit(solution)/shard_map/cond/branch_1_fun/attend_back/pallas_call | solution.py:1204
  597.3 5.2 convolution_convert_fusion.5
  602.5 9.0 %reduce-scatter.9.cloned.1.call-done.pieces_ref = bf16[4,64,2816]{2,1,0:T(8,128)(2,1)} async-done(((bf16[4,256,2816]{2,1,0:T(8,128)(2,1)}), bf16[4,64,2816]{2,1,0:T(8,128)(2,1)}) %reduce-scatter.9.cloned.1.call-update) | async-done | bytes 1441808 | tf_op jit(solution)/shard_map/cond/branch_1_fun/reduce_scatter | solution.py:1524
  611.5 98.4 %qkv_back.3 = (f32[64,3072]{1,0:T(8,128)}, f32[384,2048]{1,0:T(8,128)}, f32[64,11264]{1,0:T(8,128)}, f32[64,2048]{1,0:T(8,128)}) custom-call(bf16[384,2048]{1,0:T(8,128)(2,1)} %get-tuple-element.167.normed_ref, bf16[384,3072]{1,0:T(8,128)(2,1)} %get-tuple-element.171.grad_ref, bf16[2048,3072]{1,0:T(8,128)(2,1)} %bitcast.147, ...), custom_call_target="tpu_custom_call" | custom-call | flops 115964116992 | bytes 18874368 | tf_op jit(solution)/shard_map/cond/branch_1_fun/qkv_back/pallas_call | solution.py:649
  710.0 2.6 multiply_reduce_fusion.3
  713.8 6.1 convolution_convert_fusion.4
  725.0 2.6 add_multiply_fusion.4
  730.3 4.2 add_multiply_fusion.2
  736.0 4.5 add_multiply_fusion.1
  (221 shorter events, 65.8 us)
Async XLA Ops:
  7.2 110.0 %copy-start.78 = (s32[2,1024]{1,0:T(2,128)S(1)}, s32[2,1024]{1,0:T(2,128)}, u32[]{:S(2)}) copy-start(s32[2,1024]{1,0:T(2,128)} %param.27) | copy-start | bytes 24580
  12.0 105.2 %copy-start.94 = (bf16[2,64]{1,0:T(2,128)(2,1)}, bf16[2,64]{1,0:T(2,128)(2,1)S(1)}, u32[]{:S(2)}) copy-start(bf16[2,64]{1,0:T(2,128)(2,1)S(1)} %convert_element_type.213) | copy-start | bytes 772
  117.2 607.8 %copy-start.7 = (f32[64,2048]{1,0:T(8,128)S(1)}, f32[64,2048]{1,0:T(8,128)}, u32[]{:S(2)}) copy-start(f32[64,2048]{1,0:T(8,128)} %out_ref.1) | copy-start | bytes 1572868
  125.8 11.3 %copy-start.39 = (bf16[2,256,2048]{2,1,0:T(8,128)(2,1)S(1)}, bf16[2,256,2048]{2,1,0:T(8,128)(2,1)}, u32[]{:S(2)}) copy-start(bf16[2,256,2048]{2,1,0:T(8,128)(2,1)} %get-tuple-element.259) | copy-start | bytes 6291460 | tf_op jit(solution)/shard_map/conditional.1
  125.8 182.8 %all-gather.9.cloned.1.call-start = ((), (), s32[]{:S(2)}) async-start(), calls=%async_computation.8 | async-start | bytes 4718592 | tf_op jit(solution)/shard_map/cond/branch_1_fun/all_gather | solution.py:1335
  127.9 185.8 %all-gather.11.cloned.1.call-start = ((), (), s32[]{:S(2)}) async-start(), calls=%async_computation.9 | async-start | bytes 8257536 | tf_op jit(solution)/shard_map/cond/branch_1_fun/all_gather | solution.py:1335
  142.0 94.2 %copy-start.13 = (f32[384,128]{1,0:T(8,128)}, f32[384,128]{1,0:T(8,128)S(1)}, u32[]{:S(2)}) copy-start(f32[384,128]{1,0:T(8,128)S(1)} %pad_maximum_fusion.6.refs_3_.refs_9_) | copy-start | bytes 589828 | tf_op jit(solution)/shard_map/conditional.1
  142.7 93.5 %copy-start.16 = (s32[1,384]{1,0:T(1,128)}, s32[1,384]{1,0:T(1,128)S(1)}, u32[]{:S(2)}) copy-start(s32[1,384]{1,0:T(1,128)S(1)} %get-tuple-element.530.refs_7_) | copy-start | bytes 4612 | tf_op jit(solution)/shard_map/conditional.1
  142.7 93.5 %copy-start.17 = (s32[1,384]{1,0:T(1,128)}, s32[1,384]{1,0:T(1,128)S(1)}, u32[]{:S(2)}) copy-start(s32[1,384]{1,0:T(1,128)S(1)} %get-tuple-element.531.refs_6_) | copy-start | bytes 4612 | tf_op jit(solution)/shard_map/conditional.1
  236.2 375.3 %reduce-scatter.9.cloned.1.call-start = ((), (), s32[]{:S(2)}) async-start(), calls=%async_computation.10 | async-start | bytes 7208960 | tf_op jit(solution)/shard_map/cond/branch_1_fun/reduce_scatter | solution.py:1524
  236.3 229.8 %copy-start.68 = (f32[2048]{0:T(1024)}, f32[2048]{0:T(1024)S(1)}, u32[]{:S(2)}) copy-start(f32[2048]{0:T(1024)S(1)} %mul.468) | copy-start | bytes 24580 | tf_op jit(solution)/shard_map/conditional.1
  245.3 220.8 %copy-start.84 = (f32[384]{0:T(512)}, f32[384]{0:T(512)S(1)}, u32[]{:S(2)}) copy-start(f32[384]{0:T(512)S(1)} %add_rsqrt_fusion.1) | copy-start | bytes 4612 | tf_op jit(solution)/shard_map/conditional.1
  248.4 36.0 %collective-permute-start.10 = (bf16[384,2048]{1,0:T(8,128)(2,1)}, bf16[384,2048]{1,0:T(8,128)(2,1)S(1)}, u32[]{:S(2)}, u32[]{:S(2)}) collective-permute-start(bf16[384,2048]{1,0:T(8,128)(2,1)} %multiply_convert_fusion.1.rows_ref.refs_3_), channel_id=1, source_target_pairs={{0,16},{1,17},{2,18},{3,19},{4,20},{5,21},{6,22},{7,23},{8,24},{9,... | collective-permute-start | bytes 4718600 | tf_op jit(solution)/shard_map/cond/branch_1_fun/ppermute | solution.py:1274
  248.9 38.2 %collective-permute-start.9 = (bf16[384,2048]{1,0:T(8,128)(2,1)}, bf16[384,2048]{1,0:T(8,128)(2,1)}, u32[]{:S(2)}, u32[]{:S(2)}) collective-permute-start(bf16[384,2048]{1,0:T(8,128)(2,1)} %multiply_convert_fusion.1.rows_ref.refs_3_), channel_id=1, source_target_pairs={{0,8},{1,9},{2,10},{3,11},{4,12},{5,13},{6,14},{7,15},{8,0},{9,1},... | collective-permute-start | bytes 4718600 | tf_op jit(solution)/shard_map/cond/branch_1_fun/ppermute | solution.py:1274
  252.3 38.5 %copy-start.99 = (s32[2]{0:T(128)S(1)}, s32[2]{0:T(128)}, u32[]{:S(2)}) copy-start(s32[2]{0:T(128)} %constant.361) | copy-start | bytes 28 | tf_op jit(solution)/shard_map/conditional.1
  252.5 33.4 %copy-start.56 = (bf16[768,2048]{1,0:T(8,128)(2,1)}, bf16[768,2048]{1,0:T(8,128)(2,1)S(1)}, u32[]{:S(2)}) copy-start(bf16[768,2048]{1,0:T(8,128)(2,1)S(1)} %constant_dynamic-update-slice_fusion.7.grad_ref.refs_13_) | copy-start | bytes 9437188 | tf_op jit(solution)/shard_map/conditional.1
  285.4 18.5 %collective-permute-start.11 = (bf16[192,2048]{1,0:T(8,128)(2,1)}, bf16[192,2048]{1,0:T(8,128)(2,1)}, u32[]{:S(2)}, u32[]{:S(2)}) collective-permute-start(bf16[192,2048]{1,0:T(8,128)(2,1)} %slice.112), channel_id=1, source_target_pairs={{0,8},{1,9},{2,10},{3,11},{4,12},{5,13},{6,14},{7,15},{8,0},{9,1},... | collective-permute-start | bytes 2359304 | tf_op jit(solution)/shard_map/cond/branch_1_fun/ppermute | solution.py:1274
  289.2 18.2 %collective-permute-start.12 = (bf16[192,2048]{1,0:T(8,128)(2,1)}, bf16[192,2048]{1,0:T(8,128)(2,1)}, u32[]{:S(2)}, u32[]{:S(2)}) collective-permute-start(bf16[192,2048]{1,0:T(8,128)(2,1)} %slice.113), channel_id=1, source_target_pairs={{0,16},{1,17},{2,18},{3,19},{4,20},{5,21},{6,22},{7,23},{8,24},{9,... | collective-permute-start | bytes 2359304 | tf_op jit(solution)/shard_map/cond/branch_1_fun/ppermute | solution.py:1274
  308.6 24.8 %copy-start.60 = (bf16[384,2048]{1,0:T(8,128)(2,1)}, bf16[384,2048]{1,0:T(8,128)(2,1)S(1)}, u32[]{:S(2)}) copy-start(bf16[384,2048]{1,0:T(8,128)(2,1)S(1)} %constant_dynamic-update-slice_fusion.9.rows_ref.refs_5_) | copy-start | bytes 4718596 | tf_op jit(solution)/shard_map/conditional.1
  459.4 263.0 %reduce-scatter.11.cloned.1.call-start = ((), (), s32[]{:S(2)}) async-start(), calls=%async_computation.11 | async-start | bytes 3604480 | tf_op jit(solution)/shard_map/cond/branch_1_fun/reduce_scatter | solution.py:1550
  481.8 115.5 %copy-start.71 = (s32[512]{0:T(512)S(1)}, s32[512]{0:T(512)}, u32[]{:S(2)}) copy-start(s32[512]{0:T(512)} %copy-done.70) | copy-start | bytes 6148 | tf_op jit(solution)/shard_map/conditional.1
  481.8 115.5 %copy-start.82 = (pred[512]{0:T(512)(128)(4,1)S(1)}, pred[512]{0:T(512)(128)(4,1)}, u32[]{:S(2)}) copy-start(pred[512]{0:T(512)(128)(4,1)} %copy-done.81) | copy-start | bytes 1540 | tf_op jit(solution)/shard_map/conditional.1
  611.5 98.4 %copy-start.32 = (f32[384,2048]{1,0:T(8,128)S(1)}, f32[384,2048]{1,0:T(8,128)}, u32[]{:S(2)}) copy-start(f32[384,2048]{1,0:T(8,128)} %fusion.77.refs_0_) | copy-start | bytes 9437188 | tf_op jit(solution)/shard_map/conditional.1
  611.5 98.4 %copy-start.83 = (f32[2048]{0:T(1024)S(1)}, f32[2048]{0:T(1024)}, u32[]{:S(2)}) copy-start(f32[2048]{0:T(1024)} %mul.480) | copy-start | bytes 24580 | tf_op jit(solution)/shard_map/conditional.1
  (46 other events, 196.1 us)
Sparse Core Ops, SparseCore 0:
  128.8 58.4 all-gather.8
  236.3 77.2 all-gather.10
  459.5 151.9 reduce-scatter.8
  613.7 71.2 reduce-scatter.10

commit v5 on v4

--- a/solution.py
+++ b/solution.py
@@ -41,6 +41,10 @@
 
 def unit_groups(units):
     return [(low, min(low + UNIT_GROUP, units)) for low in range(0, units, UNIT_GROUP)]
+
+
+def first_columns(units):
+    return 2 * UNIT_GROUP * max(units // UNIT_GROUP * 2 // 5, 1)
 
 
 def mlp_kernel(
@@ -281,8 +285,8 @@
 
 
 def gather_kernel(
-    n, qkv_ref, out_ref, gateup_ref, down_ref, ext_ref, qkv_all, out_all, ext_all, came, down_all,
-    qkv_low, out_low, trade_low, down_low, send_sems, recv_sems, local_sems,
+    n, qkv_ref, out_ref, gateup_ref, down_ref, ext_ref, qkv_all, out_all, ext_all, came_first, came_last,
+    down_all, qkv_low, out_low, trade_low, down_low, send_sems, recv_sems, local_sems,
 ):
     p = Place(n)
     c = Copies(send_sems, recv_sems)
@@ -314,9 +318,14 @@
         for first, last in unit_groups(units):
             for to, start in ((2 * first, k * units), (first + last, gateup_ref.shape[1] // 2 + k * units)):
                 trade_low[k, :, to : to + last - first] = gateup_ref[:, start + first : start + last].astype(low)
-    place(trade_low.at[t], came.at[t])
+    cut = came_first.shape[2]
+    halves = ((slice(0, cut), came_first), (slice(cut, 2 * units), came_last))
+    for cols, came in halves:
+        place(trade_low.at[t, :, cols], came.at[t])
     trade = [
-        c.make(trade_low.at[k], came.at[t], to) for k, to in ((p.t_x, p.by_x), (p.t_y, p.by_y), (p.t_d, p.by_d))
+        c.make(trade_low.at[k, :, cols], came.at[t], to)
+        for cols, came in halves
+        for k, to in ((p.t_x, p.by_x), (p.t_y, p.by_y), (p.t_d, p.by_d))
     ]
     c.go(trade)
     out_low[...] = out_ref[...].astype(low)
@@ -384,18 +393,20 @@
     rows = qkv.shape[0]
     part = gateup.shape[1] // planes
     low = jnp.bfloat16
-    copies = 64
+    copies = 72
+    cut = first_columns(part // 2)
     return pl.pallas_call(
         functools.partial(gather_kernel, n),
         out_shape=(
             jax.ShapeDtypeStruct((planes, 2, n, rows, qkv.shape[1]), low),
             jax.ShapeDtypeStruct((planes, 2, n, rows, out.shape[1]), low),
             jax.ShapeDtypeStruct((planes, 2, n) + ext.shape, low),
-            jax.ShapeDtypeStruct((planes, rows, part), low),
+            jax.ShapeDtypeStruct((planes, rows, cut), low),
+            jax.ShapeDtypeStruct((planes, rows, part - cut), low),
             jax.ShapeDtypeStruct((2, n) + down.shape, low),
         ),
         in_specs=[pl.BlockSpec(memory_space=pltpu.VMEM)] * 5,
-        out_specs=(any_spec,) * 5,
+        out_specs=(any_spec,) * 6,
         scratch_shapes=[
             pltpu.VMEM(qkv.shape, low),
             pltpu.VMEM(out.shape, low),
@@ -1357,7 +1368,7 @@
             digits = jnp.stack([count // 16, count % 16]).astype(low)
             ext = jnp.concatenate([gains.reshape(1, 2 * rows), jnp.zeros((15, 2 * rows), gains.dtype)])
             ext = lax.dynamic_update_slice(ext, digits[None], (1, 0))
-            qkv_all, out_all, ext_all, came, down_all = gather_first(
+            qkv_all, out_all, ext_all, *came, down_all = gather_first(
                 qkv, out, gateup, down, ext, self.planes, self.n
             )
             ext_all = ext_all.reshape(self.wide * self.n, 16, 2 * rows)
@@ -1371,10 +1382,12 @@
                 gain_full,
                 digits[:, 0] * 16 + digits[:, 1],
             )
+        came = self.trade_columns(split_columns(gateup.astype(low), self.planes))
+        cut = first_columns(came.shape[2] // 2)
         return (
             lax.all_gather(qkv.astype(low), MESH_AXES, axis=0, tiled=True),
             lax.all_gather(out.astype(low), MESH_AXES, axis=0, tiled=True),
-            self.trade_columns(split_columns(gateup.astype(low), self.planes)),
+            (came[:, :, :cut], came[:, :, cut:]),
             lax.all_gather(
                 down.astype(low), MESH_AXES, axis=0, tiled=True, axis_index_groups=self.same_chip
             ),
@@ -1443,12 +1456,11 @@
     seq_len = n * span_len
     kv_width = KV_HEADS * HEAD_DIM
     ff_part = FF // planes
-    shard_rows = pieces.shape[1]
+    shard_rows = pieces[0].shape[1]
     low = jnp.bfloat16
 
 
-    first_cols = 2 * UNIT_GROUP * max(ff_part // UNIT_GROUP * 2 // 5, 1)
-    gateup_first = links.gather_chip(pieces[:, :, :first_cols])
+    gateup_first = links.gather_chip(pieces[0])
 
     def codes_of(block):
         mask = lax.dynamic_slice_in_dim(active, jnp.maximum(block, 0) * span_len, span_len, 1)
@@ -1489,7 +1501,7 @@
         )
         down_grad_blocks = [down_grad, *others]
         out_low = out_all.reshape(width, width)
-    pieces_last, attended_low = lax.optimization_barrier((pieces[:, :, first_cols:], attended_low))
+    pieces_last, attended_low = lax.optimization_barrier((pieces[1], attended_low))
     gateup_last = links.gather_chip(pieces_last)
     middle = inputs + live_rows * dot32(attended_low, out_low)
     normed_mid, inverse_two = norm_forward(middle, gain_full[1])

time: 761 us -> 764 us (level)
  transfers between devices with their start and end apart: 8 -> 8, of which waited for: 5 -> 5; matrix products, arithmetic and copies ran while one was open for 10% -> 10% of each run, Pallas kernels for 41% -> 40%
where the time goes in v5:
time: 764 us; the launch traced here: 756 us
  Pallas kernels  556 us (73%)
  waiting for transfers between devices  59 us (8%)
  other arithmetic  41.8 us (5%)
  matrix products  37 us (5%)
  local copies, waits for them, and re-layouts  31.1 us (4%)
  between operations  17.4 us (2%)
  loops' own time  9.44 us (1%)
    pallas_call x1, Pallas kernels, attend_back(): pl.pallas_call(functools.partial(attend_back_kernel, n, parts), in_specs=...  114 us
    pallas_call x1, Pallas kernels, qkv_back(): pl.pallas_call(functools.partial(qkv_back_kernel, n, parts), in_specs=[in...  98.4 us
    pallas_call x1, Pallas kernels, gather_first(): pl.pallas_call(functools.partial(gather_kernel, n), out_shape=(jax.ShapeD...  98.3 us
    pallas_call x1, Pallas kernels, attend(): pl.pallas_call(functools.partial(attend_kernel, n, out_all is not None),...  93.3 us
    pallas_call x3, Pallas kernels, mlp_block(): pl.pallas_call(functools.partial(mlp_kernel, cap, counts), grid_spec=pltp...  78.5 us
    pallas_call x1, Pallas kernels, mid_back(): pl.pallas_call(functools.partial(mid_back_kernel, n, cap, units), in_spec...  74.1 us
    ppermute x4, waiting for transfers between devices, swap(): return lax.ppermute(values, MESH_AXES, pairs)  43.2 us
  transfers between devices with their start and end apart: 8, of which 5 were waited for; matrix products, arithmetic and copies ran while one was open for 10% of the time, Pallas kernels for 40%

profile of v5, /device:TPU:0, one launch (start us, length us, event | category | flops | bytes accessed | tf_op | source)
XLA Modules:
  0.0 756.3 jit_solution(5214301166908048240)
XLA Ops:
  17.5 98.3 %gather_first.1 = (bf16[4,2,4,64,3072]{4,3,2,1,0:T(8,128)(2,1)}, bf16[4,2,4,64,2048]{4,3,2,1,0:T(8,128)(2,1)}, bf16[4,2,4,16,128]{4,3,2,1,0:T(8,128)(2,1)S(1)}, ...) custom-call(f32[64,3072]{1,0:T(8,128)S(1)} %copy-done.4, ...), custom_call_target="tpu_custom_call" | custom-call | tf_op jit(solution)/shard_map/gather_first/pallas_call | solution.py:398
  117.4 612.7 %conditional.3 = (bf16[2,256,2048]{2,1,0:T(8,128)(2,1)}, bf16[2,256,2048]{2,1,0:T(8,128)(2,1)}, f32[64,3072]{1,0:T(8,128)}, f32[64,2048]{1,0:T(8,128)S(1)}, f32[64,11264]{1,0:T(8,128)}, /*index=5*/f32[176,2048]{1,0:T(8,128)}) conditional(s32[]{:T(128)} %convert_element_type.216, (s32[]{:T(128)}, s32[2,1024]{1,0:T(2,128)S(1)}, ...), branch_computations={%region_2.20_spmd, %region_20.38_spmd} | conditional | flops 566066282496 | bytes 812538560
  133.6 4.2 convolution_convert_fusion.7.refs_8_.grad_ref.refs_12_
  137.8 2.7 fusion.77.refs_0_
  141.3 93.3 %attend.3 = (bf16[384,2048]{1,0:T(8,128)(2,1)}, f32[384,1]{1,0:T(8,128)S(1)}, bf16[384,2048]{1,0:T(8,128)(2,1)}, bf16[384,2048]{1,0:T(8,128)(2,1)}, f32[4,4,384]...) custom-call(f32[384,2048]{1,0:T(8,128)} %fusion.77.refs_0_, ...), custom_call_target="tpu_custom_call", output_to_operand_aliasing={{6}: (9, {})} | custom-call | flops 77309411328 | bytes 6291456 | tf_op jit(solution)/shard_map/cond/branch_1_fun/attend/pallas_call | solution.py:1050
  235.5 8.3 %multiply_reduce_fusion.5 = (f32[384]{0:T(512)S(1)}, f32[384,2048]{1,0:T(8,128)S(1)}) fusion(f32[384,2048]{1,0:T(8,128)} %fusion.77.refs_0_, bf16[384,2048]{1,0:T(8,128)(2,1)} %get-tuple-element.140.refs_4_, bf16[2048,2048]{1,0:T(8,128)(2,1)} %bitcast.152, f32[384]{0:T(512)S(1)} %fusion.100), kind=kOutput, calls=%fused_computation.158 | convolution fusion | flops 3224370688 | bytes 16256000 | tf_op jit(solution)/shard_map/cond/branch_1_fun/dot_general | solution.py:1400
  251.1 32.0 %collective-permute-done.10 = bf16[384,2048]{1,0:T(8,128)(2,1)S(1)} collective-permute-done((bf16[384,2048]{1,0:T(8,128)(2,1)}, bf16[384,2048]{1,0:T(8,128)(2,1)S(1)}, u32[]{:S(2)}, u32[]{:S(2)}) %collective-permute-start.10) | collective-permute-done | bytes 1572896 | tf_op jit(solution)/shard_map/cond/branch_1_fun/ppermute | solution.py:1285
  293.9 8.8 %collective-permute-done.11 = bf16[192,2048]{1,0:T(8,128)(2,1)} collective-permute-done((bf16[192,2048]{1,0:T(8,128)(2,1)}, bf16[192,2048]{1,0:T(8,128)(2,1)}, u32[]{:S(2)}, u32[]{:S(2)}) %collective-permute-start.11) | collective-permute-done | bytes 786464 | tf_op jit(solution)/shard_map/cond/branch_1_fun/ppermute | solution.py:1285
  307.5 5.3 all-gather.11.cloned.1.call-done
  312.9 21.8 %mlp_block.9 = (bf16[384,1408]{1,0:T(8,128)(2,1)}, bf16[384,2816]{1,0:T(8,128)(2,1)}, bf16[384,2048]{1,0:T(8,128)(2,1)}, bf16[384,2048]{1,0:T(8,128)(2,1)}) custom-call(s32[1]{0:T(128)} %get-tuple-element.547.live_ref, bf16[384,2048]{1,0:T(8,128)(2,1)} %multiply_convert_fusion.1.rows_ref.refs_3_, ...), custom_call_target="tpu_custom_call" | custom-call | flops 13287555072 | bytes 26738688 | tf_op jit(solution)/shard_map/cond/branch_1_fun/mlp_block/pallas_call | solution.py:135
  334.6 20.0 %mlp_block.11 = (bf16[384,1408]{1,0:T(8,128)(2,1)}, bf16[384,2816]{1,0:T(8,128)(2,1)}, bf16[384,2048]{1,0:T(8,128)(2,1)}, bf16[384,2048]{1,0:T(8,128)(2,1)}) custom-call(s32[1]{0:T(128)} %get-tuple-element.546.live_ref, bf16[384,2048]{1,0:T(8,128)(2,1)} %copy-done.59, bf16[384,2048]{1,0:T(8,128)(2,1)} %get-tuple-element.158.grad_ref.refs_14_, ...), custom_call_target="tpu_custom_call" | custom-call | flops 13287555072 | bytes 26738688 | tf_op jit(solution)/shard_map/cond/branch_1_fun/mlp_block/pallas_call | solution.py:135
  354.7 36.7 %mlp_block.10 = (bf16[768,1408]{1,0:T(8,128)(2,1)}, bf16[768,2816]{1,0:T(8,128)(2,1)}, bf16[768,2048]{1,0:T(8,128)(2,1)}, bf16[768,2048]{1,0:T(8,128)(2,1)}) custom-call(s32[2]{0:T(128)} %gather_fusion.3, bf16[768,2048]{1,0:T(8,128)(2,1)} %copy-done.56, bf16[768,2048]{1,0:T(8,128)(2,1)} %copy-done.55, bf16[2048,1024]{1,0:T(8,128)(2,1)} %bitcast.171, ...), custom_call_target="tpu_custom_call" | custom-call | flops 26575110144 | bytes 36175872 | tf_op jit(solution)/shard_map/cond/branch_1_fun/mlp_block/pallas_call | solution.py:135
  391.4 74.1 %mid_back.1 = (f32[384,2048]{1,0:T(8,128)}, bf16[704,2048]{1,0:T(8,128)(2,1)}, bf16[4,256,2816]{2,1,0:T(8,128)(2,1)}) custom-call(bf16[384,2048]{1,0:T(8,128)(2,1)} %get-tuple-element.152.refs_0_, bf16[768,2048]{1,0:T(8,128)(2,1)} %get-tuple-element.156.refs_1_, bf16[384,2048]{1,0:T(8,128)(2,1)} %get-tuple-element.159.refs_2_, ...), custom_call_target="tpu_custom_call" | custom-call | flops 53150220288 | bytes 42467328 | tf_op jit(solution)/shard_map/cond/branch_1_fun/mid_back/pallas_call | solution.py:833
  468.9 3.9 multiply_reduce_fusion.4
  474.7 2.7 fusion.101.refs_10_
  477.4 10.7 %convolution_convert_fusion.6.refs_2_ = bf16[384,2048]{1,0:T(8,128)(2,1)} fusion(bf16[384,2048]{1,0:T(8,128)(2,1)S(1)} %fusion.101.refs_10_, bf16[2048,2048]{1,0:T(8,128)(2,1)} %bitcast.153), kind=kOutput, calls=%fused_computation.162 | convolution fusion | flops 3222011904 | bytes 11534336 | tf_op jit(solution)/shard_map/cond/branch_1_fun/dot_general | solution.py:1404
  488.0 113.7 %attend_back.3 = (bf16[384,3072]{1,0:T(8,128)(2,1)}, bf16[256,2048]{1,0:T(8,128)(2,1)}, bf16[384,2048]{1,0:T(8,128)(2,1)}, bf16[384,2048]{1,0:T(8,128)(2,1)}) custom-call(bf16[384,2048]{1,0:T(8,128)(2,1)} %get-tuple-element.150.refs_0_, bf16[1536,1024]{1,0:T(8,128)(2,1)} %get-tuple-element.151.refs_1_, bf16[384,2048]{1,0:T(8,128)(2,1)} %convolution_convert_fusion.6.refs_2_, ...), custom_call_target="tpu_custom_call" | custom-call | flops 86973087744 | bytes 12582912 | tf_op jit(solution)/shard_map/cond/branch_1_fun/attend_back/pallas_call | solution.py:1215
  601.8 5.2 convolution_convert_fusion.5
  606.9 9.7 %reduce-scatter.9.cloned.1.call-done.pieces_ref = bf16[4,64,2816]{2,1,0:T(8,128)(2,1)} async-done(((bf16[4,256,2816]{2,1,0:T(8,128)(2,1)}), bf16[4,64,2816]{2,1,0:T(8,128)(2,1)}) %reduce-scatter.9.cloned.1.call-update) | async-done | bytes 1441808 | tf_op jit(solution)/shard_map/cond/branch_1_fun/reduce_scatter | solution.py:1536
  616.7 98.4 %qkv_back.3 = (f32[64,3072]{1,0:T(8,128)}, f32[384,2048]{1,0:T(8,128)}, f32[64,11264]{1,0:T(8,128)}, f32[64,2048]{1,0:T(8,128)}) custom-call(bf16[384,2048]{1,0:T(8,128)(2,1)} %get-tuple-element.173.normed_ref, bf16[384,3072]{1,0:T(8,128)(2,1)} %get-tuple-element.177.grad_ref, bf16[2048,3072]{1,0:T(8,128)(2,1)} %bitcast.147, ...), custom_call_target="tpu_custom_call" | custom-call | flops 115964116992 | bytes 18874368 | tf_op jit(solution)/shard_map/cond/branch_1_fun/qkv_back/pallas_call | solution.py:660
  719.0 6.1 convolution_convert_fusion.4
  730.2 2.6 add_multiply_fusion.4
  735.5 4.2 add_multiply_fusion.2
  741.2 4.5 add_multiply_fusion.1
  (217 shorter events, 62.3 us)
Async XLA Ops:
  7.2 110.2 %copy-start.77 = (s32[2,1024]{1,0:T(2,128)S(1)}, s32[2,1024]{1,0:T(2,128)}, u32[]{:S(2)}) copy-start(s32[2,1024]{1,0:T(2,128)} %param.27) | copy-start | bytes 24580
  12.0 105.3 %copy-start.93 = (bf16[2,64]{1,0:T(2,128)(2,1)}, bf16[2,64]{1,0:T(2,128)(2,1)S(1)}, u32[]{:S(2)}) copy-start(bf16[2,64]{1,0:T(2,128)(2,1)S(1)} %convert_element_type.213) | copy-start | bytes 772
  117.4 612.8 %copy-start.7 = (f32[64,2048]{1,0:T(8,128)S(1)}, f32[64,2048]{1,0:T(8,128)}, u32[]{:S(2)}) copy-start(f32[64,2048]{1,0:T(8,128)} %out_ref.1) | copy-start | bytes 1572868
  125.9 181.6 %all-gather.9.cloned.1.call-start = ((), (), s32[]{:S(2)}) async-start(), calls=%async_computation.8 | async-start | bytes 4718592 | tf_op jit(solution)/shard_map/cond/branch_1_fun/all_gather | solution.py:1346
  126.6 186.2 %all-gather.11.cloned.1.call-start = ((), (), s32[]{:S(2)}) async-start(), calls=%async_computation.9 | async-start | bytes 8257536 | tf_op jit(solution)/shard_map/cond/branch_1_fun/all_gather | solution.py:1346
  140.6 94.1 %copy-start.13 = (f32[384,128]{1,0:T(8,128)}, f32[384,128]{1,0:T(8,128)S(1)}, u32[]{:S(2)}) copy-start(f32[384,128]{1,0:T(8,128)S(1)} %pad_maximum_fusion.6.refs_3_.refs_9_) | copy-start | bytes 589828 | tf_op jit(solution)/shard_map/conditional.1
  141.3 93.4 %copy-start.16 = (s32[1,384]{1,0:T(1,128)}, s32[1,384]{1,0:T(1,128)S(1)}, u32[]{:S(2)}) copy-start(s32[1,384]{1,0:T(1,128)S(1)} %get-tuple-element.542.refs_7_) | copy-start | bytes 4612 | tf_op jit(solution)/shard_map/conditional.1
  141.3 93.4 %copy-start.17 = (s32[1,384]{1,0:T(1,128)}, s32[1,384]{1,0:T(1,128)S(1)}, u32[]{:S(2)}) copy-start(s32[1,384]{1,0:T(1,128)S(1)} %get-tuple-element.543.refs_6_) | copy-start | bytes 4612 | tf_op jit(solution)/shard_map/conditional.1
  234.7 381.9 %reduce-scatter.9.cloned.1.call-start = ((), (), s32[]{:S(2)}) async-start(), calls=%async_computation.10 | async-start | bytes 7208960 | tf_op jit(solution)/shard_map/cond/branch_1_fun/reduce_scatter | solution.py:1536
  234.9 237.9 %copy-start.67 = (f32[2048]{0:T(1024)}, f32[2048]{0:T(1024)S(1)}, u32[]{:S(2)}) copy-start(f32[2048]{0:T(1024)S(1)} %mul.468) | copy-start | bytes 24580 | tf_op jit(solution)/shard_map/conditional.1
  243.8 228.9 %copy-start.83 = (f32[384]{0:T(512)}, f32[384]{0:T(512)S(1)}, u32[]{:S(2)}) copy-start(f32[384]{0:T(512)S(1)} %add_rsqrt_fusion.1) | copy-start | bytes 4612 | tf_op jit(solution)/shard_map/conditional.1
  246.9 36.2 %collective-permute-start.10 = (bf16[384,2048]{1,0:T(8,128)(2,1)}, bf16[384,2048]{1,0:T(8,128)(2,1)S(1)}, u32[]{:S(2)}, u32[]{:S(2)}) collective-permute-start(bf16[384,2048]{1,0:T(8,128)(2,1)} %multiply_convert_fusion.1.rows_ref.refs_3_), channel_id=1, source_target_pairs={{0,16},{1,17},{2,18},{3,19},{4,20},{5,21},{6,22},{7,23},{8,24},{9,... | collective-permute-start | bytes 4718600 | tf_op jit(solution)/shard_map/cond/branch_1_fun/ppermute | solution.py:1285
  247.5 38.4 %collective-permute-start.9 = (bf16[384,2048]{1,0:T(8,128)(2,1)}, bf16[384,2048]{1,0:T(8,128)(2,1)}, u32[]{:S(2)}, u32[]{:S(2)}) collective-permute-start(bf16[384,2048]{1,0:T(8,128)(2,1)} %multiply_convert_fusion.1.rows_ref.refs_3_), channel_id=1, source_target_pairs={{0,8},{1,9},{2,10},{3,11},{4,12},{5,13},{6,14},{7,15},{8,0},{9,1},... | collective-permute-start | bytes 4718600 | tf_op jit(solution)/shard_map/cond/branch_1_fun/ppermute | solution.py:1285
  250.9 38.5 %copy-start.98 = (s32[2]{0:T(128)S(1)}, s32[2]{0:T(128)}, u32[]{:S(2)}) copy-start(s32[2]{0:T(128)} %constant.361) | copy-start | bytes 28 | tf_op jit(solution)/shard_map/conditional.1
  251.1 33.5 %copy-start.55 = (bf16[768,2048]{1,0:T(8,128)(2,1)}, bf16[768,2048]{1,0:T(8,128)(2,1)S(1)}, u32[]{:S(2)}) copy-start(bf16[768,2048]{1,0:T(8,128)(2,1)S(1)} %constant_dynamic-update-slice_fusion.7.grad_ref.refs_13_) | copy-start | bytes 9437188 | tf_op jit(solution)/shard_map/conditional.1
  284.1 18.6 %collective-permute-start.11 = (bf16[192,2048]{1,0:T(8,128)(2,1)}, bf16[192,2048]{1,0:T(8,128)(2,1)}, u32[]{:S(2)}, u32[]{:S(2)}) collective-permute-start(bf16[192,2048]{1,0:T(8,128)(2,1)} %slice.100), channel_id=1, source_target_pairs={{0,8},{1,9},{2,10},{3,11},{4,12},{5,13},{6,14},{7,15},{8,0},{9,1},... | collective-permute-start | bytes 2359304 | tf_op jit(solution)/shard_map/cond/branch_1_fun/ppermute | solution.py:1285
  287.9 18.4 %collective-permute-start.12 = (bf16[192,2048]{1,0:T(8,128)(2,1)}, bf16[192,2048]{1,0:T(8,128)(2,1)}, u32[]{:S(2)}, u32[]{:S(2)}) collective-permute-start(bf16[192,2048]{1,0:T(8,128)(2,1)} %slice.101), channel_id=1, source_target_pairs={{0,16},{1,17},{2,18},{3,19},{4,20},{5,21},{6,22},{7,23},{8,24},{9,... | collective-permute-start | bytes 2359304 | tf_op jit(solution)/shard_map/cond/branch_1_fun/ppermute | solution.py:1285
  307.5 27.1 %copy-start.59 = (bf16[384,2048]{1,0:T(8,128)(2,1)}, bf16[384,2048]{1,0:T(8,128)(2,1)S(1)}, u32[]{:S(2)}) copy-start(bf16[384,2048]{1,0:T(8,128)(2,1)S(1)} %constant_dynamic-update-slice_fusion.9.rows_ref.refs_5_) | copy-start | bytes 4718596 | tf_op jit(solution)/shard_map/conditional.1
  465.6 262.0 %reduce-scatter.11.cloned.1.call-start = ((), (), s32[]{:S(2)}) async-start(), calls=%async_computation.11 | async-start | bytes 3604480 | tf_op jit(solution)/shard_map/cond/branch_1_fun/reduce_scatter | solution.py:1562
  477.4 10.7 %copy-start.51 = (bf16[384,2048]{1,0:T(8,128)(2,1)}, bf16[384,2048]{1,0:T(8,128)(2,1)S(1)}, u32[]{:S(2)}) copy-start(bf16[384,2048]{1,0:T(8,128)(2,1)S(1)} %fusion.101.refs_10_) | copy-start | bytes 4718596 | tf_op jit(solution)/shard_map/conditional.1
  488.0 113.7 %copy-start.70 = (s32[512]{0:T(512)S(1)}, s32[512]{0:T(512)}, u32[]{:S(2)}) copy-start(s32[512]{0:T(512)} %copy-done.69) | copy-start | bytes 6148 | tf_op jit(solution)/shard_map/conditional.1
  488.0 113.7 %copy-start.81 = (pred[512]{0:T(512)(128)(4,1)S(1)}, pred[512]{0:T(512)(128)(4,1)}, u32[]{:S(2)}) copy-start(pred[512]{0:T(512)(128)(4,1)} %copy-done.80) | copy-start | bytes 1540 | tf_op jit(solution)/shard_map/conditional.1
  616.7 98.4 %copy-start.32 = (f32[384,2048]{1,0:T(8,128)S(1)}, f32[384,2048]{1,0:T(8,128)}, u32[]{:S(2)}) copy-start(f32[384,2048]{1,0:T(8,128)} %fusion.77.refs_0_) | copy-start | bytes 9437188 | tf_op jit(solution)/shard_map/conditional.1
  616.7 98.4 %copy-start.82 = (f32[2048]{0:T(1024)S(1)}, f32[2048]{0:T(1024)}, u32[]{:S(2)}) copy-start(f32[2048]{0:T(1024)} %mul.480) | copy-start | bytes 24580 | tf_op jit(solution)/shard_map/conditional.1
  (45 other events, 190.7 us)
Sparse Core Ops, SparseCore 0:
  128.3 58.4 all-gather.8
  234.9 77.9 all-gather.10
  465.7 150.9 reduce-scatter.8
  618.8 71.2 reduce-scatter.10
